TPU v7x, 512 devices: a whole 4x8x8 slice. The times are simulated.
512 devices in a mesh: bfly: 16 (over x, z_hi), cols: 32 (over z_lo, y, core).
Axes of the slice: x: 4, y: 8, z: 8 (z_hi: 4, z_lo: 2; z = z_hi * 2 + z_lo), core: 2. Of those that a mesh axis runs over, the one named last changes fastest.
Arguments:
- right_side: bfloat16 [16, 32768, 512], P('bfly', 'cols'), may hold values from -6 to 6
- column_leaf_factors: bfloat16 [16, 32768, 256], P('bfly', 'cols'), may hold values from -0.1875 to 0.1875
- leaf_out: bfloat16 [16, 32768, 256], P('bfly', 'cols'), may hold values from -0.0625 to 0.0625
- transfer: bfloat16 [4, 16, 32, 2, 256, 256], P(None, 'bfly', 'cols'), may hold values from -0.25 to 0.25
Outputs:
- solution: float32 [16, 32768, 512], P('bfly', 'cols')
All inputs are finite; a program needn't handle non-finite values.
Results may differ from a plain program's by a relative error of at most 0.03.
Values may be sent and summed in bfloat16 or wider, within the bound.
No kernel may reach another device: no remote copies, remote signals or barrier semaphores. Data moves between devices by JAX's collectives and lax.ppermute only.
A program may use at most 64 MiB of HBM per device.

v0:
```python
import jax
import jax.numpy as jnp
from jax import lax
from jax.sharding import PartitionSpec as P

ITERS = 2


def from_partner(block, axis, bit):
    count = lax.axis_size(axis)
    route = []
    for low in range(count):
        high = low | 1 << bit
        if high != low and high < count:
            route += [(low, high), (high, low)]
    return lax.ppermute(block, axis, route)


def split_up(shard, dim, size):
    before, after = (shard.shape[:dim], shard.shape[dim + 1 :])
    return jnp.moveaxis(shard.reshape(*before, size, -1, *after), dim, 0)


def summed_on_arrival(shard, axis, dim):
    size = lax.axis_size(axis)
    blocks = lax.all_to_all(split_up(shard, dim, size), axis, 0, 0, tiled=True)
    return jnp.sum(blocks.astype(jnp.float32), axis=0)


def copy_for_each(shard, axis):
    copies = jnp.broadcast_to(shard, (lax.axis_size(axis), *shard.shape))
    return lax.all_to_all(copies, axis, split_axis=0, concat_axis=0, tiled=True)


def laid_out(blocks, dim):
    blocks = jnp.moveaxis(blocks, 0, dim)
    dims = blocks.shape
    return blocks.reshape(*dims[:dim], dims[dim] * dims[dim + 1], *dims[dim + 2 :])


def gather_directly(shard, axis, dim):
    blocks = copy_for_each(shard, axis)
    return laid_out(blocks, dim)


def apply_operator(iterate, column_leaf_factors, leaf_out, transfer):
    input_vector = iterate[0].astype(jnp.bfloat16)
    coefficient = jnp.einsum(
        "lk,lr->kr", column_leaf_factors[0], input_vector, preferred_element_type=jnp.float32
    ).astype(jnp.bfloat16)
    for level_index in range(lax.axis_size("bfly").bit_length() - 1):
        partner = from_partner(coefficient, "bfly", level_index)
        combined = jnp.dot(
            transfer[level_index, 0, 0, 0], coefficient, preferred_element_type=jnp.float32
        )
        combined = combined + jnp.dot(
            transfer[level_index, 0, 0, 1], partner, preferred_element_type=jnp.float32
        )
        coefficient = combined.astype(jnp.bfloat16)
    running_total_sum = coefficient.astype(jnp.float32)
    part_sum = summed_on_arrival(running_total_sum.astype(jnp.bfloat16), "cols", 1).astype(
        jnp.bfloat16
    )
    reduced_total = gather_directly(part_sum, "cols", 1)
    result_row_values = jnp.dot(leaf_out[0], reduced_total, preferred_element_type=jnp.float32)
    return result_row_values[None]


def body(right_side, column_leaf_factors, leaf_out, transfer):
    initial = right_side.astype(jnp.float32)
    iterate = initial
    for iteration in range(ITERS):
        iterate = initial - apply_operator(iterate, column_leaf_factors, leaf_out, transfer)
    return iterate


def solution(mesh):
    in_specs = (
        P("bfly", "cols", None),
        P("bfly", "cols", None),
        P("bfly", "cols", None),
        P(None, "bfly", "cols", None, None, None),
    )
    out_specs = P("bfly", "cols", None)
    return jax.shard_map(body, mesh=mesh, in_specs=in_specs, out_specs=out_specs, check_vma=False)
```

profile of v0, /device:TPU:1, one launch (start us, length us, event | category | flops | bytes accessed | tf_op | source)
XLA Modules:
  0.0 195.0 jit_solution(17683803394975746642)
XLA Ops:
  0.0 2.0 %convolution_convert_fusion.1 = bf16[256,512]{1,0:T(8,128)(2,1)S(1)} fusion(bf16[1,1024,512]{2,1,0:T(8,128)(2,1)} %param.4, bf16[1,1024,256]{2,1,0:T(8,128)(2,1)} %param.5), kind=kOutput, calls=%fused_computation.13 | convolution fusion | flops 268566528 | bytes 1835008 | tf_op jit(solution)/shard_map/lk,lr->kr/dot_general | solution.py:48
  2.0 6.6 %collective-permute-start = (bf16[256,512]{1,0:T(8,128)(2,1)S(1)}, bf16[256,512]{1,0:T(8,128)(2,1)S(1)}, u32[]{:S(2)}, u32[]{:S(2)}) collective-permute-start(bf16[256,512]{1,0:T(8,128)(2,1)S(1)} %convolution_convert_fusion.1), channel_id=1, source_target_pairs={{0,32},{32,0},{64,96},{96,64},{128,160},{160,128},{192,224},{224,1... | collective-permute-start | bytes 786440 | tf_op jit(solution)/shard_map/ppermute | solution.py:16
  8.6 0.3 fusion.38
  8.9 10.2 %collective-permute-done = bf16[256,512]{1,0:T(8,128)(2,1)S(1)} collective-permute-done((bf16[256,512]{1,0:T(8,128)(2,1)S(1)}, bf16[256,512]{1,0:T(8,128)(2,1)S(1)}, u32[]{:S(2)}, u32[]{:S(2)}) %collective-permute-start) | collective-permute-done | bytes 262176 | tf_op jit(solution)/shard_map/ppermute | solution.py:16
  19.1 0.3 fusion.2
  19.4 10.0 %collective-permute-start.1 = (bf16[256,512]{0,1:T(8,128)(2,1)S(1)}, bf16[256,512]{0,1:T(8,128)(2,1)S(1)}, u32[]{:S(2)}, u32[]{:S(2)}) collective-permute-start(bf16[256,512]{0,1:T(8,128)(2,1)S(1)} %bitcast.111), channel_id=1, source_target_pairs={{0,64},{64,0},{32,96},{96,32},{128,192},{192,128},{160,224},{224,1... | collective-permute-start | bytes 786440 | tf_op jit(solution)/shard_map/ppermute | solution.py:16
  29.7 7.8 %collective-permute-done.1 = bf16[256,512]{0,1:T(8,128)(2,1)S(1)} collective-permute-done((bf16[256,512]{0,1:T(8,128)(2,1)S(1)}, bf16[256,512]{0,1:T(8,128)(2,1)S(1)}, u32[]{:S(2)}, u32[]{:S(2)}) %collective-permute-start.1) | collective-permute-done | bytes 262176 | tf_op jit(solution)/shard_map/ppermute | solution.py:16
  37.5 0.3 fusion.3
  37.8 3.1 %collective-permute-start.2 = (bf16[256,512]{0,1:T(8,128)(2,1)S(1)}, bf16[256,512]{0,1:T(8,128)(2,1)S(1)}, u32[]{:S(2)}, u32[]{:S(2)}) collective-permute-start(bf16[256,512]{0,1:T(8,128)(2,1)S(1)} %bitcast.112), channel_id=1, source_target_pairs={{0,128},{128,0},{32,160},{160,32},{64,192},{192,64},{96,224},{224,... | collective-permute-start | bytes 786440 | tf_op jit(solution)/shard_map/ppermute | solution.py:16
  41.2 3.7 %collective-permute-done.2 = bf16[256,512]{0,1:T(8,128)(2,1)S(1)} collective-permute-done((bf16[256,512]{0,1:T(8,128)(2,1)S(1)}, bf16[256,512]{0,1:T(8,128)(2,1)S(1)}, u32[]{:S(2)}, u32[]{:S(2)}) %collective-permute-start.2) | collective-permute-done | bytes 262176 | tf_op jit(solution)/shard_map/ppermute | solution.py:16
  44.9 0.3 fusion.4
  45.2 4.6 %collective-permute-start.3 = (bf16[256,512]{0,1:T(8,128)(2,1)S(1)}, bf16[256,512]{0,1:T(8,128)(2,1)S(1)}, u32[]{:S(2)}, u32[]{:S(2)}) collective-permute-start(bf16[256,512]{0,1:T(8,128)(2,1)S(1)} %bitcast.113), channel_id=1, source_target_pairs={{0,256},{256,0},{32,288},{288,32},{64,320},{320,64},{96,352},{352,... | collective-permute-start | bytes 786440 | tf_op jit(solution)/shard_map/ppermute | solution.py:16
  50.1 5.1 %collective-permute-done.3 = bf16[256,512]{0,1:T(8,128)(2,1)S(1)} collective-permute-done((bf16[256,512]{0,1:T(8,128)(2,1)S(1)}, bf16[256,512]{0,1:T(8,128)(2,1)S(1)}, u32[]{:S(2)}, u32[]{:S(2)}) %collective-permute-start.3) | collective-permute-done | bytes 262176 | tf_op jit(solution)/shard_map/ppermute | solution.py:16
  55.2 0.3 fusion.5
  55.4 24.7 %all_to_all.20 = bf16[32,256,16]{1,2,0:T(8,128)(2,1)S(1)} all-to-all(bf16[32,256,16]{1,2,0:T(8,128)(2,1)S(1)} %bitcast.117), channel_id=1, replica_groups=mesh['bfly'=16,'cols'=32] {'cols'}, dimensions={0} | all-to-all | bytes 524288 | tf_op jit(solution)/shard_map/all_to_all | solution.py:26
  80.2 0.7 broadcast_in_dim.12
  80.9 5.0 %all-to-all-start.1 = ((bf16[32,256,16]{1,2,0:T(8,128)(2,1)}), bf16[32,256,16]{1,2,0:T(8,128)(2,1)S(1)}, u32[]{:S(2)}, u32[]{:S(2)}) async-start(bf16[32,256,16]{1,2,0:T(8,128)(2,1)} %broadcast_in_dim.12), calls=%async_computation.1 | async-start | bytes 524288 | tf_op jit(solution)/shard_map/all_to_all | solution.py:32
  85.9 1.5 copy.7
  87.4 10.5 %all-to-all-done.1 = bf16[32,256,16]{1,2,0:T(8,128)(2,1)S(1)} async-done(((bf16[32,256,16]{1,2,0:T(8,128)(2,1)}), bf16[32,256,16]{1,2,0:T(8,128)(2,1)S(1)}, u32[]{:S(2)}, u32[]{:S(2)}) %all-to-all-start.1) | async-done | bytes 262176 | tf_op jit(solution)/shard_map/all_to_all | solution.py:32
  98.0 1.9 convolution_convert_fusion
  99.9 7.4 %collective-permute-start.4 = (bf16[256,512]{0,1:T(8,128)(2,1)S(1)}, bf16[256,512]{0,1:T(8,128)(2,1)S(1)}, u32[]{:S(2)}, u32[]{:S(2)}) collective-permute-start(bf16[256,512]{0,1:T(8,128)(2,1)S(1)} %bitcast.120), channel_id=1, source_target_pairs={{0,32},{32,0},{64,96},{96,64},{128,160},{160,128},{192,224},{224,1... | collective-permute-start | bytes 786440 | tf_op jit(solution)/shard_map/ppermute | solution.py:16
  107.6 11.6 %collective-permute-done.4 = bf16[256,512]{0,1:T(8,128)(2,1)S(1)} collective-permute-done((bf16[256,512]{0,1:T(8,128)(2,1)S(1)}, bf16[256,512]{0,1:T(8,128)(2,1)S(1)}, u32[]{:S(2)}, u32[]{:S(2)}) %collective-permute-start.4) | collective-permute-done | bytes 262176 | tf_op jit(solution)/shard_map/ppermute | solution.py:16
  119.4 3.7 %collective-permute-start.5 = (bf16[256,512]{0,1:T(8,128)(2,1)S(1)}, bf16[256,512]{0,1:T(8,128)(2,1)S(1)}, u32[]{:S(2)}, u32[]{:S(2)}) collective-permute-start(bf16[256,512]{0,1:T(8,128)(2,1)S(1)} %bitcast.114), channel_id=1, source_target_pairs={{0,64},{64,0},{32,96},{96,32},{128,192},{192,128},{160,224},{224,1... | collective-permute-start | bytes 786440 | tf_op jit(solution)/shard_map/ppermute | solution.py:16
  123.4 14.4 %collective-permute-done.5 = bf16[256,512]{0,1:T(8,128)(2,1)S(1)} collective-permute-done((bf16[256,512]{0,1:T(8,128)(2,1)S(1)}, bf16[256,512]{0,1:T(8,128)(2,1)S(1)}, u32[]{:S(2)}, u32[]{:S(2)}) %collective-permute-start.5) | collective-permute-done | bytes 262176 | tf_op jit(solution)/shard_map/ppermute | solution.py:16
  138.0 3.1 %collective-permute-start.6 = (bf16[256,512]{0,1:T(8,128)(2,1)S(1)}, bf16[256,512]{0,1:T(8,128)(2,1)S(1)}, u32[]{:S(2)}, u32[]{:S(2)}) collective-permute-start(bf16[256,512]{0,1:T(8,128)(2,1)S(1)} %bitcast.115), channel_id=1, source_target_pairs={{0,128},{128,0},{32,160},{160,32},{64,192},{192,64},{96,224},{224,... | collective-permute-start | bytes 786440 | tf_op jit(solution)/shard_map/ppermute | solution.py:16
  141.4 5.9 %collective-permute-done.6 = bf16[256,512]{0,1:T(8,128)(2,1)S(1)} collective-permute-done((bf16[256,512]{0,1:T(8,128)(2,1)S(1)}, bf16[256,512]{0,1:T(8,128)(2,1)S(1)}, u32[]{:S(2)}, u32[]{:S(2)}) %collective-permute-start.6) | collective-permute-done | bytes 262176 | tf_op jit(solution)/shard_map/ppermute | solution.py:16
  147.6 4.7 %collective-permute-start.7 = (bf16[256,512]{0,1:T(8,128)(2,1)S(1)}, bf16[256,512]{0,1:T(8,128)(2,1)S(1)}, u32[]{:S(2)}, u32[]{:S(2)}) collective-permute-start(bf16[256,512]{0,1:T(8,128)(2,1)S(1)} %bitcast.116), channel_id=1, source_target_pairs={{0,256},{256,0},{32,288},{288,32},{64,320},{320,64},{96,352},{352,... | collective-permute-start | bytes 786440 | tf_op jit(solution)/shard_map/ppermute | solution.py:16
  152.5 4.9 %collective-permute-done.7 = bf16[256,512]{0,1:T(8,128)(2,1)S(1)} collective-permute-done((bf16[256,512]{0,1:T(8,128)(2,1)S(1)}, bf16[256,512]{0,1:T(8,128)(2,1)S(1)}, u32[]{:S(2)}, u32[]{:S(2)}) %collective-permute-start.7) | collective-permute-done | bytes 262176 | tf_op jit(solution)/shard_map/ppermute | solution.py:16
  157.7 17.5 %all_to_all.21 = bf16[32,256,16]{1,2,0:T(8,128)(2,1)S(1)} all-to-all(bf16[32,256,16]{1,2,0:T(8,128)(2,1)S(1)} %bitcast.118), channel_id=1, replica_groups=mesh['bfly'=16,'cols'=32] {'cols'}, dimensions={0} | all-to-all | bytes 524288 | tf_op jit(solution)/shard_map/all_to_all | solution.py:26
  175.3 16.2 %all_to_all.22 = bf16[32,256,16]{1,2,0:T(8,128)(2,1)S(1)} all-to-all(bf16[32,256,16]{1,2,0:T(8,128)(2,1)S(1)} %broadcast_in_dim.14), channel_id=1, replica_groups=mesh['bfly'=16,'cols'=32] {'cols'}, dimensions={0} | all-to-all | bytes 524288 | tf_op jit(solution)/shard_map/all_to_all | solution.py:32
  191.4 1.7 convert_subtract_fusion
  193.1 1.8 copy.8
  (20 shorter events, 3.0 us)
Async XLA Ops:
  0.0 98.0 %copy-start = (bf16[1,1024,256]{2,1,0:T(8,128)(2,1)S(1)}, bf16[1,1024,256]{2,1,0:T(8,128)(2,1)}, u32[]{:S(2)}) copy-start(bf16[1,1024,256]{2,1,0:T(8,128)(2,1)} %param.6) | copy-start | bytes 1572868
  0.0 8.6 %copy-start.1 = (bf16[4,1,1,2,256,256]{5,4,3,2,1,0:T(8,128)(2,1)S(1)}, bf16[4,1,1,2,256,256]{5,4,3,2,1,0:T(8,128)(2,1)}, u32[]{:S(2)}) copy-start(bf16[4,1,1,2,256,256]{5,4,3,2,1,0:T(8,128)(2,1)} %param.7) | copy-start | bytes 3145732
  2.0 17.1 %collective-permute-start = (bf16[256,512]{1,0:T(8,128)(2,1)S(1)}, bf16[256,512]{1,0:T(8,128)(2,1)S(1)}, u32[]{:S(2)}, u32[]{:S(2)}) collective-permute-start(bf16[256,512]{1,0:T(8,128)(2,1)S(1)} %convolution_convert_fusion.1), channel_id=1, source_target_pairs={{0,32},{32,0},{64,96},{96,64},{128,160},{160,128},{192,224},{224,1... | collective-permute-start | bytes 786440 | tf_op jit(solution)/shard_map/ppermute | solution.py:16
  19.4 18.1 %collective-permute-start.1 = (bf16[256,512]{0,1:T(8,128)(2,1)S(1)}, bf16[256,512]{0,1:T(8,128)(2,1)S(1)}, u32[]{:S(2)}, u32[]{:S(2)}) collective-permute-start(bf16[256,512]{0,1:T(8,128)(2,1)S(1)} %bitcast.111), channel_id=1, source_target_pairs={{0,64},{64,0},{32,96},{96,32},{128,192},{192,128},{160,224},{224,1... | collective-permute-start | bytes 786440 | tf_op jit(solution)/shard_map/ppermute | solution.py:16
  37.8 7.1 %collective-permute-start.2 = (bf16[256,512]{0,1:T(8,128)(2,1)S(1)}, bf16[256,512]{0,1:T(8,128)(2,1)S(1)}, u32[]{:S(2)}, u32[]{:S(2)}) collective-permute-start(bf16[256,512]{0,1:T(8,128)(2,1)S(1)} %bitcast.112), channel_id=1, source_target_pairs={{0,128},{128,0},{32,160},{160,32},{64,192},{192,64},{96,224},{224,... | collective-permute-start | bytes 786440 | tf_op jit(solution)/shard_map/ppermute | solution.py:16
  45.2 10.0 %collective-permute-start.3 = (bf16[256,512]{0,1:T(8,128)(2,1)S(1)}, bf16[256,512]{0,1:T(8,128)(2,1)S(1)}, u32[]{:S(2)}, u32[]{:S(2)}) collective-permute-start(bf16[256,512]{0,1:T(8,128)(2,1)S(1)} %bitcast.113), channel_id=1, source_target_pairs={{0,256},{256,0},{32,288},{288,32},{64,320},{320,64},{96,352},{352,... | collective-permute-start | bytes 786440 | tf_op jit(solution)/shard_map/ppermute | solution.py:16
  80.9 17.1 %all-to-all-start.1 = ((bf16[32,256,16]{1,2,0:T(8,128)(2,1)}), bf16[32,256,16]{1,2,0:T(8,128)(2,1)S(1)}, u32[]{:S(2)}, u32[]{:S(2)}) async-start(bf16[32,256,16]{1,2,0:T(8,128)(2,1)} %broadcast_in_dim.12), calls=%async_computation.1 | async-start | bytes 524288 | tf_op jit(solution)/shard_map/all_to_all | solution.py:32
  87.4 87.8 %copy-start.2 = (bf16[1,1024,512]{1,2,0:T(8,128)(2,1)}, bf16[1,1024,512]{1,2,0:T(8,128)(2,1)S(1)}, u32[]{:S(2)}) copy-start(bf16[1,1024,512]{1,2,0:T(8,128)(2,1)S(1)} %copy.7) | copy-start | bytes 3145732
  99.9 19.3 %collective-permute-start.4 = (bf16[256,512]{0,1:T(8,128)(2,1)S(1)}, bf16[256,512]{0,1:T(8,128)(2,1)S(1)}, u32[]{:S(2)}, u32[]{:S(2)}) collective-permute-start(bf16[256,512]{0,1:T(8,128)(2,1)S(1)} %bitcast.120), channel_id=1, source_target_pairs={{0,32},{32,0},{64,96},{96,64},{128,160},{160,128},{192,224},{224,1... | collective-permute-start | bytes 786440 | tf_op jit(solution)/shard_map/ppermute | solution.py:16
  119.4 18.4 %collective-permute-start.5 = (bf16[256,512]{0,1:T(8,128)(2,1)S(1)}, bf16[256,512]{0,1:T(8,128)(2,1)S(1)}, u32[]{:S(2)}, u32[]{:S(2)}) collective-permute-start(bf16[256,512]{0,1:T(8,128)(2,1)S(1)} %bitcast.114), channel_id=1, source_target_pairs={{0,64},{64,0},{32,96},{96,32},{128,192},{192,128},{160,224},{224,1... | collective-permute-start | bytes 786440 | tf_op jit(solution)/shard_map/ppermute | solution.py:16
  138.0 9.3 %collective-permute-start.6 = (bf16[256,512]{0,1:T(8,128)(2,1)S(1)}, bf16[256,512]{0,1:T(8,128)(2,1)S(1)}, u32[]{:S(2)}, u32[]{:S(2)}) collective-permute-start(bf16[256,512]{0,1:T(8,128)(2,1)S(1)} %bitcast.115), channel_id=1, source_target_pairs={{0,128},{128,0},{32,160},{160,32},{64,192},{192,64},{96,224},{224,... | collective-permute-start | bytes 786440 | tf_op jit(solution)/shard_map/ppermute | solution.py:16
  147.6 9.9 %collective-permute-start.7 = (bf16[256,512]{0,1:T(8,128)(2,1)S(1)}, bf16[256,512]{0,1:T(8,128)(2,1)S(1)}, u32[]{:S(2)}, u32[]{:S(2)}) collective-permute-start(bf16[256,512]{0,1:T(8,128)(2,1)S(1)} %bitcast.116), channel_id=1, source_target_pairs={{0,256},{256,0},{32,288},{288,32},{64,320},{320,64},{96,352},{352,... | collective-permute-start | bytes 786440 | tf_op jit(solution)/shard_map/ppermute | solution.py:16
where the time goes:
time: 196 us; the launch traced here: 195 us
  waiting for transfers between devices  74.2 us (38%)
  blocking collectives  58.3 us (30%)
  starting transfers between devices  48.4 us (25%)
  matrix products  9.67 us (5%)
  local copies, waits for them, and re-layouts  4.06 us (2%)
    ppermute x8, waiting for transfers between devices, from_partner(): return lax.ppermute(block, axis, route)  63.7 us
    ppermute x8, starting transfers between devices, from_partner(): return lax.ppermute(block, axis, route)  43.4 us
    all_to_all x2, blocking collectives, summed_on_arrival(): blocks = lax.all_to_all(split_up(shard, dim, size), axis, 0, 0, tiled=True)  42.2 us
    all_to_all x1, blocking collectives, copy_for_each(): return lax.all_to_all(copies, axis, split_axis=0, concat_axis=0, tiled=True)  16.2 us
    all_to_all x1, waiting for transfers between devices, copy_for_each(): return lax.all_to_all(copies, axis, split_axis=0, concat_axis=0, tiled=True)  10.5 us
    all_to_all x1, starting transfers between devices, copy_for_each(): return lax.all_to_all(copies, axis, split_axis=0, concat_axis=0, tiled=True)  5.02 us
  transfers between devices with their start and end apart: 9, of which 9 were waited for; matrix products, arithmetic and copies ran while one was open for 2% of the time, Pallas kernels for 0%

commit v1 on v0

v1 whole, which is shorter than its diff:
```python
import jax
import jax.numpy as jnp
from jax import lax
from jax.experimental import pallas as pl
from jax.experimental.pallas import tpu as pltpu
from jax.sharding import Mesh, PartitionSpec as P

ITERS = 2
BF = jnp.bfloat16
F32 = jnp.float32
LINE = ("zl", "y")


def swap(block, axis, bit):
    size = lax.axis_size(axis)
    return lax.ppermute(block, axis, [(i, i ^ bit) for i in range(size)])


def mm(spec, a, b):
    return jnp.einsum(spec, a, b, preferred_element_type=F32)


def by_target(blocks):
    me = lax.axis_index("x")
    for bit in (1, 2):
        turned = [blocks[d ^ bit] for d in range(len(blocks))]
        blocks = [jnp.where(me & bit == bit, t, b) for t, b in zip(turned, blocks)]
    return blocks


def finish_kernel(rhs_ref, basis_ref, total_ref, out_ref):
    half = total_ref.shape[2]
    for core in range(2):
        cols = slice(core * half, (core + 1) * half)
        update = jnp.dot(basis_ref[...], total_ref[core], preferred_element_type=F32)
        out_ref[:, cols] = rhs_ref[:, cols].astype(F32) - update


def finish(rhs, basis, total):
    rows, width = rhs.shape
    rank = basis.shape[1]
    block = rows // 4
    return pl.pallas_call(
        finish_kernel,
        grid=(rows // block,),
        in_specs=[
            pl.BlockSpec((block, width), lambda i: (i, 0)),
            pl.BlockSpec((block, rank), lambda i: (i, 0)),
            pl.BlockSpec(total.shape, lambda i: (0, 0, 0)),
        ],
        out_specs=pl.BlockSpec((block, width), lambda i: (i, 0)),
        out_shape=jax.ShapeDtypeStruct((rows, width), F32),
    )(rhs, basis, total)


def body(right_side, column_leaf_factors, leaf_out, transfer):
    rhs = right_side[0]
    basis = column_leaf_factors[0]
    out_basis = leaf_out[0]
    half = rhs.shape[1] // 2
    rank = basis.shape[1]
    core = lax.axis_index("c")

    first = mm("lk,lr->kr", basis, rhs).astype(BF)
    first = lax.all_gather(first, "c")
    first = lax.dynamic_slice_in_dim(first, core * half, half, 2)
    first, transfer, basis_late = lax.optimization_barrier((first, transfer, basis))

    own = transfer[:, 0, 0, 0]
    other = transfer[:, 0, 0, 1]
    far = swap(other[3], "x", 2)
    levels = [lax.all_gather(transfer[0, 0, 0], "c")]
    gram = mm("li,lj->ij", basis_late, out_basis).astype(BF)
    more = lax.all_gather(jnp.concatenate([transfer[1, 0, 0], gram[None]], 0), "c")
    levels.append(more[:, :2])
    gram = more[:, 2]
    wide = jnp.concatenate([own[3], far], 0)
    kept = mm("ij,jk->ik", wide, own[2]).astype(BF)
    sent = mm("ij,jk->ik", wide, other[2]).astype(BF)
    came = swap(sent, "x", 1)
    tail = by_target([kept[:rank], came[:rank], kept[rank:], came[rank:]])
    tail = [lax.all_gather(jnp.concatenate(tail[i : i + 2], 0), "c") for i in (0, 2)]

    coefficient = first
    for iteration in range(ITERS):
        for level, axis in enumerate(("za", "zb")):
            partner = swap(coefficient, axis, 1)
            coefficient = (
                mm("cij,cjr->cir", levels[level][:, 0], coefficient)
                + mm("cij,cjr->cir", levels[level][:, 1], partner)
            ).astype(BF)
        spread = jnp.concatenate([mm("cij,cjr->ir", t, coefficient).astype(BF) for t in tail], 0)
        count = lax.axis_size(("x",) + LINE)
        pieces = spread.reshape(count, -1, half)
        pieces = lax.all_to_all(pieces, ("x",) + LINE, 0, 0, tiled=True)
        share = jnp.sum(pieces.astype(F32), axis=0).astype(BF)
        copies = jnp.broadcast_to(share, (lax.axis_size(LINE), *share.shape))
        total = lax.all_to_all(copies, LINE, 0, 0, tiled=True).reshape(rank, half)
        if iteration < ITERS - 1:
            coefficient = (first.astype(F32) - mm("cij,jr->cir", gram, total)).astype(BF)
    total = lax.all_gather(total, "c")
    return finish(rhs, out_basis, total)[None]


def solution(mesh):
    devices = mesh.devices.reshape(4, 2, 2, 2, 8, 2)
    fine = Mesh(devices, ("x", "zb", "za", "zl", "y", "c"))
    bfly, cols = ("x", "zb", "za"), ("zl", "y", "c")
    in_specs = (
        P(bfly, cols, None),
        P(bfly, cols, None),
        P(bfly, cols, None),
        P(None, bfly, cols, None, None, None),
    )
    out_specs = P(bfly, cols, None)
    return jax.shard_map(body, mesh=fine, in_specs=in_specs, out_specs=out_specs, check_vma=False)
```

time: 196 us -> 168 us (0.86)
  waiting for transfers between devices: 74.2 us -> 30.5 us
  blocking collectives: 58.3 us -> 91.4 us
  starting transfers between devices: 48.4 us -> 30.1 us
  Pallas kernels: 0 us -> 4.15 us
  local copies, waits for them, and re-layouts: 4.06 us -> 1.87 us
  matrix products: 9.67 us -> 7.49 us
    ppermute x8 -> x6, waiting for transfers between devices: 63.7 us -> 30.5 us  [swap(): return lax.ppermute(block, axis, [(i, i ^ bit) for i in range(size)])]
    all_gather x0 -> x6, blocking collectives: none -> 24 us  [the longest x1 8.69 us: body(): first = lax.all_gather(first, 'c')]
    ppermute x8 -> x6, starting transfers between devices: 43.4 us -> 30.1 us  [swap(): return lax.ppermute(block, axis, [(i, i ^ bit) for i in range(size)])]
    all_to_all x1 -> x0, waiting for transfers between devices: 10.5 us -> none  [copy_for_each(): return lax.all_to_all(copies, axis, split_axis=0, concat_axis=0, tiled=True)]
    all_to_all x3 -> x4, blocking collectives: 58.3 us -> 67.4 us  [the longest x2 42.8 us: body(): pieces = lax.all_to_all(pieces, ('x',) + LINE, 0, 0, tiled=True)]
    all_to_all x1 -> x0, starting transfers between devices: 5.02 us -> none  [copy_for_each(): return lax.all_to_all(copies, axis, split_axis=0, concat_axis=0, tiled=True)]
    pallas_call x0 -> x1, Pallas kernels: none -> 4.15 us  [finish(): pl.pallas_call(finish_kernel, grid=(rows // block,), in_specs=[pl.BlockSp...]
    dot_general x19 -> x17, matrix products: 9.67 us -> 7.49 us  [mm(): return jnp.einsum(spec, a, b, preferred_element_type=F32)]
  transfers between devices with their start and end apart: 9 -> 6, of which waited for: 9 -> 4; matrix products, arithmetic and copies ran while one was open for 2% -> 2% of each run, Pallas kernels for 0% -> 0%
where the time goes in v1:
time: 168 us; the launch traced here: 167 us
  blocking collectives  91.4 us (54%)
  waiting for transfers between devices  30.5 us (18%)
  starting transfers between devices  30.1 us (18%)
  matrix products  7.49 us (4%)
  Pallas kernels  4.15 us (2%)
  local copies, waits for them, and re-layouts  1.87 us (1%)
    all_to_all x2, blocking collectives, body(): pieces = lax.all_to_all(pieces, ('x',) + LINE, 0, 0, tiled=True)  42.8 us
    ppermute x6, waiting for transfers between devices, swap(): return lax.ppermute(block, axis, [(i, i ^ bit) for i in range(size)])  30.5 us
    ppermute x6, starting transfers between devices, swap(): return lax.ppermute(block, axis, [(i, i ^ bit) for i in range(size)])  30.1 us
    all_to_all x2, blocking collectives, body(): total = lax.all_to_all(copies, LINE, 0, 0, tiled=True).reshape(rank, half)  24.6 us
    all_gather x1, blocking collectives, body(): first = lax.all_gather(first, 'c')  8.69 us
    dot_general x17, matrix products, mm(): return jnp.einsum(spec, a, b, preferred_element_type=F32)  7.49 us
    all_gather x2, blocking collectives, body(): lax.all_gather(jnp.concatenate(tail[i:i + 2], 0), 'c')  5.67 us
    all_gather x1, blocking collectives, body(): total = lax.all_gather(total, 'c')  4.41 us
  transfers between devices with their start and end apart: 6, of which 4 were waited for; matrix products, arithmetic and copies ran while one was open for 2% of the time, Pallas kernels for 0%

profile of v1, /device:TPU:1, one launch (start us, length us, event | category | flops | bytes accessed | tf_op | source)
XLA Modules:
  0.0 167.3 jit_solution(5120938491200430413)
XLA Ops:
  0.0 1.0 copy-done
  1.0 1.7 %convolution_convert_fusion.2 = bf16[256,512]{1,0:T(8,128)(2,1)S(1)} fusion(bf16[1,1024,256]{2,1,0:T(8,128)(2,1)S(1)} %copy-done, bf16[1,1024,512]{2,1,0:T(8,128)(2,1)} %param.4), kind=kOutput, calls=%fused_computation.15 | convolution fusion | flops 268566528 | bytes 1835008 | tf_op jit(solution)/shard_map/lk,lr->kr/dot_general | solution.py:20
  2.7 8.7 %all-gather = bf16[512,512]{1,0:T(8,128)(2,1)S(1)} all-gather(bf16[256,512]{1,0:T(8,128)(2,1)S(1)} %convolution_convert_fusion.2), channel_id=2, replica_groups=mesh['x'=4,'zb'=2,'za'=2,'zl'=2,'y'=8,'c'=2] {'c'}, dimensions={0}, use_global_device_ids=true | all-gather | bytes 786432 | tf_op jit(solution)/shard_map/all_gather | solution.py:65
  11.4 0.7 slice_bitcast_fusion.16
  12.1 1.9 %collective-permute-start = (bf16[256,256]{1,0:T(8,128)(2,1)}, bf16[256,256]{1,0:T(8,128)(2,1)}, u32[]{:S(2)}, u32[]{:S(2)}) collective-permute-start(bf16[256,256]{1,0:T(8,128)(2,1)} %get-tuple-element.12), channel_id=1, source_target_pairs={{0,256},{128,384},{256,0},{384,128},{1,257},{129,385},{257,1},{385... | collective-permute-start | bytes 393224 | tf_op jit(solution)/shard_map/ppermute | solution.py:16
  14.0 3.2 %collective-permute-start.2 = (bf16[2,256,256]{2,1,0:T(8,128)(2,1)S(1)}, bf16[2,256,256]{2,1,0:T(8,128)(2,1)S(1)}, u32[]{:S(2)}, u32[]{:S(2)}) collective-permute-start(bf16[2,256,256]{2,1,0:T(8,128)(2,1)S(1)} %constant_dynamic-slice_fusion), channel_id=1, source_target_pairs={{0,32},{32,0},{1,33},{33,1},{2,34},{34,2},{3,35},{35,3},{4,36},{36... | collective-permute-start | bytes 786440 | tf_op jit(solution)/shard_map/ppermute | solution.py:16
  17.4 2.9 %all-gather.3 = bf16[2,1,1,2,256,256]{5,4,0,3,2,1:T(8,128)(2,1)S(1)} all-gather(bf16[1,1,1,2,256,256]{5,4,0,3,2,1:T(8,128)(2,1)S(1)} %slice.82), channel_id=5, replica_groups=mesh['x'=4,'zb'=2,'za'=2,'zl'=2,'y'=8,'c'=2] {'c'}, dimensions={0}, use_global_device_ids=true | all-gather | bytes 786432 | tf_op jit(solution)/shard_map/all_gather | solution.py:72
  20.5 0.3 fusion.9
  20.9 2.4 %all-gather.2 = bf16[6,256,256]{2,1,0:T(8,128)(2,1)S(1)} all-gather(bf16[3,256,256]{2,1,0:T(8,128)(2,1)S(1)} %pad_maximum_fusion.2), channel_id=4, replica_groups=mesh['x'=4,'zb'=2,'za'=2,'zl'=2,'y'=8,'c'=2] {'c'}, dimensions={0}, use_global_device_ids=true | all-gather | bytes 1179648 | tf_op jit(solution)/shard_map/all_gather | solution.py:74
  23.2 1.1 convolution_convert_fusion.1
  24.4 2.2 %collective-permute-start.1 = (bf16[512,256]{1,0:T(8,128)(2,1)S(1)}, bf16[512,256]{1,0:T(8,128)(2,1)S(1)}, u32[]{:S(2)}, u32[]{:S(2)}) collective-permute-start(bf16[512,256]{1,0:T(8,128)(2,1)S(1)} %convolution_convert_fusion.1), channel_id=1, source_target_pairs={{0,128},{128,0},{256,384},{384,256},{1,129},{129,1},{257,385},{385... | collective-permute-start | bytes 786440 | tf_op jit(solution)/shard_map/ppermute | solution.py:16
  26.6 1.1 convolution_convert_fusion
  27.7 2.3 %collective-permute-done.2 = bf16[2,256,256]{2,1,0:T(8,128)(2,1)S(1)} collective-permute-done((bf16[2,256,256]{2,1,0:T(8,128)(2,1)S(1)}, bf16[2,256,256]{2,1,0:T(8,128)(2,1)S(1)}, u32[]{:S(2)}, u32[]{:S(2)}) %collective-permute-start.2) | collective-permute-done | bytes 262176 | tf_op jit(solution)/shard_map/ppermute | solution.py:16
  30.2 7.8 %collective-permute-start.3 = (bf16[2,256,256]{2,1,0:T(8,128)(2,1)S(1)}, bf16[2,256,256]{2,1,0:T(8,128)(2,1)S(1)}, u32[]{:S(2)}, u32[]{:S(2)}) collective-permute-start(bf16[2,256,256]{2,1,0:T(8,128)(2,1)S(1)} %fusion.4), channel_id=1, source_target_pairs={{0,64},{64,0},{1,65},{65,1},{2,66},{66,2},{3,67},{67,3},{4,68},{68... | collective-permute-start | bytes 786440 | tf_op jit(solution)/shard_map/ppermute | solution.py:16
  38.4 3.5 %all-gather.1 = bf16[1024,256]{1,0:T(8,128)(2,1)S(1)} all-gather(bf16[512,256]{1,0:T(8,128)(2,1)S(1)} %pad_maximum_fusion.4), channel_id=3, replica_groups=mesh['x'=4,'zb'=2,'za'=2,'zl'=2,'y'=8,'c'=2] {'c'}, dimensions={0}, use_global_device_ids=true | all-gather | bytes 786432 | tf_op jit(solution)/shard_map/all_gather | solution.py:82
  41.9 2.2 %all-gather.4 = bf16[1024,256]{1,0:T(8,128)(2,1)S(1)} all-gather(bf16[512,256]{1,0:T(8,128)(2,1)S(1)} %pad_maximum_fusion.5), channel_id=6, replica_groups=mesh['x'=4,'zb'=2,'za'=2,'zl'=2,'y'=8,'c'=2] {'c'}, dimensions={0}, use_global_device_ids=true | all-gather | bytes 786432 | tf_op jit(solution)/shard_map/all_gather | solution.py:82
  44.0 2.1 %collective-permute-done.3 = bf16[2,256,256]{2,1,0:T(8,128)(2,1)S(1)} collective-permute-done((bf16[2,256,256]{2,1,0:T(8,128)(2,1)S(1)}, bf16[2,256,256]{2,1,0:T(8,128)(2,1)S(1)}, u32[]{:S(2)}, u32[]{:S(2)}) %collective-permute-start.3) | collective-permute-done | bytes 262176 | tf_op jit(solution)/shard_map/ppermute | solution.py:16
  46.3 0.3 fusion.1
  46.6 0.3 fusion
  47.0 22.9 %all_to_all.20 = bf16[64,16,256]{2,1,0:T(8,128)(2,1)} all-to-all(bf16[64,16,256]{2,1,0:T(8,128)(2,1)S(1)} %bitcast.108), channel_id=1, replica_groups=mesh['x'=4,'zb'=2,'za'=2,'zl'=2,'y'=8,'c'=2] {'x','zl','y'}, dimensions={0} | all-to-all | bytes 1048576 | tf_op jit(solution)/shard_map/all_to_all | solution.py:95
  69.9 1.1 reduce_sum.24
  71.0 11.9 %all_to_all.21 = bf16[16,16,256]{2,1,0:T(8,128)(2,1)S(1)} all-to-all(bf16[16,16,256]{2,1,0:T(8,128)(2,1)S(1)} %broadcast_in_dim.13), channel_id=1, replica_groups=mesh['x'=4,'zb'=2,'za'=2,'zl'=2,'y'=8,'c'=2] {'zl','y'}, dimensions={0} | all-to-all | bytes 262144 | tf_op jit(solution)/shard_map/all_to_all | solution.py:98
  83.1 11.4 %collective-permute-start.4 = (bf16[2,256,256]{2,1,0:T(8,128)(2,1)S(1)}, bf16[2,256,256]{2,1,0:T(8,128)(2,1)S(1)}, u32[]{:S(2)}, u32[]{:S(2)}) collective-permute-start(bf16[2,256,256]{2,1,0:T(8,128)(2,1)S(1)} %fusion.6), channel_id=1, source_target_pairs={{0,32},{32,0},{1,33},{33,1},{2,34},{34,2},{3,35},{35,3},{4,36},{36... | collective-permute-start | bytes 786440 | tf_op jit(solution)/shard_map/ppermute | solution.py:16
  94.7 11.8 %collective-permute-done.4 = bf16[2,256,256]{2,1,0:T(8,128)(2,1)S(1)} collective-permute-done((bf16[2,256,256]{2,1,0:T(8,128)(2,1)S(1)}, bf16[2,256,256]{2,1,0:T(8,128)(2,1)S(1)}, u32[]{:S(2)}, u32[]{:S(2)}) %collective-permute-start.4) | collective-permute-done | bytes 262176 | tf_op jit(solution)/shard_map/ppermute | solution.py:16
  106.8 3.6 %collective-permute-start.5 = (bf16[2,256,256]{2,1,0:T(8,128)(2,1)S(1)}, bf16[2,256,256]{2,1,0:T(8,128)(2,1)S(1)}, u32[]{:S(2)}, u32[]{:S(2)}) collective-permute-start(bf16[2,256,256]{2,1,0:T(8,128)(2,1)S(1)} %fusion.7), channel_id=1, source_target_pairs={{0,64},{64,0},{1,65},{65,1},{2,66},{66,2},{3,67},{67,3},{4,68},{68... | collective-permute-start | bytes 786440 | tf_op jit(solution)/shard_map/ppermute | solution.py:16
  110.6 14.4 %collective-permute-done.5 = bf16[2,256,256]{2,1,0:T(8,128)(2,1)S(1)} collective-permute-done((bf16[2,256,256]{2,1,0:T(8,128)(2,1)S(1)}, bf16[2,256,256]{2,1,0:T(8,128)(2,1)S(1)}, u32[]{:S(2)}, u32[]{:S(2)}) %collective-permute-start.5) | collective-permute-done | bytes 262176 | tf_op jit(solution)/shard_map/ppermute | solution.py:16
  125.3 0.3 fusion.3
  125.6 0.3 fusion.2
  125.9 19.9 %all_to_all.22 = bf16[64,16,256]{2,1,0:T(8,128)(2,1)S(1)} all-to-all(bf16[64,16,256]{2,1,0:T(8,128)(2,1)S(1)} %bitcast.109), channel_id=1, replica_groups=mesh['x'=4,'zb'=2,'za'=2,'zl'=2,'y'=8,'c'=2] {'x','zl','y'}, dimensions={0} | all-to-all | bytes 1048576 | tf_op jit(solution)/shard_map/all_to_all | solution.py:95
  146.0 12.7 %all_to_all.23 = bf16[16,16,256]{2,1,0:T(8,128)(2,1)S(1)} all-to-all(bf16[16,16,256]{2,1,0:T(8,128)(2,1)S(1)} %broadcast_in_dim.14), channel_id=1, replica_groups=mesh['x'=4,'zb'=2,'za'=2,'zl'=2,'y'=8,'c'=2] {'zl','y'}, dimensions={0} | all-to-all | bytes 262144 | tf_op jit(solution)/shard_map/all_to_all | solution.py:98
  158.7 4.4 %all_gather.39.total_ref = bf16[2,256,256]{2,1,0:T(8,128)(2,1)} all-gather(bf16[1,256,256]{2,1,0:T(8,128)(2,1)S(1)} %bitcast.114), channel_id=1, replica_groups=mesh['x'=4,'zb'=2,'za'=2,'zl'=2,'y'=8,'c'=2] {'c'}, dimensions={0}, use_global_device_ids=true | all-gather | bytes 393216 | tf_op jit(solution)/shard_map/all_gather | solution.py:101
  163.1 4.2 %shard_map.46 = f32[1024,512]{1,0:T(8,128)} custom-call(bf16[1024,512]{1,0:T(8,128)(2,1)} %bitcast.111, bf16[1024,256]{1,0:T(8,128)(2,1)} %bitcast.112, bf16[2,256,256]{2,1,0:T(8,128)(2,1)} %all_gather.39.total_ref), custom_call_target="tpu_custom_call" | custom-call | tf_op jit(solution)/shard_map/pallas_call | solution.py:43
  (29 shorter events, 2.5 us)
Async XLA Ops:
  0.0 1.0 copy-start
  0.0 11.4 %copy-start.1 = (bf16[4,1,1,2,256,256]{5,4,3,2,1,0:T(8,128)(2,1)S(1)}, bf16[4,1,1,2,256,256]{5,4,3,2,1,0:T(8,128)(2,1)}, u32[]{:S(2)}) copy-start(bf16[4,1,1,2,256,256]{5,4,3,2,1,0:T(8,128)(2,1)} %param.7) | copy-start | bytes 3145732
  12.1 11.1 %collective-permute-start = (bf16[256,256]{1,0:T(8,128)(2,1)}, bf16[256,256]{1,0:T(8,128)(2,1)}, u32[]{:S(2)}, u32[]{:S(2)}) collective-permute-start(bf16[256,256]{1,0:T(8,128)(2,1)} %get-tuple-element.12), channel_id=1, source_target_pairs={{0,256},{128,384},{256,0},{384,128},{1,257},{129,385},{257,1},{385... | collective-permute-start | bytes 393224 | tf_op jit(solution)/shard_map/ppermute | solution.py:16
  14.0 16.0 %collective-permute-start.2 = (bf16[2,256,256]{2,1,0:T(8,128)(2,1)S(1)}, bf16[2,256,256]{2,1,0:T(8,128)(2,1)S(1)}, u32[]{:S(2)}, u32[]{:S(2)}) collective-permute-start(bf16[2,256,256]{2,1,0:T(8,128)(2,1)S(1)} %constant_dynamic-slice_fusion), channel_id=1, source_target_pairs={{0,32},{32,0},{1,33},{33,1},{2,34},{34,2},{3,35},{35,3},{4,36},{36... | collective-permute-start | bytes 786440 | tf_op jit(solution)/shard_map/ppermute | solution.py:16
  17.3 3.1 %copy-start.2 = (bf16[1,1024,256]{2,1,0:T(8,128)(2,1)S(1)}, bf16[1,1024,256]{2,1,0:T(8,128)(2,1)}, u32[]{:S(2)}) copy-start(bf16[1,1024,256]{2,1,0:T(8,128)(2,1)} %param.6) | copy-start | bytes 1572868
  24.4 13.8 %collective-permute-start.1 = (bf16[512,256]{1,0:T(8,128)(2,1)S(1)}, bf16[512,256]{1,0:T(8,128)(2,1)S(1)}, u32[]{:S(2)}, u32[]{:S(2)}) collective-permute-start(bf16[512,256]{1,0:T(8,128)(2,1)S(1)} %convolution_convert_fusion.1), channel_id=1, source_target_pairs={{0,128},{128,0},{256,384},{384,256},{1,129},{129,1},{257,385},{385... | collective-permute-start | bytes 786440 | tf_op jit(solution)/shard_map/ppermute | solution.py:16
  30.2 15.9 %collective-permute-start.3 = (bf16[2,256,256]{2,1,0:T(8,128)(2,1)S(1)}, bf16[2,256,256]{2,1,0:T(8,128)(2,1)S(1)}, u32[]{:S(2)}, u32[]{:S(2)}) collective-permute-start(bf16[2,256,256]{2,1,0:T(8,128)(2,1)S(1)} %fusion.4), channel_id=1, source_target_pairs={{0,64},{64,0},{1,65},{65,1},{2,66},{66,2},{3,67},{67,3},{4,68},{68... | collective-permute-start | bytes 786440 | tf_op jit(solution)/shard_map/ppermute | solution.py:16
  83.1 23.4 %collective-permute-start.4 = (bf16[2,256,256]{2,1,0:T(8,128)(2,1)S(1)}, bf16[2,256,256]{2,1,0:T(8,128)(2,1)S(1)}, u32[]{:S(2)}, u32[]{:S(2)}) collective-permute-start(bf16[2,256,256]{2,1,0:T(8,128)(2,1)S(1)} %fusion.6), channel_id=1, source_target_pairs={{0,32},{32,0},{1,33},{33,1},{2,34},{34,2},{3,35},{35,3},{4,36},{36... | collective-permute-start | bytes 786440 | tf_op jit(solution)/shard_map/ppermute | solution.py:16
  106.8 18.3 %collective-permute-start.5 = (bf16[2,256,256]{2,1,0:T(8,128)(2,1)S(1)}, bf16[2,256,256]{2,1,0:T(8,128)(2,1)S(1)}, u32[]{:S(2)}, u32[]{:S(2)}) collective-permute-start(bf16[2,256,256]{2,1,0:T(8,128)(2,1)S(1)} %fusion.7), channel_id=1, source_target_pairs={{0,64},{64,0},{1,65},{65,1},{2,66},{66,2},{3,67},{67,3},{4,68},{68... | collective-permute-start | bytes 786440 | tf_op jit(solution)/shard_map/ppermute | solution.py:16

commit v2 on v1

--- a/solution.py
+++ b/solution.py
@@ -6,6 +6,7 @@
 from jax.sharding import Mesh, PartitionSpec as P
 
 ITERS = 2
+PARTS = 2
 BF = jnp.bfloat16
 F32 = jnp.float32
 LINE = ("zl", "y")
@@ -26,6 +27,23 @@
         turned = [blocks[d ^ bit] for d in range(len(blocks))]
         blocks = [jnp.where(me & bit == bit, t, b) for t, b in zip(turned, blocks)]
     return blocks
+
+
+def mix(pair, mine, partner):
+    return (mm("cij,cjr->cir", pair[:, 0], mine) + mm("cij,cjr->cir", pair[:, 1], partner)).astype(BF)
+
+
+def add_up(tail, coefficient):
+    spread = jnp.concatenate([mm("cij,cjr->ir", t, coefficient).astype(BF) for t in tail], 0)
+    count = lax.axis_size(("x",) + LINE)
+    pieces = spread.reshape(count, -1, coefficient.shape[2])
+    pieces = lax.all_to_all(pieces, ("x",) + LINE, 0, 0, tiled=True)
+    return jnp.sum(pieces.astype(F32), axis=0).astype(BF)
+
+
+def hand_out(share, rank):
+    copies = jnp.broadcast_to(share, (lax.axis_size(LINE), *share.shape))
+    return lax.all_to_all(copies, LINE, 0, 0, tiled=True).reshape(rank, -1)
 
 
 def finish_kernel(rhs_ref, basis_ref, total_ref, out_ref):
@@ -58,6 +76,7 @@
     basis = column_leaf_factors[0]
     out_basis = leaf_out[0]
     half = rhs.shape[1] // 2
+    part = half // PARTS
     rank = basis.shape[1]
     core = lax.axis_index("c")
 
@@ -81,23 +100,20 @@
     tail = by_target([kept[:rank], came[:rank], kept[rank:], came[rank:]])
     tail = [lax.all_gather(jnp.concatenate(tail[i : i + 2], 0), "c") for i in (0, 2)]
 
-    coefficient = first
+    parts = [first[:, :, i * part : (i + 1) * part] for i in range(PARTS)]
+    coefficients = list(parts)
     for iteration in range(ITERS):
         for level, axis in enumerate(("za", "zb")):
-            partner = swap(coefficient, axis, 1)
-            coefficient = (
-                mm("cij,cjr->cir", levels[level][:, 0], coefficient)
-                + mm("cij,cjr->cir", levels[level][:, 1], partner)
-            ).astype(BF)
-        spread = jnp.concatenate([mm("cij,cjr->ir", t, coefficient).astype(BF) for t in tail], 0)
-        count = lax.axis_size(("x",) + LINE)
-        pieces = spread.reshape(count, -1, half)
-        pieces = lax.all_to_all(pieces, ("x",) + LINE, 0, 0, tiled=True)
-        share = jnp.sum(pieces.astype(F32), axis=0).astype(BF)
-        copies = jnp.broadcast_to(share, (lax.axis_size(LINE), *share.shape))
-        total = lax.all_to_all(copies, LINE, 0, 0, tiled=True).reshape(rank, half)
+            for i in range(PARTS):
+                coefficients[i] = mix(levels[level], coefficients[i], swap(coefficients[i], axis, 1))
+        shares = [None] * PARTS
+        for i in range(PARTS):
+            shares[i] = add_up(tail, coefficients[i])
+        totals = [hand_out(share, rank) for share in shares]
         if iteration < ITERS - 1:
-            coefficient = (first.astype(F32) - mm("cij,jr->cir", gram, total)).astype(BF)
+            for i in range(PARTS):
+                coefficients[i] = (parts[i].astype(F32) - mm("cij,jr->cir", gram, totals[i])).astype(BF)
+    total = jnp.concatenate(totals, 1)
     total = lax.all_gather(total, "c")
     return finish(rhs, out_basis, total)[None]
 

time: 168 us -> 220 us (1.31)
  starting transfers between devices: 30.1 us -> 80.9 us
  blocking collectives: 91.4 us -> 42.8 us
  waiting for transfers between devices: 30.5 us -> 65.4 us
  matrix products: 7.49 us -> 15.8 us
  other arithmetic: 1.45 us -> 4.28 us
  local copies, waits for them, and re-layouts: 1.87 us -> 4.53 us
    all_to_all x0 -> x7, waiting for transfers between devices: none -> 59 us  [the longest x4 41.7 us: add_up(): pieces = lax.all_to_all(pieces, ('x',) + LINE, 0, 0, tiled=True)]
    all_to_all x4 -> x1, blocking collectives: 67.4 us -> 10.1 us  [hand_out(): return lax.all_to_all(copies, LINE, 0, 0, tiled=True).reshape(rank, -1)]
    all_to_all x0 -> x7, starting transfers between devices: none -> 44.4 us  [the longest x4 33.3 us: add_up(): pieces = lax.all_to_all(pieces, ('x',) + LINE, 0, 0, tiled=True)]
    ppermute x6 -> x10, waiting for transfers between devices: 30.5 us -> 6.34 us  [swap(): return lax.ppermute(block, axis, [(i, i ^ bit) for i in range(size)])]
    all_gather x1, blocking collectives: 4.41 us -> 14.3 us  [body(): total = lax.all_gather(total, 'c')]
    dot_general x17 -> x30, matrix products: 7.49 us -> 15.8 us  [mm(): return jnp.einsum(spec, a, b, preferred_element_type=F32)]
    ppermute x6 -> x10, starting transfers between devices: 30.1 us -> 36.5 us  [swap(): return lax.ppermute(block, axis, [(i, i ^ bit) for i in range(size)])]
    concatenate x2 -> x5, other arithmetic: 0.07 us -> 2.91 us  [the longest x4 2.89 us: add_up(): jnp.concatenate([mm('cij,cjr->ir', t, coefficient).astype(BF) for t in ta...]
  transfers between devices with their start and end apart: 6 -> 17, of which waited for: 4 -> 8; matrix products, arithmetic and copies ran while one was open for 2% -> 8% of each run, Pallas kernels for 0% -> 0%
where the time goes in v2:
time: 220 us; the launch traced here: 218 us
  starting transfers between devices  80.9 us (37%)
  waiting for transfers between devices  65.4 us (30%)
  blocking collectives  42.8 us (19%)
  matrix products  15.8 us (7%)
  local copies, waits for them, and re-layouts  4.53 us (2%)
  other arithmetic  4.28 us (2%)
  Pallas kernels  4.16 us (2%)
    all_to_all x4, waiting for transfers between devices, add_up(): pieces = lax.all_to_all(pieces, ('x',) + LINE, 0, 0, tiled=True)  41.7 us
    ppermute x10, starting transfers between devices, swap(): return lax.ppermute(block, axis, [(i, i ^ bit) for i in range(size)])  36.5 us
    all_to_all x4, starting transfers between devices, add_up(): pieces = lax.all_to_all(pieces, ('x',) + LINE, 0, 0, tiled=True)  33.3 us
    all_to_all x3, waiting for transfers between devices, hand_out(): return lax.all_to_all(copies, LINE, 0, 0, tiled=True).reshape(rank, -1)  17.3 us
    dot_general x30, matrix products, mm(): return jnp.einsum(spec, a, b, preferred_element_type=F32)  15.8 us
    all_gather x1, blocking collectives, body(): total = lax.all_gather(total, 'c')  14.3 us
    all_to_all x3, starting transfers between devices, hand_out(): return lax.all_to_all(copies, LINE, 0, 0, tiled=True).reshape(rank, -1)  11.2 us
    all_to_all x1, blocking collectives, hand_out(): return lax.all_to_all(copies, LINE, 0, 0, tiled=True).reshape(rank, -1)  10.1 us
  transfers between devices with their start and end apart: 17, of which 8 were waited for; matrix products, arithmetic and copies ran while one was open for 8% of the time, Pallas kernels for 0%

profile of v2, /device:TPU:1, one launch (start us, length us, event | category | flops | bytes accessed | tf_op | source)
XLA Modules:
  0.0 218.4 jit_solution(4971519687445754488)
XLA Ops:
  2.7 8.7 %all-gather = bf16[512,512]{1,0:T(8,128)(2,1)S(1)} all-gather(bf16[256,512]{1,0:T(8,128)(2,1)S(1)} %convolution_convert_fusion.2), channel_id=2, replica_groups=mesh['x'=4,'zb'=2,'za'=2,'zl'=2,'y'=8,'c'=2] {'c'}, dimensions={0}, use_global_device_ids=true | all-gather | bytes 786432 | tf_op jit(solution)/shard_map/all_gather | solution.py:84
  14.8 3.2 %collective-permute-start = (bf16[256,256]{1,0:T(8,128)(2,1)}, bf16[256,256]{1,0:T(8,128)(2,1)}, u32[]{:S(2)}, u32[]{:S(2)}) collective-permute-start(bf16[256,256]{1,0:T(8,128)(2,1)} %get-tuple-element.12), channel_id=1, source_target_pairs={{0,256},{128,384},{256,0},{384,128},{1,257},{129,385},{257,1},{385... | collective-permute-start | bytes 393224 | tf_op jit(solution)/shard_map/ppermute | solution.py:17
  18.0 3.0 %collective-permute-start.6 = (bf16[2,256,128]{2,1,0:T(8,128)(2,1)}, bf16[2,256,128]{2,1,0:T(8,128)(2,1)}, u32[]{:S(2)}, u32[]{:S(2)}) collective-permute-start(bf16[2,256,128]{2,1,0:T(8,128)(2,1)} %get-tuple-element.18), channel_id=1, source_target_pairs={{0,32},{32,0},{1,33},{33,1},{2,34},{34,2},{3,35},{35,3},{4,36},{36... | collective-permute-start | bytes 393224 | tf_op jit(solution)/shard_map/ppermute | solution.py:17
  21.1 2.7 %all-gather.3 = bf16[2,1,1,2,256,256]{5,4,0,3,2,1:T(8,128)(2,1)S(1)} all-gather(bf16[1,1,1,2,256,256]{5,4,0,3,2,1:T(8,128)(2,1)S(1)} %slice.98), channel_id=5, replica_groups=mesh['x'=4,'zb'=2,'za'=2,'zl'=2,'y'=8,'c'=2] {'c'}, dimensions={0}, use_global_device_ids=true | all-gather | bytes 786432 | tf_op jit(solution)/shard_map/all_gather | solution.py:91
  26.5 2.4 %all-gather.2 = bf16[6,256,256]{2,1,0:T(8,128)(2,1)S(1)} all-gather(bf16[3,256,256]{2,1,0:T(8,128)(2,1)S(1)} %pad_maximum_fusion), channel_id=4, replica_groups=mesh['x'=4,'zb'=2,'za'=2,'zl'=2,'y'=8,'c'=2] {'c'}, dimensions={0}, use_global_device_ids=true | all-gather | bytes 1179648 | tf_op jit(solution)/shard_map/all_gather | solution.py:93
  30.0 8.3 %collective-permute-start.3 = (bf16[2,256,128]{2,1,0:T(8,128)(2,1)S(1)}, bf16[2,256,128]{2,1,0:T(8,128)(2,1)S(1)}, u32[]{:S(2)}, u32[]{:S(2)}) collective-permute-start(bf16[2,256,128]{2,1,0:T(8,128)(2,1)S(1)} %fusion), channel_id=1, source_target_pairs={{0,64},{64,0},{1,65},{65,1},{2,66},{66,2},{3,67},{67,3},{4,68},{68... | collective-permute-start | bytes 393224 | tf_op jit(solution)/shard_map/ppermute | solution.py:17
  39.6 1.9 collective-permute-start.7
  42.9 2.2 %collective-permute-start.1 = (bf16[512,256]{1,0:T(8,128)(2,1)S(1)}, bf16[512,256]{1,0:T(8,128)(2,1)S(1)}, u32[]{:S(2)}, u32[]{:S(2)}) collective-permute-start(bf16[512,256]{1,0:T(8,128)(2,1)S(1)} %convolution_convert_fusion.1), channel_id=1, source_target_pairs={{0,128},{128,0},{256,384},{384,256},{1,129},{129,1},{257,385},{385... | collective-permute-start | bytes 786440 | tf_op jit(solution)/shard_map/ppermute | solution.py:17
  46.5 6.3 %collective-permute-done.7 = bf16[2,256,128]{2,1,0:T(8,128)(2,1)S(1)} collective-permute-done((bf16[2,256,128]{2,1,0:T(8,128)(2,1)S(1)}, bf16[2,256,128]{2,1,0:T(8,128)(2,1)S(1)}, u32[]{:S(2)}, u32[]{:S(2)}) %collective-permute-start.7) | collective-permute-done | bytes 131104 | tf_op jit(solution)/shard_map/ppermute | solution.py:17
  53.2 2.4 %all-gather.1 = bf16[1024,256]{1,0:T(8,128)(2,1)S(1)} all-gather(bf16[512,256]{1,0:T(8,128)(2,1)S(1)} %pad_maximum_fusion.2), channel_id=3, replica_groups=mesh['x'=4,'zb'=2,'za'=2,'zl'=2,'y'=8,'c'=2] {'c'}, dimensions={0}, use_global_device_ids=true | all-gather | bytes 786432 | tf_op jit(solution)/shard_map/all_gather | solution.py:101
  55.6 2.2 all-gather.4
  59.1 10.0 %all-to-all-start = ((bf16[64,16,128]{2,1,0:T(8,128)(2,1)}), bf16[64,16,128]{2,1,0:T(8,128)(2,1)S(1)}, u32[]{:S(2)}, u32[]{:S(2)}) async-start(bf16[64,16,128]{2,1,0:T(8,128)(2,1)} %bitcast.170), calls=%async_computation | async-start | bytes 524288 | tf_op jit(solution)/shard_map/all_to_all | solution.py:40
  70.4 10.6 %all-to-all-done = bf16[64,16,128]{2,1,0:T(8,128)(2,1)S(1)} async-done(((bf16[64,16,128]{2,1,0:T(8,128)(2,1)}), bf16[64,16,128]{2,1,0:T(8,128)(2,1)S(1)}, u32[]{:S(2)}, u32[]{:S(2)}) %all-to-all-start) | async-done | bytes 262176 | tf_op jit(solution)/shard_map/all_to_all | solution.py:40
  81.0 5.9 %all-to-all-start.4 = ((bf16[64,16,128]{2,1,0:T(8,128)(2,1)}), bf16[64,16,128]{2,1,0:T(8,128)(2,1)}, u32[]{:S(2)}, u32[]{:S(2)}) async-start(bf16[64,16,128]{2,1,0:T(8,128)(2,1)} %bitcast.169), calls=%async_computation.4 | async-start | bytes 524288 | tf_op jit(solution)/shard_map/all_to_all | solution.py:40
  87.0 10.8 %all-to-all-done.4 = bf16[64,16,128]{2,1,0:T(8,128)(2,1)} async-done(((bf16[64,16,128]{2,1,0:T(8,128)(2,1)}), bf16[64,16,128]{2,1,0:T(8,128)(2,1)}, u32[]{:S(2)}, u32[]{:S(2)}) %all-to-all-start.4) | async-done | bytes 262176 | tf_op jit(solution)/shard_map/all_to_all | solution.py:40
  98.4 3.5 %all-to-all-start.1 = ((bf16[16,16,128]{2,1,0:T(8,128)(2,1)}), bf16[16,16,128]{2,1,0:T(8,128)(2,1)S(1)}, u32[]{:S(2)}, u32[]{:S(2)}) async-start(bf16[16,16,128]{2,1,0:T(8,128)(2,1)} %broadcast_in_dim.19), calls=%async_computation.1 | async-start | bytes 131072 | tf_op jit(solution)/shard_map/all_to_all | solution.py:46
  102.9 6.3 %all-to-all-done.1 = bf16[16,16,128]{2,1,0:T(8,128)(2,1)S(1)} async-done(((bf16[16,16,128]{2,1,0:T(8,128)(2,1)}), bf16[16,16,128]{2,1,0:T(8,128)(2,1)S(1)}, u32[]{:S(2)}, u32[]{:S(2)}) %all-to-all-start.1) | async-done | bytes 65568 | tf_op jit(solution)/shard_map/all_to_all | solution.py:46
  109.9 4.2 %all-to-all-start.5 = ((bf16[16,16,128]{2,1,0:T(8,128)(2,1)}), bf16[16,16,128]{2,1,0:T(8,128)(2,1)}, u32[]{:S(2)}, u32[]{:S(2)}) async-start(bf16[16,16,128]{2,1,0:T(8,128)(2,1)} %broadcast_in_dim.21), calls=%async_computation.5 | async-start | bytes 131072 | tf_op jit(solution)/shard_map/all_to_all | solution.py:46
  114.3 3.2 %collective-permute-start.4 = (bf16[2,256,128]{2,1,0:T(8,128)(2,1)S(1)}, bf16[2,256,128]{2,1,0:T(8,128)(2,1)}, u32[]{:S(2)}, u32[]{:S(2)}) collective-permute-start(bf16[2,256,128]{2,1,0:T(8,128)(2,1)S(1)} %fusion.2), channel_id=1, source_target_pairs={{0,32},{32,0},{1,33},{33,1},{2,34},{34,2},{3,35},{35,3},{4,36},{36... | collective-permute-start | bytes 393224 | tf_op jit(solution)/shard_map/ppermute | solution.py:17
  117.7 3.8 %all-to-all-done.5 = bf16[16,16,128]{2,1,0:T(8,128)(2,1)} async-done(((bf16[16,16,128]{2,1,0:T(8,128)(2,1)}), bf16[16,16,128]{2,1,0:T(8,128)(2,1)}, u32[]{:S(2)}, u32[]{:S(2)}) %all-to-all-start.5) | async-done | bytes 65568 | tf_op jit(solution)/shard_map/all_to_all | solution.py:46
  122.5 3.2 %collective-permute-start.8 = (bf16[2,256,128]{2,1,0:T(8,128)(2,1)S(1)}, bf16[2,256,128]{2,1,0:T(8,128)(2,1)S(1)}, u32[]{:S(2)}, u32[]{:S(2)}) collective-permute-start(bf16[2,256,128]{2,1,0:T(8,128)(2,1)S(1)} %fusion.7), channel_id=1, source_target_pairs={{0,32},{32,0},{1,33},{33,1},{2,34},{34,2},{3,35},{35,3},{4,36},{36... | collective-permute-start | bytes 393224 | tf_op jit(solution)/shard_map/ppermute | solution.py:17
  127.0 7.3 %collective-permute-start.5 = (bf16[2,256,128]{2,1,0:T(8,128)(2,1)S(1)}, bf16[2,256,128]{2,1,0:T(8,128)(2,1)S(1)}, u32[]{:S(2)}, u32[]{:S(2)}) collective-permute-start(bf16[2,256,128]{2,1,0:T(8,128)(2,1)S(1)} %fusion.3), channel_id=1, source_target_pairs={{0,64},{64,0},{1,65},{65,1},{2,66},{66,2},{3,67},{67,3},{4,68},{68... | collective-permute-start | bytes 393224 | tf_op jit(solution)/shard_map/ppermute | solution.py:17
  134.7 2.4 %collective-permute-start.9 = (bf16[2,256,128]{2,1,0:T(8,128)(2,1)S(1)}, bf16[2,256,128]{2,1,0:T(8,128)(2,1)S(1)}, u32[]{:S(2)}, u32[]{:S(2)}) collective-permute-start(bf16[2,256,128]{2,1,0:T(8,128)(2,1)S(1)} %fusion.8), channel_id=1, source_target_pairs={{0,64},{64,0},{1,65},{65,1},{2,66},{66,2},{3,67},{67,3},{4,68},{68... | collective-permute-start | bytes 393224 | tf_op jit(solution)/shard_map/ppermute | solution.py:17
  138.9 12.8 %all-to-all-start.2 = ((bf16[64,16,128]{2,1,0:T(8,128)(2,1)}), bf16[64,16,128]{2,1,0:T(8,128)(2,1)S(1)}, u32[]{:S(2)}, u32[]{:S(2)}) async-start(bf16[64,16,128]{2,1,0:T(8,128)(2,1)} %bitcast.26), calls=%async_computation.2 | async-start | bytes 524288 | tf_op jit(solution)/shard_map/all_to_all | solution.py:40
  153.2 9.4 %all-to-all-done.2 = bf16[64,16,128]{2,1,0:T(8,128)(2,1)S(1)} async-done(((bf16[64,16,128]{2,1,0:T(8,128)(2,1)}), bf16[64,16,128]{2,1,0:T(8,128)(2,1)S(1)}, u32[]{:S(2)}, u32[]{:S(2)}) %all-to-all-start.2) | async-done | bytes 262176 | tf_op jit(solution)/shard_map/all_to_all | solution.py:40
  162.7 4.6 %all-to-all-start.6 = ((bf16[64,16,128]{2,1,0:T(8,128)(2,1)}), bf16[64,16,128]{2,1,0:T(8,128)(2,1)S(1)}, u32[]{:S(2)}, u32[]{:S(2)}) async-start(bf16[64,16,128]{2,1,0:T(8,128)(2,1)} %bitcast.35), calls=%async_computation.6 | async-start | bytes 524288 | tf_op jit(solution)/shard_map/all_to_all | solution.py:40
  167.4 10.9 %all-to-all-done.6 = bf16[64,16,128]{2,1,0:T(8,128)(2,1)S(1)} async-done(((bf16[64,16,128]{2,1,0:T(8,128)(2,1)}), bf16[64,16,128]{2,1,0:T(8,128)(2,1)S(1)}, u32[]{:S(2)}, u32[]{:S(2)}) %all-to-all-start.6) | async-done | bytes 262176 | tf_op jit(solution)/shard_map/all_to_all | solution.py:40
  178.9 3.5 %all-to-all-start.3 = ((bf16[16,16,128]{2,1,0:T(8,128)(2,1)}), bf16[16,16,128]{2,1,0:T(8,128)(2,1)S(1)}, u32[]{:S(2)}, u32[]{:S(2)}) async-start(bf16[16,16,128]{2,1,0:T(8,128)(2,1)} %broadcast_in_dim.20), calls=%async_computation.3 | async-start | bytes 131072 | tf_op jit(solution)/shard_map/all_to_all | solution.py:46
  182.5 7.3 %all-to-all-done.3 = bf16[16,16,128]{2,1,0:T(8,128)(2,1)S(1)} async-done(((bf16[16,16,128]{2,1,0:T(8,128)(2,1)}), bf16[16,16,128]{2,1,0:T(8,128)(2,1)S(1)}, u32[]{:S(2)}, u32[]{:S(2)}) %all-to-all-start.3) | async-done | bytes 65568 | tf_op jit(solution)/shard_map/all_to_all | solution.py:46
  189.8 10.1 %all_to_all.40 = bf16[16,16,128]{2,1,0:T(8,128)(2,1)S(1)} all-to-all(bf16[16,16,128]{2,1,0:T(8,128)(2,1)S(1)} %broadcast_in_dim.22), channel_id=1, replica_groups=mesh['x'=4,'zb'=2,'za'=2,'zl'=2,'y'=8,'c'=2] {'zl','y'}, dimensions={0} | all-to-all | bytes 131072 | tf_op jit(solution)/shard_map/all_to_all | solution.py:46
  199.9 14.3 %all-gather.5 = bf16[512,256]{1,0:T(8,128)(2,1)} all-gather(bf16[256,256]{1,0:T(8,128)(2,1)S(1)} %pad_maximum_fusion.10), channel_id=7, replica_groups=mesh['x'=4,'zb'=2,'za'=2,'zl'=2,'y'=8,'c'=2] {'c'}, dimensions={0}, use_global_device_ids=true | all-gather | bytes 393216 | tf_op jit(solution)/shard_map/all_gather | solution.py:117
  214.2 4.2 %shard_map.46 = f32[1024,512]{1,0:T(8,128)} custom-call(bf16[1024,512]{1,0:T(8,128)(2,1)} %bitcast.171, bf16[1024,256]{1,0:T(8,128)(2,1)} %bitcast.173, bf16[2,256,256]{2,1,0:T(8,128)(2,1)} %bitcast.172), custom_call_target="tpu_custom_call" | custom-call | tf_op jit(solution)/shard_map/pallas_call | solution.py:61
  (69 shorter events, 26.6 us)
Async XLA Ops:
  0.0 1.0 copy-start
  0.0 14.1 %copy-start.1 = (bf16[4,1,1,2,256,256]{5,4,3,2,1,0:T(8,128)(2,1)S(1)}, bf16[4,1,1,2,256,256]{5,4,3,2,1,0:T(8,128)(2,1)}, u32[]{:S(2)}) copy-start(bf16[4,1,1,2,256,256]{5,4,3,2,1,0:T(8,128)(2,1)} %param.7) | copy-start | bytes 3145732
  12.2 16.7 %collective-permute-start.2 = (bf16[2,256,128]{2,1,0:T(8,128)(2,1)}, bf16[2,256,128]{2,1,0:T(8,128)(2,1)}, u32[]{:S(2)}, u32[]{:S(2)}) collective-permute-start(bf16[2,256,128]{2,1,0:T(8,128)(2,1)} %get-tuple-element.17), channel_id=1, source_target_pairs={{0,32},{32,0},{1,33},{33,1},{2,34},{34,2},{3,35},{35,3},{4,36},{36... | collective-permute-start | bytes 393224 | tf_op jit(solution)/shard_map/ppermute | solution.py:17
  14.8 27.0 %collective-permute-start = (bf16[256,256]{1,0:T(8,128)(2,1)}, bf16[256,256]{1,0:T(8,128)(2,1)}, u32[]{:S(2)}, u32[]{:S(2)}) collective-permute-start(bf16[256,256]{1,0:T(8,128)(2,1)} %get-tuple-element.12), channel_id=1, source_target_pairs={{0,256},{128,384},{256,0},{384,128},{1,257},{129,385},{257,1},{385... | collective-permute-start | bytes 393224 | tf_op jit(solution)/shard_map/ppermute | solution.py:17
  18.0 20.5 %collective-permute-start.6 = (bf16[2,256,128]{2,1,0:T(8,128)(2,1)}, bf16[2,256,128]{2,1,0:T(8,128)(2,1)}, u32[]{:S(2)}, u32[]{:S(2)}) collective-permute-start(bf16[2,256,128]{2,1,0:T(8,128)(2,1)} %get-tuple-element.18), channel_id=1, source_target_pairs={{0,32},{32,0},{1,33},{33,1},{2,34},{34,2},{3,35},{35,3},{4,36},{36... | collective-permute-start | bytes 393224 | tf_op jit(solution)/shard_map/ppermute | solution.py:17
  25.0 3.9 %copy-start.2 = (f32[2,256,128]{2,1,0:T(8,128)S(1)}, f32[2,256,128]{2,1,0:T(8,128)}, u32[]{:S(2)}) copy-start(f32[2,256,128]{2,1,0:T(8,128)} %fusion.26) | copy-start | bytes 786436
  30.0 16.3 %collective-permute-start.3 = (bf16[2,256,128]{2,1,0:T(8,128)(2,1)S(1)}, bf16[2,256,128]{2,1,0:T(8,128)(2,1)S(1)}, u32[]{:S(2)}, u32[]{:S(2)}) collective-permute-start(bf16[2,256,128]{2,1,0:T(8,128)(2,1)S(1)} %fusion), channel_id=1, source_target_pairs={{0,64},{64,0},{1,65},{65,1},{2,66},{66,2},{3,67},{67,3},{4,68},{68... | collective-permute-start | bytes 393224 | tf_op jit(solution)/shard_map/ppermute | solution.py:17
  39.6 13.2 %collective-permute-start.7 = (bf16[2,256,128]{2,1,0:T(8,128)(2,1)S(1)}, bf16[2,256,128]{2,1,0:T(8,128)(2,1)S(1)}, u32[]{:S(2)}, u32[]{:S(2)}) collective-permute-start(bf16[2,256,128]{2,1,0:T(8,128)(2,1)S(1)} %fusion.5), channel_id=1, source_target_pairs={{0,64},{64,0},{1,65},{65,1},{2,66},{66,2},{3,67},{67,3},{4,68},{68... | collective-permute-start | bytes 393224 | tf_op jit(solution)/shard_map/ppermute | solution.py:17
  42.9 10.1 %collective-permute-start.1 = (bf16[512,256]{1,0:T(8,128)(2,1)S(1)}, bf16[512,256]{1,0:T(8,128)(2,1)S(1)}, u32[]{:S(2)}, u32[]{:S(2)}) collective-permute-start(bf16[512,256]{1,0:T(8,128)(2,1)S(1)} %convolution_convert_fusion.1), channel_id=1, source_target_pairs={{0,128},{128,0},{256,384},{384,256},{1,129},{129,1},{257,385},{385... | collective-permute-start | bytes 786440 | tf_op jit(solution)/shard_map/ppermute | solution.py:17
  59.1 21.9 %all-to-all-start = ((bf16[64,16,128]{2,1,0:T(8,128)(2,1)}), bf16[64,16,128]{2,1,0:T(8,128)(2,1)S(1)}, u32[]{:S(2)}, u32[]{:S(2)}) async-start(bf16[64,16,128]{2,1,0:T(8,128)(2,1)} %bitcast.170), calls=%async_computation | async-start | bytes 524288 | tf_op jit(solution)/shard_map/all_to_all | solution.py:40
  81.0 16.7 %all-to-all-start.4 = ((bf16[64,16,128]{2,1,0:T(8,128)(2,1)}), bf16[64,16,128]{2,1,0:T(8,128)(2,1)}, u32[]{:S(2)}, u32[]{:S(2)}) async-start(bf16[64,16,128]{2,1,0:T(8,128)(2,1)} %bitcast.169), calls=%async_computation.4 | async-start | bytes 524288 | tf_op jit(solution)/shard_map/all_to_all | solution.py:40
  98.4 10.8 %all-to-all-start.1 = ((bf16[16,16,128]{2,1,0:T(8,128)(2,1)}), bf16[16,16,128]{2,1,0:T(8,128)(2,1)S(1)}, u32[]{:S(2)}, u32[]{:S(2)}) async-start(bf16[16,16,128]{2,1,0:T(8,128)(2,1)} %broadcast_in_dim.19), calls=%async_computation.1 | async-start | bytes 131072 | tf_op jit(solution)/shard_map/all_to_all | solution.py:46
  109.9 11.5 %all-to-all-start.5 = ((bf16[16,16,128]{2,1,0:T(8,128)(2,1)}), bf16[16,16,128]{2,1,0:T(8,128)(2,1)}, u32[]{:S(2)}, u32[]{:S(2)}) async-start(bf16[16,16,128]{2,1,0:T(8,128)(2,1)} %broadcast_in_dim.21), calls=%async_computation.5 | async-start | bytes 131072 | tf_op jit(solution)/shard_map/all_to_all | solution.py:46
  114.3 11.6 %collective-permute-start.4 = (bf16[2,256,128]{2,1,0:T(8,128)(2,1)S(1)}, bf16[2,256,128]{2,1,0:T(8,128)(2,1)}, u32[]{:S(2)}, u32[]{:S(2)}) collective-permute-start(bf16[2,256,128]{2,1,0:T(8,128)(2,1)S(1)} %fusion.2), channel_id=1, source_target_pairs={{0,32},{32,0},{1,33},{33,1},{2,34},{34,2},{3,35},{35,3},{4,36},{36... | collective-permute-start | bytes 393224 | tf_op jit(solution)/shard_map/ppermute | solution.py:17
  122.5 12.0 %collective-permute-start.8 = (bf16[2,256,128]{2,1,0:T(8,128)(2,1)S(1)}, bf16[2,256,128]{2,1,0:T(8,128)(2,1)S(1)}, u32[]{:S(2)}, u32[]{:S(2)}) collective-permute-start(bf16[2,256,128]{2,1,0:T(8,128)(2,1)S(1)} %fusion.7), channel_id=1, source_target_pairs={{0,32},{32,0},{1,33},{33,1},{2,34},{34,2},{3,35},{35,3},{4,36},{36... | collective-permute-start | bytes 393224 | tf_op jit(solution)/shard_map/ppermute | solution.py:17
  127.0 10.4 %collective-permute-start.5 = (bf16[2,256,128]{2,1,0:T(8,128)(2,1)S(1)}, bf16[2,256,128]{2,1,0:T(8,128)(2,1)S(1)}, u32[]{:S(2)}, u32[]{:S(2)}) collective-permute-start(bf16[2,256,128]{2,1,0:T(8,128)(2,1)S(1)} %fusion.3), channel_id=1, source_target_pairs={{0,64},{64,0},{1,65},{65,1},{2,66},{66,2},{3,67},{67,3},{4,68},{68... | collective-permute-start | bytes 393224 | tf_op jit(solution)/shard_map/ppermute | solution.py:17
  134.7 17.0 %collective-permute-start.9 = (bf16[2,256,128]{2,1,0:T(8,128)(2,1)S(1)}, bf16[2,256,128]{2,1,0:T(8,128)(2,1)S(1)}, u32[]{:S(2)}, u32[]{:S(2)}) collective-permute-start(bf16[2,256,128]{2,1,0:T(8,128)(2,1)S(1)} %fusion.8), channel_id=1, source_target_pairs={{0,64},{64,0},{1,65},{65,1},{2,66},{66,2},{3,67},{67,3},{4,68},{68... | collective-permute-start | bytes 393224 | tf_op jit(solution)/shard_map/ppermute | solution.py:17
  138.9 23.7 %all-to-all-start.2 = ((bf16[64,16,128]{2,1,0:T(8,128)(2,1)}), bf16[64,16,128]{2,1,0:T(8,128)(2,1)S(1)}, u32[]{:S(2)}, u32[]{:S(2)}) async-start(bf16[64,16,128]{2,1,0:T(8,128)(2,1)} %bitcast.26), calls=%async_computation.2 | async-start | bytes 524288 | tf_op jit(solution)/shard_map/all_to_all | solution.py:40
  162.7 15.6 %all-to-all-start.6 = ((bf16[64,16,128]{2,1,0:T(8,128)(2,1)}), bf16[64,16,128]{2,1,0:T(8,128)(2,1)S(1)}, u32[]{:S(2)}, u32[]{:S(2)}) async-start(bf16[64,16,128]{2,1,0:T(8,128)(2,1)} %bitcast.35), calls=%async_computation.6 | async-start | bytes 524288 | tf_op jit(solution)/shard_map/all_to_all | solution.py:40
  178.9 10.8 %all-to-all-start.3 = ((bf16[16,16,128]{2,1,0:T(8,128)(2,1)}), bf16[16,16,128]{2,1,0:T(8,128)(2,1)S(1)}, u32[]{:S(2)}, u32[]{:S(2)}) async-start(bf16[16,16,128]{2,1,0:T(8,128)(2,1)} %broadcast_in_dim.20), calls=%async_computation.3 | async-start | bytes 131072 | tf_op jit(solution)/shard_map/all_to_all | solution.py:46

commit v3 on v1

v3 whole, which is shorter than its diff:
```python
import jax
import jax.numpy as jnp
from jax import lax
from jax.experimental import pallas as pl
from jax.experimental.pallas import tpu as pltpu
from jax.sharding import Mesh, PartitionSpec as P

BF = jnp.bfloat16
F32 = jnp.float32
LINE = ("zl", "y")
QUAD = ("zb", "za")
CHUNKS = 4


def swap(block, axis, bit):
    size = lax.axis_size(axis)
    return lax.ppermute(block, axis, [(i, i ^ bit) for i in range(size)])


def mm(spec, a, b):
    return jnp.einsum(spec, a, b, preferred_element_type=F32)


def dot(a, b):
    return jnp.dot(a, b, preferred_element_type=F32)


def in_order(blocks, axis):
    me = lax.axis_index(axis)
    for bit in (1, 2):
        turned = [blocks[d ^ bit] for d in range(len(blocks))]
        blocks = [jnp.where(me & bit == bit, t, b) for t, b in zip(turned, blocks)]
    return blocks


def add_up(tail, coefficient):
    spread = jnp.concatenate([mm("cij,cjr->ir", t, coefficient).astype(BF) for t in tail], 0)
    group = ("x",) + LINE
    pieces = spread.reshape(lax.axis_size(group), -1, coefficient.shape[2])
    pieces = lax.all_to_all(pieces, group, 0, 0, tiled=True)
    return jnp.sum(pieces.astype(F32), axis=0).astype(BF)


def hand_out(share, axes):
    copies = jnp.broadcast_to(share, (lax.axis_size(axes), *share.shape))
    return lax.all_to_all(copies, axes, 0, 0, tiled=True)


def finish_kernel(rhs_hbm, basis_hbm, total_hbm, out_hbm, rhs, basis, total, out, sems):
    rows = rhs.shape[0] // CHUNKS
    half = total.shape[2]
    first = pltpu.make_async_copy(total_hbm, total, sems.at[0, CHUNKS])
    first.start()
    loads = []
    for i in range(CHUNKS):
        part = pl.ds(i * rows, rows)
        loads.append(
            (
                pltpu.make_async_copy(basis_hbm.at[part], basis.at[part], sems.at[0, i]),
                pltpu.make_async_copy(rhs_hbm.at[part], rhs.at[part], sems.at[1, i]),
            )
        )
        for load in loads[-1]:
            load.start()
    first.wait()
    stores = []
    for i in range(CHUNKS):
        part = pl.ds(i * rows, rows)
        for load in loads[i]:
            load.wait()
        for core in range(2):
            cols = slice(core * half, (core + 1) * half)
            out[part, cols] = rhs[part, cols].astype(F32) - dot(basis[part], total[core])
        stores.append(pltpu.make_async_copy(out.at[part], out_hbm.at[part], sems.at[2, i]))
        stores[-1].start()
    for store in stores:
        store.wait()


def finish(rhs, basis, total):
    return pl.pallas_call(
        finish_kernel,
        in_specs=[pl.BlockSpec(memory_space=pl.ANY)] * 3,
        out_specs=pl.BlockSpec(memory_space=pl.ANY),
        out_shape=jax.ShapeDtypeStruct(rhs.shape, F32),
        scratch_shapes=[
            pltpu.VMEM(rhs.shape, BF),
            pltpu.VMEM(basis.shape, BF),
            pltpu.VMEM(total.shape, BF),
            pltpu.VMEM(rhs.shape, F32),
            pltpu.SemaphoreType.DMA((3, CHUNKS + 1)),
        ],
        compiler_params=pltpu.CompilerParams(vmem_limit_bytes=16 * 1024 * 1024),
    )(rhs, basis, total)


def body(right_side, column_leaf_factors, leaf_out, transfer):
    rhs, basis, out_basis = right_side[0], column_leaf_factors[0], leaf_out[0]
    half = rhs.shape[1] // 2
    rank = basis.shape[1]
    core = lax.axis_index("c")

    start = mm("lk,lr->kr", basis, rhs).astype(BF)
    start, transfer, basis, out_late = lax.optimization_barrier((start, transfer, basis, out_basis))
    own = transfer[:, 0, 0, 0]
    other = transfer[:, 0, 0, 1]
    gram = mm("li,lj->ij", basis, out_late).astype(BF)
    gram, far = lax.optimization_barrier((gram, other[3]))
    far = swap(far, "x", 2)

    field = (dot(own[0], start) + dot(other[0], swap(start, "za", 1))).astype(BF)
    near = swap(gram, "za", 1)
    field, near = lax.optimization_barrier((field, near))
    chain = jnp.concatenate([dot(own[0], gram).astype(BF), dot(other[0], near).astype(BF)], 1)
    field = (dot(own[1], field) + dot(other[1], swap(field, "zb", 1))).astype(BF)

    wide = jnp.concatenate([own[3], far], 0)
    kept = dot(wide, own[2]).astype(BF)
    came = swap(dot(wide, other[2]).astype(BF), "x", 1)
    tail = in_order([kept[:rank], came[:rank], kept[rank:], came[rank:]], "x")
    tail = [lax.all_gather(jnp.concatenate(tail[i : i + 2], 0), "c") for i in (0, 2)]

    field = lax.all_gather(field, "c")
    field = lax.dynamic_slice_in_dim(field, core * half, half, 2)
    share = add_up(tail, field)
    totals = hand_out(share, QUAD + LINE).reshape(2, 2 * rank, half)

    chain_far = swap(chain, "zb", 1)
    mine = dot(own[1], chain).astype(BF)
    theirs = dot(other[1], chain_far).astype(BF)
    back = in_order([mine[:, :rank], mine[:, rank:], theirs[:, :rank], theirs[:, rank:]], QUAD)
    back = [lax.all_gather(jnp.concatenate(back[i : i + 2], 1), "c") for i in (0, 2)]

    change = mm("cij,jr->cir", back[0], totals[0]) + mm("cij,jr->cir", back[1], totals[1])
    field = (field.astype(F32) - change).astype(BF)
    share = add_up(tail, field)
    total = hand_out(share, LINE).reshape(rank, half)
    return finish(rhs, out_basis, lax.all_gather(total, "c"))[None]


def solution(mesh):
    devices = mesh.devices.reshape(4, 2, 2, 2, 8, 2)
    fine = Mesh(devices, ("x", "zb", "za", "zl", "y", "c"))
    bfly, cols = ("x", "zb", "za"), ("zl", "y", "c")
    in_specs = (
        P(bfly, cols, None),
        P(bfly, cols, None),
        P(bfly, cols, None),
        P(None, bfly, cols, None, None, None),
    )
    out_specs = P(bfly, cols, None)
    return jax.shard_map(body, mesh=fine, in_specs=in_specs, out_specs=out_specs, check_vma=False)
```

time: 168 us -> 155 us (0.923)
  blocking collectives: 91.4 us -> 59.5 us
  starting transfers between devices: 30.1 us -> 48.7 us
  matrix products: 7.49 us -> 11.9 us
  waiting for transfers between devices: 30.5 us -> 26.7 us
    all_to_all x4 -> x2, blocking collectives: 67.4 us -> 33.9 us  [the longest x1 21.4 us: add_up(): pieces = lax.all_to_all(pieces, group, 0, 0, tiled=True)]
    ppermute x6, waiting for transfers between devices: 30.5 us -> 11.9 us  [swap(): return lax.ppermute(block, axis, [(i, i ^ bit) for i in range(size)])]
    all_to_all x0 -> x2, starting transfers between devices: none -> 18.4 us  [the longest x1 10 us: hand_out(): return lax.all_to_all(copies, axes, 0, 0, tiled=True)]
    all_to_all x0 -> x2, waiting for transfers between devices: none -> 14.7 us  [the longest x1 8.27 us: add_up(): pieces = lax.all_to_all(pieces, group, 0, 0, tiled=True)]
    dot_general x0 -> x10, matrix products: none -> 6.96 us  [dot(): return jnp.dot(a, b, preferred_element_type=F32)]
    dot_general x17 -> x8, matrix products: 7.49 us -> 4.99 us  [mm(): return jnp.einsum(spec, a, b, preferred_element_type=F32)]
  transfers between devices with their start and end apart: 6 -> 8, of which waited for: 4 -> 5; matrix products, arithmetic and copies ran while one was open for 2% -> 5% of each run, Pallas kernels for 0% -> 0%
where the time goes in v3:
time: 155 us; the launch traced here: 154 us
  blocking collectives  59.5 us (38%)
  starting transfers between devices  48.7 us (31%)
  waiting for transfers between devices  26.7 us (17%)
  matrix products  11.9 us (8%)
  Pallas kernels  2.61 us (2%)
  local copies, waits for them, and re-layouts  2.37 us (2%)
  other arithmetic  1.98 us (1%)
    ppermute x6, starting transfers between devices, swap(): return lax.ppermute(block, axis, [(i, i ^ bit) for i in range(size)])  30.3 us
    all_to_all x1, blocking collectives, add_up(): pieces = lax.all_to_all(pieces, group, 0, 0, tiled=True)  21.4 us
    all_to_all x1, blocking collectives, hand_out(): return lax.all_to_all(copies, axes, 0, 0, tiled=True)  12.6 us
    ppermute x6, waiting for transfers between devices, swap(): return lax.ppermute(block, axis, [(i, i ^ bit) for i in range(size)])  11.9 us
    all_to_all x1, starting transfers between devices, hand_out(): return lax.all_to_all(copies, axes, 0, 0, tiled=True)  10 us
    all_to_all x1, starting transfers between devices, add_up(): pieces = lax.all_to_all(pieces, group, 0, 0, tiled=True)  8.41 us
    all_to_all x1, waiting for transfers between devices, add_up(): pieces = lax.all_to_all(pieces, group, 0, 0, tiled=True)  8.27 us
    dot_general x10, matrix products, dot(): return jnp.dot(a, b, preferred_element_type=F32)  6.96 us
  transfers between devices with their start and end apart: 8, of which 5 were waited for; matrix products, arithmetic and copies ran while one was open for 5% of the time, Pallas kernels for 0%

profile of v3, /device:TPU:1, one launch (start us, length us, event | category | flops | bytes accessed | tf_op | source)
XLA Modules:
  0.0 154.2 jit_solution(4568424788840418470)
XLA Ops:
  0.0 1.0 copy-done
  1.0 1.8 %convolution_convert_fusion.4 = bf16[256,512]{1,0:T(8,128)(2,1)S(1)} fusion(bf16[1,1024,256]{2,1,0:T(8,128)(2,1)S(1)} %copy-done, bf16[1,1024,512]{2,1,0:T(8,128)(2,1)} %param.4), kind=kOutput, calls=%fused_computation.17 | convolution fusion | flops 268566528 | bytes 1835008 | tf_op jit(solution)/shard_map/lk,lr->kr/dot_general | solution.py:21
  3.2 5.5 %collective-permute-start = (bf16[256,256]{1,0:T(8,128)(2,1)S(1)}, bf16[256,256]{1,0:T(8,128)(2,1)S(1)}, u32[]{:S(2)}, u32[]{:S(2)}) collective-permute-start(bf16[256,256]{1,0:T(8,128)(2,1)S(1)} %get-tuple-element.16), channel_id=1, source_target_pairs={{0,256},{128,384},{256,0},{384,128},{1,257},{129,385},{257,1},{385... | collective-permute-start | bytes 393224 | tf_op jit(solution)/shard_map/ppermute | solution.py:17
  8.7 5.8 %collective-permute-start.2 = (bf16[256,512]{1,0:T(8,128)(2,1)S(1)}, bf16[256,512]{1,0:T(8,128)(2,1)S(1)}, u32[]{:S(2)}, u32[]{:S(2)}) collective-permute-start(bf16[256,512]{1,0:T(8,128)(2,1)S(1)} %convolution_convert_fusion.4), channel_id=1, source_target_pairs={{0,32},{32,0},{1,33},{33,1},{2,34},{34,2},{3,35},{35,3},{4,36},{36... | collective-permute-start | bytes 786440 | tf_op jit(solution)/shard_map/ppermute | solution.py:17
  14.5 1.9 %collective-permute-start.3 = (bf16[256,256]{1,0:T(8,128)(2,1)S(1)}, bf16[256,256]{1,0:T(8,128)(2,1)S(1)}, u32[]{:S(2)}, u32[]{:S(2)}) collective-permute-start(bf16[256,256]{1,0:T(8,128)(2,1)S(1)} %convolution_convert_fusion.5), channel_id=1, source_target_pairs={{0,32},{32,0},{1,33},{33,1},{2,34},{34,2},{3,35},{35,3},{4,36},{36... | collective-permute-start | bytes 393224 | tf_op jit(solution)/shard_map/ppermute | solution.py:17
  17.4 2.2 %collective-permute-start.1 = (bf16[512,256]{1,0:T(8,128)(2,1)S(1)}, bf16[512,256]{1,0:T(8,128)(2,1)S(1)}, u32[]{:S(2)}, u32[]{:S(2)}) collective-permute-start(bf16[512,256]{1,0:T(8,128)(2,1)S(1)} %convolution_convert_fusion.3), channel_id=1, source_target_pairs={{0,128},{128,0},{256,384},{384,256},{1,129},{129,1},{257,385},{385... | collective-permute-start | bytes 786440 | tf_op jit(solution)/shard_map/ppermute | solution.py:17
  19.6 1.1 convolution_convert_fusion.2
  20.7 7.1 %collective-permute-done.2 = bf16[256,512]{1,0:T(8,128)(2,1)S(1)} collective-permute-done((bf16[256,512]{1,0:T(8,128)(2,1)S(1)}, bf16[256,512]{1,0:T(8,128)(2,1)S(1)}, u32[]{:S(2)}, u32[]{:S(2)}) %collective-permute-start.2) | collective-permute-done | bytes 262176 | tf_op jit(solution)/shard_map/ppermute | solution.py:17
  28.1 2.6 %collective-permute-done.3 = bf16[256,256]{1,0:T(8,128)(2,1)S(1)} collective-permute-done((bf16[256,256]{1,0:T(8,128)(2,1)S(1)}, bf16[256,256]{1,0:T(8,128)(2,1)S(1)}, u32[]{:S(2)}, u32[]{:S(2)}) %collective-permute-start.3) | collective-permute-done | bytes 131104 | tf_op jit(solution)/shard_map/ppermute | solution.py:17
  30.6 10.0 %collective-permute-start.4 = (bf16[256,512]{1,0:T(8,128)(2,1)S(1)}, bf16[256,512]{1,0:T(8,128)(2,1)S(1)}, u32[]{:S(2)}, u32[]{:S(2)}) collective-permute-start(bf16[256,512]{1,0:T(8,128)(2,1)S(1)} %fusion.6), channel_id=1, source_target_pairs={{0,64},{64,0},{1,65},{65,1},{2,66},{66,2},{3,67},{67,3},{4,68},{68... | collective-permute-start | bytes 786440 | tf_op jit(solution)/shard_map/ppermute | solution.py:17
  40.8 3.6 %all-gather.3 = bf16[1024,256]{1,0:T(8,128)(2,1)S(1)} all-gather(bf16[512,256]{1,0:T(8,128)(2,1)S(1)} %pad_maximum_fusion.6), channel_id=5, replica_groups=mesh['x'=4,'zb'=2,'za'=2,'zl'=2,'y'=8,'c'=2] {'c'}, dimensions={0}, use_global_device_ids=true | all-gather | bytes 786432 | tf_op jit(solution)/shard_map/all_gather | solution.py:121
  44.3 2.2 %all-gather = bf16[1024,256]{1,0:T(8,128)(2,1)S(1)} all-gather(bf16[512,256]{1,0:T(8,128)(2,1)S(1)} %pad_maximum_fusion.3), channel_id=2, replica_groups=mesh['x'=4,'zb'=2,'za'=2,'zl'=2,'y'=8,'c'=2] {'c'}, dimensions={0}, use_global_device_ids=true | all-gather | bytes 786432 | tf_op jit(solution)/shard_map/all_gather | solution.py:121
  46.5 2.2 %collective-permute-done.4 = bf16[256,512]{1,0:T(8,128)(2,1)S(1)} collective-permute-done((bf16[256,512]{1,0:T(8,128)(2,1)S(1)}, bf16[256,512]{1,0:T(8,128)(2,1)S(1)}, u32[]{:S(2)}, u32[]{:S(2)}) %collective-permute-start.4) | collective-permute-done | bytes 262176 | tf_op jit(solution)/shard_map/ppermute | solution.py:17
  49.1 6.7 %all-gather.1 = bf16[512,512]{1,0:T(8,128)(2,1)S(1)} all-gather(bf16[256,512]{1,0:T(8,128)(2,1)S(1)} %fusion.7), channel_id=3, replica_groups=mesh['x'=4,'zb'=2,'za'=2,'zl'=2,'y'=8,'c'=2] {'c'}, dimensions={0}, use_global_device_ids=true | all-gather | bytes 786432 | tf_op jit(solution)/shard_map/all_gather | solution.py:123
  56.5 0.8 pad_maximum_fusion
  57.3 8.4 %all-to-all-start = ((bf16[64,16,256]{2,1,0:T(8,128)(2,1)}), bf16[64,16,256]{2,1,0:T(8,128)(2,1)S(1)}, u32[]{:S(2)}, u32[]{:S(2)}) async-start(bf16[64,16,256]{2,1,0:T(8,128)(2,1)} %bitcast.98), calls=%async_computation | async-start | bytes 1048576 | tf_op jit(solution)/shard_map/all_to_all | solution.py:40
  65.7 1.1 convolution_convert_fusion.7
  66.8 1.1 convolution_convert_fusion.6
  68.7 4.9 %collective-permute-start.5 = (bf16[256,512]{0,1:T(8,128)(2,1)}, bf16[256,512]{0,1:T(8,128)(2,1)}, u32[]{:S(2)}, u32[]{:S(2)}) collective-permute-start(bf16[256,512]{0,1:T(8,128)(2,1)} %pad_maximum_fusion.4), channel_id=1, source_target_pairs={{0,64},{64,0},{1,65},{65,1},{2,66},{66,2},{3,67},{67,3},{4,68},{68... | collective-permute-start | bytes 786440 | tf_op jit(solution)/shard_map/ppermute | solution.py:17
  73.6 8.3 %all-to-all-done = bf16[64,16,256]{2,1,0:T(8,128)(2,1)S(1)} async-done(((bf16[64,16,256]{2,1,0:T(8,128)(2,1)}), bf16[64,16,256]{2,1,0:T(8,128)(2,1)S(1)}, u32[]{:S(2)}, u32[]{:S(2)}) %all-to-all-start) | async-done | bytes 524320 | tf_op jit(solution)/shard_map/all_to_all | solution.py:40
  82.0 0.8 broadcast_in_dim.9
  82.8 10.0 %all-to-all-start.1 = ((bf16[64,16,256]{2,1,0:T(8,128)(2,1)}), bf16[64,16,256]{2,1,0:T(8,128)(2,1)S(1)}, u32[]{:S(2)}, u32[]{:S(2)}) async-start(bf16[64,16,256]{2,1,0:T(8,128)(2,1)} %broadcast_in_dim.9), calls=%async_computation.1 | async-start | bytes 1048576 | tf_op jit(solution)/shard_map/all_to_all | solution.py:46
  92.9 1.2 convolution_convert_fusion
  94.0 1.3 convolution_convert_fusion.1
  95.5 4.2 %all-gather.2 = bf16[512,512]{1,0:T(8,128)(2,1)} all-gather(bf16[256,512]{1,0:T(8,128)(2,1)S(1)} %pad_maximum_fusion.5), channel_id=4, replica_groups=mesh['x'=4,'zb'=2,'za'=2,'zl'=2,'y'=8,'c'=2] {'c'}, dimensions={0}, use_global_device_ids=true | all-gather | bytes 786432 | tf_op jit(solution)/shard_map/all_gather | solution.py:132
  99.6 2.3 %all-gather.4 = bf16[512,512]{1,0:T(8,128)(2,1)} all-gather(bf16[256,512]{1,0:T(8,128)(2,1)S(1)} %pad_maximum_fusion.7), channel_id=6, replica_groups=mesh['x'=4,'zb'=2,'za'=2,'zl'=2,'y'=8,'c'=2] {'c'}, dimensions={0}, use_global_device_ids=true | all-gather | bytes 786432 | tf_op jit(solution)/shard_map/all_gather | solution.py:132
  101.9 6.5 %all-to-all-done.1 = bf16[64,16,256]{2,1,0:T(8,128)(2,1)S(1)} async-done(((bf16[64,16,256]{2,1,0:T(8,128)(2,1)}), bf16[64,16,256]{2,1,0:T(8,128)(2,1)S(1)}, u32[]{:S(2)}, u32[]{:S(2)}) %all-to-all-start.1) | async-done | bytes 524320 | tf_op jit(solution)/shard_map/all_to_all | solution.py:46
  108.5 1.4 fusion.39
  110.8 21.4 %all_to_all.20 = bf16[64,16,256]{2,1,0:T(8,128)(2,1)S(1)} all-to-all(bf16[64,16,256]{2,1,0:T(8,128)(2,1)S(1)} %bitcast.100), channel_id=1, replica_groups=mesh['x'=4,'zb'=2,'za'=2,'zl'=2,'y'=8,'c'=2] {'x','zl','y'}, dimensions={0} | all-to-all | bytes 1048576 | tf_op jit(solution)/shard_map/all_to_all | solution.py:40
  132.3 12.6 %all_to_all.21 = bf16[16,16,256]{2,1,0:T(8,128)(2,1)S(1)} all-to-all(bf16[16,16,256]{2,1,0:T(8,128)(2,1)S(1)} %broadcast_in_dim.10), channel_id=1, replica_groups=mesh['x'=4,'zb'=2,'za'=2,'zl'=2,'y'=8,'c'=2] {'zl','y'}, dimensions={0} | all-to-all | bytes 262144 | tf_op jit(solution)/shard_map/all_to_all | solution.py:46
  144.9 6.7 %all_gather.43.total_hbm = bf16[2,256,256]{2,1,0:T(8,128)(2,1)S(1)} all-gather(bf16[1,256,256]{2,1,0:T(8,128)(2,1)S(1)} %bitcast.104), channel_id=1, replica_groups=mesh['x'=4,'zb'=2,'za'=2,'zl'=2,'y'=8,'c'=2] {'c'}, dimensions={0}, use_global_device_ids=true | all-gather | bytes 393216 | tf_op jit(solution)/shard_map/all_gather | solution.py:138
  151.6 2.6 %shard_map.46 = f32[1024,512]{1,0:T(8,128)} custom-call(bf16[1024,512]{1,0:T(8,128)(2,1)S(1)} %bitcast.88, bf16[1024,256]{1,0:T(8,128)(2,1)S(1)} %bitcast.90, bf16[2,256,256]{2,1,0:T(8,128)(2,1)S(1)} %all_gather.43.total_hbm), custom_call_target="tpu_custom_call" | custom-call | tf_op jit(solution)/shard_map/pallas_call | solution.py:81
  (38 shorter events, 4.6 us)
Async XLA Ops:
  0.0 1.0 copy-start
  0.0 2.9 %copy-start.2 = (bf16[1,1024,256]{2,1,0:T(8,128)(2,1)S(1)}, bf16[1,1024,256]{2,1,0:T(8,128)(2,1)}, u32[]{:S(2)}) copy-start(bf16[1,1024,256]{2,1,0:T(8,128)(2,1)} %param.6) | copy-start | bytes 1572868
  1.0 1.8 %copy-start.4 = (bf16[4,1,1,2,256,256]{5,4,3,2,1,0:T(8,128)(2,1)S(1)}, bf16[4,1,1,2,256,256]{5,4,3,2,1,0:T(8,128)(2,1)}, u32[]{:S(2)}) copy-start(bf16[4,1,1,2,256,256]{5,4,3,2,1,0:T(8,128)(2,1)} %param.7) | copy-start | bytes 3145732
  3.2 13.5 %collective-permute-start = (bf16[256,256]{1,0:T(8,128)(2,1)S(1)}, bf16[256,256]{1,0:T(8,128)(2,1)S(1)}, u32[]{:S(2)}, u32[]{:S(2)}) collective-permute-start(bf16[256,256]{1,0:T(8,128)(2,1)S(1)} %get-tuple-element.16), channel_id=1, source_target_pairs={{0,256},{128,384},{256,0},{384,128},{1,257},{129,385},{257,1},{385... | collective-permute-start | bytes 393224 | tf_op jit(solution)/shard_map/ppermute | solution.py:17
  8.7 19.1 %collective-permute-start.2 = (bf16[256,512]{1,0:T(8,128)(2,1)S(1)}, bf16[256,512]{1,0:T(8,128)(2,1)S(1)}, u32[]{:S(2)}, u32[]{:S(2)}) collective-permute-start(bf16[256,512]{1,0:T(8,128)(2,1)S(1)} %convolution_convert_fusion.4), channel_id=1, source_target_pairs={{0,32},{32,0},{1,33},{33,1},{2,34},{34,2},{3,35},{35,3},{4,36},{36... | collective-permute-start | bytes 786440 | tf_op jit(solution)/shard_map/ppermute | solution.py:17
  14.5 16.1 %collective-permute-start.3 = (bf16[256,256]{1,0:T(8,128)(2,1)S(1)}, bf16[256,256]{1,0:T(8,128)(2,1)S(1)}, u32[]{:S(2)}, u32[]{:S(2)}) collective-permute-start(bf16[256,256]{1,0:T(8,128)(2,1)S(1)} %convolution_convert_fusion.5), channel_id=1, source_target_pairs={{0,32},{32,0},{1,33},{33,1},{2,34},{34,2},{3,35},{35,3},{4,36},{36... | collective-permute-start | bytes 393224 | tf_op jit(solution)/shard_map/ppermute | solution.py:17
  16.7 0.7 copy-start.5
  17.4 23.3 %collective-permute-start.1 = (bf16[512,256]{1,0:T(8,128)(2,1)S(1)}, bf16[512,256]{1,0:T(8,128)(2,1)S(1)}, u32[]{:S(2)}, u32[]{:S(2)}) collective-permute-start(bf16[512,256]{1,0:T(8,128)(2,1)S(1)} %convolution_convert_fusion.3), channel_id=1, source_target_pairs={{0,128},{128,0},{256,384},{384,256},{1,129},{129,1},{257,385},{385... | collective-permute-start | bytes 786440 | tf_op jit(solution)/shard_map/ppermute | solution.py:17
  30.6 18.0 %collective-permute-start.4 = (bf16[256,512]{1,0:T(8,128)(2,1)S(1)}, bf16[256,512]{1,0:T(8,128)(2,1)S(1)}, u32[]{:S(2)}, u32[]{:S(2)}) collective-permute-start(bf16[256,512]{1,0:T(8,128)(2,1)S(1)} %fusion.6), channel_id=1, source_target_pairs={{0,64},{64,0},{1,65},{65,1},{2,66},{66,2},{3,67},{67,3},{4,68},{68... | collective-permute-start | bytes 786440 | tf_op jit(solution)/shard_map/ppermute | solution.py:17
  57.3 24.6 %all-to-all-start = ((bf16[64,16,256]{2,1,0:T(8,128)(2,1)}), bf16[64,16,256]{2,1,0:T(8,128)(2,1)S(1)}, u32[]{:S(2)}, u32[]{:S(2)}) async-start(bf16[64,16,256]{2,1,0:T(8,128)(2,1)} %bitcast.98), calls=%async_computation | async-start | bytes 1048576 | tf_op jit(solution)/shard_map/all_to_all | solution.py:40
  68.7 25.3 %collective-permute-start.5 = (bf16[256,512]{0,1:T(8,128)(2,1)}, bf16[256,512]{0,1:T(8,128)(2,1)}, u32[]{:S(2)}, u32[]{:S(2)}) collective-permute-start(bf16[256,512]{0,1:T(8,128)(2,1)} %pad_maximum_fusion.4), channel_id=1, source_target_pairs={{0,64},{64,0},{1,65},{65,1},{2,66},{66,2},{3,67},{67,3},{4,68},{68... | collective-permute-start | bytes 786440 | tf_op jit(solution)/shard_map/ppermute | solution.py:17
  82.8 25.6 %all-to-all-start.1 = ((bf16[64,16,256]{2,1,0:T(8,128)(2,1)}), bf16[64,16,256]{2,1,0:T(8,128)(2,1)S(1)}, u32[]{:S(2)}, u32[]{:S(2)}) async-start(bf16[64,16,256]{2,1,0:T(8,128)(2,1)} %broadcast_in_dim.9), calls=%async_computation.1 | async-start | bytes 1048576 | tf_op jit(solution)/shard_map/all_to_all | solution.py:46
  108.4 1.4 copy-start.3
  110.5 41.1 %copy-start.1 = (bf16[1,1024,512]{2,1,0:T(8,128)(2,1)S(1)}, bf16[1,1024,512]{2,1,0:T(8,128)(2,1)}, u32[]{:S(2)}) copy-start(bf16[1,1024,512]{2,1,0:T(8,128)(2,1)} %param.4) | copy-start | bytes 3145732

commit v4 on v3

--- a/solution.py
+++ b/solution.py
@@ -7,7 +7,8 @@
 
 BF = jnp.bfloat16
 F32 = jnp.float32
-LINE = ("zl", "y")
+LINE = ("y", "zl")
+GROUP = LINE + ("x",)
 QUAD = ("zb", "za")
 CHUNKS = 4
 
@@ -34,10 +35,9 @@
 
 
 def add_up(tail, coefficient):
-    spread = jnp.concatenate([mm("cij,cjr->ir", t, coefficient).astype(BF) for t in tail], 0)
-    group = ("x",) + LINE
-    pieces = spread.reshape(lax.axis_size(group), -1, coefficient.shape[2])
-    pieces = lax.all_to_all(pieces, group, 0, 0, tiled=True)
+    spread = mm("cij,cjr->ir", tail, coefficient).astype(BF)
+    pieces = spread.reshape(lax.axis_size(GROUP), -1, coefficient.shape[2])
+    pieces = lax.all_to_all(pieces, GROUP, 0, 0, tiled=True)
     return jnp.sum(pieces.astype(F32), axis=0).astype(BF)
 
 
@@ -101,39 +101,44 @@
     core = lax.axis_index("c")
 
     start = mm("lk,lr->kr", basis, rhs).astype(BF)
-    start, transfer, basis, out_late = lax.optimization_barrier((start, transfer, basis, out_basis))
+    start, transfer = lax.optimization_barrier((start, transfer))
     own = transfer[:, 0, 0, 0]
     other = transfer[:, 0, 0, 1]
-    gram = mm("li,lj->ij", basis, out_late).astype(BF)
-    gram, far = lax.optimization_barrier((gram, other[3]))
+
+    kept_part = dot(own[0], start)
+    kept_part, far = lax.optimization_barrier((kept_part, other[3]))
     far = swap(far, "x", 2)
-
-    field = (dot(own[0], start) + dot(other[0], swap(start, "za", 1))).astype(BF)
-    near = swap(gram, "za", 1)
-    field, near = lax.optimization_barrier((field, near))
-    chain = jnp.concatenate([dot(own[0], gram).astype(BF), dot(other[0], near).astype(BF)], 1)
+    field = (kept_part + dot(other[0], swap(start, "za", 1))).astype(BF)
     field = (dot(own[1], field) + dot(other[1], swap(field, "zb", 1))).astype(BF)
 
     wide = jnp.concatenate([own[3], far], 0)
     kept = dot(wide, own[2]).astype(BF)
     came = swap(dot(wide, other[2]).astype(BF), "x", 1)
     tail = in_order([kept[:rank], came[:rank], kept[rank:], came[rank:]], "x")
-    tail = [lax.all_gather(jnp.concatenate(tail[i : i + 2], 0), "c") for i in (0, 2)]
+    tail = jnp.stack([t.reshape(lax.axis_size(LINE), -1, rank) for t in tail], 1).reshape(4 * rank, rank)
+    tail = [lax.all_gather(tail[i : i + 2 * rank], "c") for i in (0, 2 * rank)]
+    tail = jnp.concatenate(tail, 1)
+
+    tail, basis = lax.optimization_barrier((tail, basis))
+    gram = mm("li,lj->ij", basis, out_basis).astype(BF)
+    near = swap(gram, "za", 1)
 
     field = lax.all_gather(field, "c")
+    field, near = lax.optimization_barrier((field, near))
+    chain = jnp.concatenate([dot(own[0], gram).astype(BF), dot(other[0], near).astype(BF)], 1)
     field = lax.dynamic_slice_in_dim(field, core * half, half, 2)
     share = add_up(tail, field)
-    totals = hand_out(share, QUAD + LINE).reshape(2, 2 * rank, half)
+    totals = hand_out(share, QUAD + LINE).reshape(4 * rank, half)
 
     chain_far = swap(chain, "zb", 1)
     mine = dot(own[1], chain).astype(BF)
     theirs = dot(other[1], chain_far).astype(BF)
     back = in_order([mine[:, :rank], mine[:, rank:], theirs[:, :rank], theirs[:, rank:]], QUAD)
     back = [lax.all_gather(jnp.concatenate(back[i : i + 2], 1), "c") for i in (0, 2)]
+    back = jnp.concatenate(back, 2)
 
-    change = mm("cij,jr->cir", back[0], totals[0]) + mm("cij,jr->cir", back[1], totals[1])
-    field = (field.astype(F32) - change).astype(BF)
-    share = add_up(tail, field)
+    field = (field.astype(F32) - mm("cij,jr->cir", back, totals)).astype(BF)
+    share = add_up(tail, lax.optimization_barrier(field))
     total = hand_out(share, LINE).reshape(rank, half)
     return finish(rhs, out_basis, lax.all_gather(total, "c"))[None]
 

time: 155 us -> 153 us (0.987)
  blocking collectives: 59.5 us -> 61.5 us
    all_to_all x1, blocking collectives: 21.4 us -> 23.2 us  [add_up(): pieces = lax.all_to_all(pieces, GROUP, 0, 0, tiled=True)]
    dot_general x8 -> x5, matrix products: 4.99 us -> 5.48 us  [mm(): return jnp.einsum(spec, a, b, preferred_element_type=F32)]
  transfers between devices with their start and end apart: 8 -> 8, of which waited for: 5 -> 4; matrix products, arithmetic and copies ran while one was open for 5% -> 5% of each run, Pallas kernels for 0% -> 0%
where the time goes in v4:
time: 153 us
  blocking collectives  61.5 us (40%)
  starting transfers between devices  47.2 us (31%)
  waiting for transfers between devices  26.2 us (17%)
  matrix products  11.5 us (8%)
  Pallas kernels  2.61 us (2%)
  local copies, waits for them, and re-layouts  1.99 us (1%)
    ppermute x6, starting transfers between devices, swap(): return lax.ppermute(block, axis, [(i, i ^ bit) for i in range(size)])  30.2 us
    all_to_all x1, blocking collectives, add_up(): pieces = lax.all_to_all(pieces, GROUP, 0, 0, tiled=True)  23.2 us
    all_to_all x1, blocking collectives, hand_out(): return lax.all_to_all(copies, axes, 0, 0, tiled=True)  13.6 us
    ppermute x6, waiting for transfers between devices, swap(): return lax.ppermute(block, axis, [(i, i ^ bit) for i in range(size)])  11 us
    all_to_all x1, starting transfers between devices, hand_out(): return lax.all_to_all(copies, axes, 0, 0, tiled=True)  8.6 us
    all_to_all x1, starting transfers between devices, add_up(): pieces = lax.all_to_all(pieces, GROUP, 0, 0, tiled=True)  8.41 us
    all_to_all x1, waiting for transfers between devices, add_up(): pieces = lax.all_to_all(pieces, GROUP, 0, 0, tiled=True)  8.08 us
    all_to_all x1, waiting for transfers between devices, hand_out(): return lax.all_to_all(copies, axes, 0, 0, tiled=True)  7.07 us
  transfers between devices with their start and end apart: 8, of which 4 were waited for; matrix products, arithmetic and copies ran while one was open for 5% of the time, Pallas kernels for 0%

profile of v4, /device:TPU:1, one launch (start us, length us, event | category | flops | bytes accessed | tf_op | source)
XLA Modules:
  0.0 152.5 jit_solution(1253428480337032214)
XLA Ops:
  0.0 1.0 copy-done
  1.0 1.7 %convolution_convert_fusion.4 = bf16[256,512]{1,0:T(8,128)(2,1)S(1)} fusion(bf16[1,1024,256]{2,1,0:T(8,128)(2,1)S(1)} %copy-done, bf16[1,1024,512]{2,1,0:T(8,128)(2,1)} %param.4), kind=kOutput, calls=%fused_computation.10 | convolution fusion | flops 268566528 | bytes 1835008 | tf_op jit(solution)/shard_map/lk,lr->kr/dot_general | solution.py:22
  3.0 5.5 %collective-permute-start = (bf16[256,256]{1,0:T(8,128)(2,1)S(1)}, bf16[256,256]{1,0:T(8,128)(2,1)S(1)}, u32[]{:S(2)}, u32[]{:S(2)}) collective-permute-start(bf16[256,256]{1,0:T(8,128)(2,1)S(1)} %get-tuple-element.15), channel_id=1, source_target_pairs={{0,256},{128,384},{256,0},{384,128},{1,257},{129,385},{257,1},{385... | collective-permute-start | bytes 393224 | tf_op jit(solution)/shard_map/ppermute | solution.py:18
  8.5 5.8 %collective-permute-start.2 = (bf16[256,512]{1,0:T(8,128)(2,1)S(1)}, bf16[256,512]{1,0:T(8,128)(2,1)S(1)}, u32[]{:S(2)}, u32[]{:S(2)}) collective-permute-start(bf16[256,512]{1,0:T(8,128)(2,1)S(1)} %convolution_convert_fusion.4), channel_id=1, source_target_pairs={{0,32},{32,0},{1,33},{33,1},{2,34},{34,2},{3,35},{35,3},{4,36},{36... | collective-permute-start | bytes 786440 | tf_op jit(solution)/shard_map/ppermute | solution.py:18
  14.6 2.2 %collective-permute-start.1 = (bf16[512,256]{1,0:T(8,128)(2,1)S(1)}, bf16[512,256]{1,0:T(8,128)(2,1)S(1)}, u32[]{:S(2)}, u32[]{:S(2)}) collective-permute-start(bf16[512,256]{1,0:T(8,128)(2,1)S(1)} %convolution_convert_fusion.3), channel_id=1, source_target_pairs={{0,128},{128,0},{256,384},{384,256},{1,129},{129,1},{257,385},{385... | collective-permute-start | bytes 786440 | tf_op jit(solution)/shard_map/ppermute | solution.py:18
  17.0 7.8 %collective-permute-done.2 = bf16[256,512]{1,0:T(8,128)(2,1)S(1)} collective-permute-done((bf16[256,512]{1,0:T(8,128)(2,1)S(1)}, bf16[256,512]{1,0:T(8,128)(2,1)S(1)}, u32[]{:S(2)}, u32[]{:S(2)}) %collective-permute-start.2) | collective-permute-done | bytes 262176 | tf_op jit(solution)/shard_map/ppermute | solution.py:18
  25.0 10.0 %collective-permute-start.3 = (bf16[256,512]{1,0:T(8,128)(2,1)S(1)}, bf16[256,512]{1,0:T(8,128)(2,1)S(1)}, u32[]{:S(2)}, u32[]{:S(2)}) collective-permute-start(bf16[256,512]{1,0:T(8,128)(2,1)S(1)} %fusion.2), channel_id=1, source_target_pairs={{0,64},{64,0},{1,65},{65,1},{2,66},{66,2},{3,67},{67,3},{4,68},{68... | collective-permute-start | bytes 786440 | tf_op jit(solution)/shard_map/ppermute | solution.py:18
  35.5 3.7 %all_gather.36 = bf16[2,512,256]{2,1,0:T(8,128)(2,1)S(1)} all-gather(bf16[1,512,256]{2,1,0:T(8,128)(2,1)S(1)} %bitcast.81), channel_id=1, replica_groups=mesh['x'=4,'zb'=2,'za'=2,'zl'=2,'y'=8,'c'=2] {'c'}, dimensions={0}, use_global_device_ids=true | all-gather | bytes 786432 | tf_op jit(solution)/shard_map/all_gather | solution.py:119
  39.2 2.2 %all_gather.34 = bf16[2,512,256]{2,1,0:T(8,128)(2,1)S(1)} all-gather(bf16[1,512,256]{2,1,0:T(8,128)(2,1)S(1)} %bitcast.82), channel_id=1, replica_groups=mesh['x'=4,'zb'=2,'za'=2,'zl'=2,'y'=8,'c'=2] {'c'}, dimensions={0}, use_global_device_ids=true | all-gather | bytes 786432 | tf_op jit(solution)/shard_map/all_gather | solution.py:119
  41.8 1.9 %collective-permute-start.4 = (bf16[256,256]{1,0:T(8,128)(2,1)S(1)}, bf16[256,256]{1,0:T(8,128)(2,1)S(1)}, u32[]{:S(2)}, u32[]{:S(2)}) collective-permute-start(bf16[256,256]{1,0:T(8,128)(2,1)S(1)} %convolution_convert_fusion.5), channel_id=1, source_target_pairs={{0,32},{32,0},{1,33},{33,1},{2,34},{34,2},{3,35},{35,3},{4,36},{36... | collective-permute-start | bytes 393224 | tf_op jit(solution)/shard_map/ppermute | solution.py:18
  44.0 7.0 %all-gather = bf16[512,512]{1,0:T(8,128)(2,1)S(1)} all-gather(bf16[256,512]{1,0:T(8,128)(2,1)S(1)} %fusion.3), channel_id=2, replica_groups=mesh['x'=4,'zb'=2,'za'=2,'zl'=2,'y'=8,'c'=2] {'c'}, dimensions={0}, use_global_device_ids=true | all-gather | bytes 786432 | tf_op jit(solution)/shard_map/all_gather | solution.py:126
  51.0 3.2 %collective-permute-done.4 = bf16[256,256]{1,0:T(8,128)(2,1)S(1)} collective-permute-done((bf16[256,256]{1,0:T(8,128)(2,1)S(1)}, bf16[256,256]{1,0:T(8,128)(2,1)S(1)}, u32[]{:S(2)}, u32[]{:S(2)}) %collective-permute-start.4) | collective-permute-done | bytes 131104 | tf_op jit(solution)/shard_map/ppermute | solution.py:18
  54.2 1.2 fusion
  55.4 8.4 %all-to-all-start = ((bf16[64,16,256]{2,1,0:T(8,128)(2,1)}), bf16[64,16,256]{2,1,0:T(8,128)(2,1)S(1)}, u32[]{:S(2)}, u32[]{:S(2)}) async-start(bf16[64,16,256]{2,1,0:T(8,128)(2,1)} %bitcast.21), calls=%async_computation | async-start | bytes 1048576 | tf_op jit(solution)/shard_map/all_to_all | solution.py:40
  63.8 1.1 convolution_convert_fusion.7
  65.0 1.1 convolution_convert_fusion.6
  66.1 0.7 pad_maximum_fusion.3
  66.8 4.8 %collective-permute-start.5 = (bf16[256,512]{0,1:T(8,128)(2,1)}, bf16[256,512]{0,1:T(8,128)(2,1)}, u32[]{:S(2)}, u32[]{:S(2)}) collective-permute-start(bf16[256,512]{0,1:T(8,128)(2,1)} %pad_maximum_fusion.3), channel_id=1, source_target_pairs={{0,64},{64,0},{1,65},{65,1},{2,66},{66,2},{3,67},{67,3},{4,68},{68... | collective-permute-start | bytes 786440 | tf_op jit(solution)/shard_map/ppermute | solution.py:18
  71.6 8.1 %all-to-all-done = bf16[64,16,256]{2,1,0:T(8,128)(2,1)S(1)} async-done(((bf16[64,16,256]{2,1,0:T(8,128)(2,1)}), bf16[64,16,256]{2,1,0:T(8,128)(2,1)S(1)}, u32[]{:S(2)}, u32[]{:S(2)}) %all-to-all-start) | async-done | bytes 524320 | tf_op jit(solution)/shard_map/all_to_all | solution.py:40
  79.8 0.8 broadcast_in_dim.9
  80.6 8.6 %all-to-all-start.1 = ((bf16[64,16,256]{2,1,0:T(8,128)(2,1)}), bf16[64,16,256]{2,1,0:T(8,128)(2,1)}, u32[]{:S(2)}, u32[]{:S(2)}) async-start(bf16[64,16,256]{2,1,0:T(8,128)(2,1)} %broadcast_in_dim.9), calls=%async_computation.1 | async-start | bytes 1048576 | tf_op jit(solution)/shard_map/all_to_all | solution.py:46
  89.2 1.2 convolution_convert_fusion
  90.4 1.3 convolution_convert_fusion.1
  91.8 3.9 %all-gather.2 = bf16[512,512]{1,0:T(8,128)(2,1)} all-gather(bf16[256,512]{1,0:T(8,128)(2,1)S(1)} %pad_maximum_fusion.5), channel_id=4, replica_groups=mesh['x'=4,'zb'=2,'za'=2,'zl'=2,'y'=8,'c'=2] {'c'}, dimensions={0}, use_global_device_ids=true | all-gather | bytes 786432 | tf_op jit(solution)/shard_map/all_gather | solution.py:137
  95.7 2.3 %all-gather.1 = bf16[512,512]{1,0:T(8,128)(2,1)} all-gather(bf16[256,512]{1,0:T(8,128)(2,1)S(1)} %pad_maximum_fusion.4), channel_id=3, replica_groups=mesh['x'=4,'zb'=2,'za'=2,'zl'=2,'y'=8,'c'=2] {'c'}, dimensions={0}, use_global_device_ids=true | all-gather | bytes 786432 | tf_op jit(solution)/shard_map/all_gather | solution.py:137
  98.0 7.1 %all-to-all-done.1 = bf16[64,16,256]{2,1,0:T(8,128)(2,1)} async-done(((bf16[64,16,256]{2,1,0:T(8,128)(2,1)}), bf16[64,16,256]{2,1,0:T(8,128)(2,1)}, u32[]{:S(2)}, u32[]{:S(2)}) %all-to-all-start.1) | async-done | bytes 524320 | tf_op jit(solution)/shard_map/all_to_all | solution.py:46
  105.0 1.8 %subtract_convert_fusion = bf16[2,256,256]{2,1,0:T(8,128)(2,1)S(1)} fusion(bf16[2,256,512]{2,1,0:T(8,128)(2,1)S(1)} %bitcast.80, s32[]{:T(128)S(6)} %select_n.87, bf16[1024,256,1]{1,0,2:T(8,128)(2,1)} %bitcast.23, bf16[2,256,512]{2,1,0:T(8,128)(2,1)} %bitcast.84, bf16[2,256,512]{2,1,0:T(8,128)(2,1)} %bitcast.85), kind=kOutput, calls=%fused_computation.22 | convolution fusion | flops 270925824 | bytes 2097156 | tf_op jit(solution)/shard_map/cij,jr->cir/dot_general | solution.py:22
  106.9 0.4 fusion.1
  107.3 23.2 %all_to_all.20 = bf16[64,16,256]{2,1,0:T(8,128)(2,1)S(1)} all-to-all(bf16[64,16,256]{2,1,0:T(8,128)(2,1)S(1)} %bitcast.78), channel_id=1, replica_groups=mesh['x'=4,'zb'=2,'za'=2,'zl'=2,'y'=8,'c'=2] {'y','zl','x'}, dimensions={0} | all-to-all | bytes 1048576 | tf_op jit(solution)/shard_map/all_to_all | solution.py:40
  130.6 13.6 %all_to_all.21 = bf16[16,16,256]{2,1,0:T(8,128)(2,1)S(1)} all-to-all(bf16[16,16,256]{2,1,0:T(8,128)(2,1)S(1)} %broadcast_in_dim.10), channel_id=1, replica_groups=mesh['x'=4,'zb'=2,'za'=2,'zl'=2,'y'=8,'c'=2] {'y','zl'}, dimensions={0} | all-to-all | bytes 262144 | tf_op jit(solution)/shard_map/all_to_all | solution.py:46
  144.2 5.7 %all_gather.43.total_hbm = bf16[2,256,256]{2,1,0:T(8,128)(2,1)S(1)} all-gather(bf16[1,256,256]{2,1,0:T(8,128)(2,1)S(1)} %bitcast.83), channel_id=1, replica_groups=mesh['x'=4,'zb'=2,'za'=2,'zl'=2,'y'=8,'c'=2] {'c'}, dimensions={0}, use_global_device_ids=true | all-gather | bytes 393216 | tf_op jit(solution)/shard_map/all_gather | solution.py:143
  149.9 2.6 %shard_map.46 = f32[1024,512]{1,0:T(8,128)} custom-call(bf16[1024,512]{1,0:T(8,128)(2,1)S(1)} %bitcast.76, bf16[1024,256]{1,0:T(8,128)(2,1)S(1)} %bitcast.77, bf16[2,256,256]{2,1,0:T(8,128)(2,1)S(1)} %all_gather.43.total_hbm), custom_call_target="tpu_custom_call" | custom-call | tf_op jit(solution)/shard_map/pallas_call | solution.py:81
  (31 shorter events, 2.3 us)
Async XLA Ops:
  0.0 1.0 copy-start
  0.0 2.7 %copy-start.3 = (bf16[4,1,1,2,256,256]{5,4,3,2,1,0:T(8,128)(2,1)S(1)}, bf16[4,1,1,2,256,256]{5,4,3,2,1,0:T(8,128)(2,1)}, u32[]{:S(2)}) copy-start(bf16[4,1,1,2,256,256]{5,4,3,2,1,0:T(8,128)(2,1)} %param.7) | copy-start | bytes 3145732
  3.0 11.3 %collective-permute-start = (bf16[256,256]{1,0:T(8,128)(2,1)S(1)}, bf16[256,256]{1,0:T(8,128)(2,1)S(1)}, u32[]{:S(2)}, u32[]{:S(2)}) collective-permute-start(bf16[256,256]{1,0:T(8,128)(2,1)S(1)} %get-tuple-element.15), channel_id=1, source_target_pairs={{0,256},{128,384},{256,0},{384,128},{1,257},{129,385},{257,1},{385... | collective-permute-start | bytes 393224 | tf_op jit(solution)/shard_map/ppermute | solution.py:18
  8.5 16.3 %collective-permute-start.2 = (bf16[256,512]{1,0:T(8,128)(2,1)S(1)}, bf16[256,512]{1,0:T(8,128)(2,1)S(1)}, u32[]{:S(2)}, u32[]{:S(2)}) collective-permute-start(bf16[256,512]{1,0:T(8,128)(2,1)S(1)} %convolution_convert_fusion.4), channel_id=1, source_target_pairs={{0,32},{32,0},{1,33},{33,1},{2,34},{34,2},{3,35},{35,3},{4,36},{36... | collective-permute-start | bytes 786440 | tf_op jit(solution)/shard_map/ppermute | solution.py:18
  14.6 20.7 %collective-permute-start.1 = (bf16[512,256]{1,0:T(8,128)(2,1)S(1)}, bf16[512,256]{1,0:T(8,128)(2,1)S(1)}, u32[]{:S(2)}, u32[]{:S(2)}) collective-permute-start(bf16[512,256]{1,0:T(8,128)(2,1)S(1)} %convolution_convert_fusion.3), channel_id=1, source_target_pairs={{0,128},{128,0},{256,384},{384,256},{1,129},{129,1},{257,385},{385... | collective-permute-start | bytes 786440 | tf_op jit(solution)/shard_map/ppermute | solution.py:18
  25.0 18.7 %collective-permute-start.3 = (bf16[256,512]{1,0:T(8,128)(2,1)S(1)}, bf16[256,512]{1,0:T(8,128)(2,1)S(1)}, u32[]{:S(2)}, u32[]{:S(2)}) collective-permute-start(bf16[256,512]{1,0:T(8,128)(2,1)S(1)} %fusion.2), channel_id=1, source_target_pairs={{0,64},{64,0},{1,65},{65,1},{2,66},{66,2},{3,67},{67,3},{4,68},{68... | collective-permute-start | bytes 786440 | tf_op jit(solution)/shard_map/ppermute | solution.py:18
  35.5 6.0 %copy-start.2 = (bf16[1,1024,256]{2,1,0:T(8,128)(2,1)S(1)}, bf16[1,1024,256]{2,1,0:T(8,128)(2,1)}, u32[]{:S(2)}) copy-start(bf16[1,1024,256]{2,1,0:T(8,128)(2,1)} %param.6) | copy-start | bytes 1572868
  41.8 12.4 %collective-permute-start.4 = (bf16[256,256]{1,0:T(8,128)(2,1)S(1)}, bf16[256,256]{1,0:T(8,128)(2,1)S(1)}, u32[]{:S(2)}, u32[]{:S(2)}) collective-permute-start(bf16[256,256]{1,0:T(8,128)(2,1)S(1)} %convolution_convert_fusion.5), channel_id=1, source_target_pairs={{0,32},{32,0},{1,33},{33,1},{2,34},{34,2},{3,35},{35,3},{4,36},{36... | collective-permute-start | bytes 393224 | tf_op jit(solution)/shard_map/ppermute | solution.py:18
  55.4 24.3 %all-to-all-start = ((bf16[64,16,256]{2,1,0:T(8,128)(2,1)}), bf16[64,16,256]{2,1,0:T(8,128)(2,1)S(1)}, u32[]{:S(2)}, u32[]{:S(2)}) async-start(bf16[64,16,256]{2,1,0:T(8,128)(2,1)} %bitcast.21), calls=%async_computation | async-start | bytes 1048576 | tf_op jit(solution)/shard_map/all_to_all | solution.py:40
  66.8 23.6 %collective-permute-start.5 = (bf16[256,512]{0,1:T(8,128)(2,1)}, bf16[256,512]{0,1:T(8,128)(2,1)}, u32[]{:S(2)}, u32[]{:S(2)}) collective-permute-start(bf16[256,512]{0,1:T(8,128)(2,1)} %pad_maximum_fusion.3), channel_id=1, source_target_pairs={{0,64},{64,0},{1,65},{65,1},{2,66},{66,2},{3,67},{67,3},{4,68},{68... | collective-permute-start | bytes 786440 | tf_op jit(solution)/shard_map/ppermute | solution.py:18
  80.6 24.4 %all-to-all-start.1 = ((bf16[64,16,256]{2,1,0:T(8,128)(2,1)}), bf16[64,16,256]{2,1,0:T(8,128)(2,1)}, u32[]{:S(2)}, u32[]{:S(2)}) async-start(bf16[64,16,256]{2,1,0:T(8,128)(2,1)} %broadcast_in_dim.9), calls=%async_computation.1 | async-start | bytes 1048576 | tf_op jit(solution)/shard_map/all_to_all | solution.py:46
  106.9 43.1 %copy-start.1 = (bf16[1,1024,512]{2,1,0:T(8,128)(2,1)S(1)}, bf16[1,1024,512]{2,1,0:T(8,128)(2,1)}, u32[]{:S(2)}) copy-start(bf16[1,1024,512]{2,1,0:T(8,128)(2,1)} %param.4) | copy-start | bytes 3145732

commit v5 on v4

--- a/solution.py
+++ b/solution.py
@@ -3,6 +3,7 @@
 from jax import lax
 from jax.experimental import pallas as pl
 from jax.experimental.pallas import tpu as pltpu
+from jax.experimental.layout import Layout, with_layout_constraint
 from jax.sharding import Mesh, PartitionSpec as P
 
 BF = jnp.bfloat16
@@ -24,6 +25,10 @@
 
 def dot(a, b):
     return jnp.dot(a, b, preferred_element_type=F32)
+
+
+def in_rows(block):
+    return with_layout_constraint(block, Layout(major_to_minor=(0, 1)))
 
 
 def in_order(blocks, axis):
@@ -100,45 +105,58 @@
     rank = basis.shape[1]
     core = lax.axis_index("c")
 
+    tie = lax.optimization_barrier
     start = mm("lk,lr->kr", basis, rhs).astype(BF)
-    start, transfer = lax.optimization_barrier((start, transfer))
+    start, transfer, basis = tie((start, transfer, basis))
     own = transfer[:, 0, 0, 0]
     other = transfer[:, 0, 0, 1]
 
-    kept_part = dot(own[0], start)
-    kept_part, far = lax.optimization_barrier((kept_part, other[3]))
-    far = swap(far, "x", 2)
-    field = (kept_part + dot(other[0], swap(start, "za", 1))).astype(BF)
-    field = (dot(own[1], field) + dot(other[1], swap(field, "zb", 1))).astype(BF)
+    far = swap(other[3], "x", 2)
+    field = (dot(own[0], start) + dot(other[0], swap(start, "za", 1))).astype(BF)
+    field, far = tie((field, far))
 
     wide = jnp.concatenate([own[3], far], 0)
+    sent = dot(wide, other[2]).astype(BF)
+    came = swap(sent, "x", 1)
+    field = (dot(own[1], field) + dot(other[1], swap(field, "zb", 1))).astype(BF)
+    field, came, basis, wide = tie((field, came, basis, wide))
+    middle = field
+
+    gram = mm("li,lj->ij", basis, out_basis).astype(BF)
+    near = swap(gram, "za", 1)
+    field = (dot(own[2], field) + dot(other[2], swap(field, "x", 1))).astype(BF)
+    field, gram_late, near = tie((field, gram, near))
+
+    chain = [dot(own[0], gram_late).astype(BF), dot(other[0], near).astype(BF)]
+    chain_far = [swap(chain[0], "zb", 1), None]
+    field = (dot(own[3], field) + dot(other[3], swap(field, "x", 2))).astype(BF)
+    both = lax.all_gather(field, "c")
+    both = lax.dynamic_slice_in_dim(both, core * half, half, 2)
+    both = (both[0].astype(F32) + both[1].astype(F32)).astype(BF)
+    both, chain[1], middle = tie((both, chain[1], middle))
+    chain_far[1] = swap(chain[1], "zb", 1)
+    middle = lax.all_gather(middle, "c")
+    middle = lax.dynamic_slice_in_dim(middle, core * half, half, 2)
+    pieces = lax.all_to_all(both.reshape(lax.axis_size(LINE), -1, half), LINE, 0, 0, tiled=True)
+    share = jnp.sum(pieces.astype(F32), axis=0).astype(BF)
+    share, *chain_far, came, wide = tie((share, *chain_far, came, wide))
+    totals = hand_out(share, QUAD + LINE).reshape(4 * rank, half)
+
     kept = dot(wide, own[2]).astype(BF)
-    came = swap(dot(wide, other[2]).astype(BF), "x", 1)
     tail = in_order([kept[:rank], came[:rank], kept[rank:], came[rank:]], "x")
     tail = jnp.stack([t.reshape(lax.axis_size(LINE), -1, rank) for t in tail], 1).reshape(4 * rank, rank)
     tail = [lax.all_gather(tail[i : i + 2 * rank], "c") for i in (0, 2 * rank)]
     tail = jnp.concatenate(tail, 1)
 
-    tail, basis = lax.optimization_barrier((tail, basis))
-    gram = mm("li,lj->ij", basis, out_basis).astype(BF)
-    near = swap(gram, "za", 1)
-
-    field = lax.all_gather(field, "c")
-    field, near = lax.optimization_barrier((field, near))
-    chain = jnp.concatenate([dot(own[0], gram).astype(BF), dot(other[0], near).astype(BF)], 1)
-    field = lax.dynamic_slice_in_dim(field, core * half, half, 2)
-    share = add_up(tail, field)
-    totals = hand_out(share, QUAD + LINE).reshape(4 * rank, half)
-
-    chain_far = swap(chain, "zb", 1)
-    mine = dot(own[1], chain).astype(BF)
-    theirs = dot(other[1], chain_far).astype(BF)
-    back = in_order([mine[:, :rank], mine[:, rank:], theirs[:, :rank], theirs[:, rank:]], QUAD)
-    back = [lax.all_gather(jnp.concatenate(back[i : i + 2], 1), "c") for i in (0, 2)]
+    back = [dot(own[1], c).astype(BF) for c in chain] + [dot(other[1], c).astype(BF) for c in chain_far]
+    back = in_order(back, QUAD)
+    back = [in_rows(jnp.concatenate(back[i : i + 2], 1)) for i in (0, 2)]
+    back = [lax.all_gather(b, "c") for b in back]
     back = jnp.concatenate(back, 2)
 
-    field = (field.astype(F32) - mm("cij,jr->cir", back, totals)).astype(BF)
-    share = add_up(tail, lax.optimization_barrier(field))
+    middle, tail, back, totals = tie((middle, tail, back, totals))
+    field = tie((middle.astype(F32) - mm("cij,jr->cir", back, totals)).astype(BF))
+    share = add_up(tail, field)
     total = hand_out(share, LINE).reshape(rank, half)
     return finish(rhs, out_basis, lax.all_gather(total, "c"))[None]
 

time: 153 us -> 164 us (1.072)
  starting transfers between devices: 47.2 us -> 58.3 us
  blocking collectives: 61.5 us -> 64 us
  waiting for transfers between devices: 26.2 us -> 24 us
    ppermute x6 -> x9, starting transfers between devices: 30.2 us -> 45.9 us  [swap(): return lax.ppermute(block, axis, [(i, i ^ bit) for i in range(size)])]
    ppermute x6 -> x9, waiting for transfers between devices: 11 us -> 14.5 us  [swap(): return lax.ppermute(block, axis, [(i, i ^ bit) for i in range(size)])]
    all_to_all x1, waiting for transfers between devices: 7.07 us -> 3.82 us  [hand_out(): return lax.all_to_all(copies, axes, 0, 0, tiled=True)]
    all_to_all x1, starting transfers between devices: 8.6 us -> 5.5 us  [hand_out(): return lax.all_to_all(copies, axes, 0, 0, tiled=True)]
    all_to_all x1, waiting for transfers between devices: 8.08 us -> 5.7 us  [body(): lax.all_to_all(both.reshape(lax.axis_size(LINE), -1, half), LINE, 0, 0, t...]
    all_gather x3 -> x4, blocking collectives: 13.2 us -> 15.3 us  [the longest x1 8.27 us: body(): both = lax.all_gather(field, 'c')]
    dot_general x5 -> x4, matrix products: 5.48 us -> 3.93 us  [mm(): return jnp.einsum(spec, a, b, preferred_element_type=F32)]
    dot_general x10 -> x16, matrix products: 6.05 us -> 6.51 us  [dot(): return jnp.dot(a, b, preferred_element_type=F32)]
  transfers between devices with their start and end apart: 8 -> 11, of which waited for: 4 -> 6; matrix products, arithmetic and copies ran while one was open for 5% -> 4% of each run, Pallas kernels for 0% -> 0%
where the time goes in v5:
time: 164 us; the launch traced here: 163 us
  blocking collectives  64 us (39%)
  starting transfers between devices  58.3 us (36%)
  waiting for transfers between devices  24 us (15%)
  matrix products  10.4 us (6%)
  Pallas kernels  2.63 us (2%)
  local copies, waits for them, and re-layouts  2.02 us (1%)
    ppermute x9, starting transfers between devices, swap(): return lax.ppermute(block, axis, [(i, i ^ bit) for i in range(size)])  45.9 us
    all_to_all x1, blocking collectives, add_up(): pieces = lax.all_to_all(pieces, GROUP, 0, 0, tiled=True)  23 us
    ppermute x9, waiting for transfers between devices, swap(): return lax.ppermute(block, axis, [(i, i ^ bit) for i in range(size)])  14.5 us
    all_to_all x1, blocking collectives, hand_out(): return lax.all_to_all(copies, axes, 0, 0, tiled=True)  13.9 us
    all_gather x1, blocking collectives, body(): both = lax.all_gather(field, 'c')  8.27 us
    all_to_all x1, starting transfers between devices, body(): lax.all_to_all(both.reshape(lax.axis_size(LINE), -1, half), LINE, 0, 0, t...  6.9 us
    dot_general x16, matrix products, dot(): return jnp.dot(a, b, preferred_element_type=F32)  6.51 us
    all_gather x2, blocking collectives, body(): tail = [lax.all_gather(tail[i:i + 2 * rank], 'c') for i in (0, 2 * rank)]  6.07 us
  transfers between devices with their start and end apart: 11, of which 6 were waited for; matrix products, arithmetic and copies ran while one was open for 4% of the time, Pallas kernels for 0%

profile of v5, /device:TPU:1, one launch (start us, length us, event | category | flops | bytes accessed | tf_op | source)
XLA Modules:
  0.0 163.1 jit_solution(7655254679305000967)
XLA Ops:
  0.0 1.0 copy-done
  1.0 1.7 %convolution_convert_fusion.2 = bf16[256,512]{1,0:T(8,128)(2,1)S(1)} fusion(bf16[1,1024,256]{2,1,0:T(8,128)(2,1)S(1)} %copy-done, bf16[1,1024,512]{2,1,0:T(8,128)(2,1)} %param.4), kind=kOutput, calls=%fused_computation.10 | convolution fusion | flops 268566528 | bytes 1835008 | tf_op jit(solution)/shard_map/lk,lr->kr/dot_general | solution.py:23
  2.7 6.6 %collective-permute-start = (bf16[256,512]{1,0:T(8,128)(2,1)S(1)}, bf16[256,512]{1,0:T(8,128)(2,1)S(1)}, u32[]{:S(2)}, u32[]{:S(2)}) collective-permute-start(bf16[256,512]{1,0:T(8,128)(2,1)S(1)} %convolution_convert_fusion.2), channel_id=1, source_target_pairs={{0,32},{32,0},{1,33},{33,1},{2,34},{34,2},{3,35},{35,3},{4,36},{36... | collective-permute-start | bytes 786440 | tf_op jit(solution)/shard_map/ppermute | solution.py:19
  9.4 4.7 %collective-permute-start.1 = (bf16[256,256]{1,0:T(8,128)(2,1)S(1)}, bf16[256,256]{1,0:T(8,128)(2,1)S(1)}, u32[]{:S(2)}, u32[]{:S(2)}) collective-permute-start(bf16[256,256]{1,0:T(8,128)(2,1)S(1)} %get-tuple-element.54), channel_id=1, source_target_pairs={{0,256},{128,384},{256,0},{384,128},{1,257},{129,385},{257,1},{385... | collective-permute-start | bytes 393224 | tf_op jit(solution)/shard_map/ppermute | solution.py:19
  14.3 5.6 %collective-permute-done = bf16[256,512]{1,0:T(8,128)(2,1)S(1)} collective-permute-done((bf16[256,512]{1,0:T(8,128)(2,1)S(1)}, bf16[256,512]{1,0:T(8,128)(2,1)S(1)}, u32[]{:S(2)}, u32[]{:S(2)}) %collective-permute-start) | collective-permute-done | bytes 262176 | tf_op jit(solution)/shard_map/ppermute | solution.py:19
  20.1 10.0 %collective-permute-start.2 = (bf16[256,512]{1,0:T(8,128)(2,1)S(1)}, bf16[256,512]{1,0:T(8,128)(2,1)S(1)}, u32[]{:S(2)}, u32[]{:S(2)}) collective-permute-start(bf16[256,512]{1,0:T(8,128)(2,1)S(1)} %fusion.2), channel_id=1, source_target_pairs={{0,64},{64,0},{1,65},{65,1},{2,66},{66,2},{3,67},{67,3},{4,68},{68... | collective-permute-start | bytes 786440 | tf_op jit(solution)/shard_map/ppermute | solution.py:19
  30.4 3.1 %collective-permute-start.3 = (bf16[512,256]{1,0:T(8,128)(2,1)S(1)}, bf16[512,256]{1,0:T(8,128)(2,1)S(1)}, u32[]{:S(2)}, u32[]{:S(2)}) collective-permute-start(bf16[512,256]{1,0:T(8,128)(2,1)S(1)} %convolution_convert_fusion.1), channel_id=1, source_target_pairs={{0,128},{128,0},{256,384},{384,256},{1,129},{129,1},{257,385},{385... | collective-permute-start | bytes 786440 | tf_op jit(solution)/shard_map/ppermute | solution.py:19
  33.5 4.7 %collective-permute-done.2 = bf16[256,512]{1,0:T(8,128)(2,1)S(1)} collective-permute-done((bf16[256,512]{1,0:T(8,128)(2,1)S(1)}, bf16[256,512]{1,0:T(8,128)(2,1)S(1)}, u32[]{:S(2)}, u32[]{:S(2)}) %collective-permute-start.2) | collective-permute-done | bytes 262176 | tf_op jit(solution)/shard_map/ppermute | solution.py:19
  38.7 3.1 %collective-permute-start.4 = (bf16[256,512]{1,0:T(8,128)(2,1)S(1)}, bf16[256,512]{1,0:T(8,128)(2,1)S(1)}, u32[]{:S(2)}, u32[]{:S(2)}) collective-permute-start(bf16[256,512]{1,0:T(8,128)(2,1)S(1)} %fusion.3), channel_id=1, source_target_pairs={{0,128},{128,0},{256,384},{384,256},{1,129},{129,1},{257,385},{385... | collective-permute-start | bytes 786440 | tf_op jit(solution)/shard_map/ppermute | solution.py:19
  42.2 1.9 %collective-permute-start.5 = (bf16[256,256]{1,0:T(8,128)(2,1)S(1)}, bf16[256,256]{1,0:T(8,128)(2,1)S(1)}, u32[]{:S(2)}, u32[]{:S(2)}) collective-permute-start(bf16[256,256]{1,0:T(8,128)(2,1)S(1)} %convolution_convert_fusion.3), channel_id=1, source_target_pairs={{0,32},{32,0},{1,33},{33,1},{2,34},{34,2},{3,35},{35,3},{4,36},{36... | collective-permute-start | bytes 393224 | tf_op jit(solution)/shard_map/ppermute | solution.py:19
  44.2 1.7 %collective-permute-done.4 = bf16[256,512]{1,0:T(8,128)(2,1)S(1)} collective-permute-done((bf16[256,512]{1,0:T(8,128)(2,1)S(1)}, bf16[256,512]{1,0:T(8,128)(2,1)S(1)}, u32[]{:S(2)}, u32[]{:S(2)}) %collective-permute-start.4) | collective-permute-done | bytes 262176 | tf_op jit(solution)/shard_map/ppermute | solution.py:19
  46.3 2.6 %collective-permute-done.5 = bf16[256,256]{1,0:T(8,128)(2,1)S(1)} collective-permute-done((bf16[256,256]{1,0:T(8,128)(2,1)S(1)}, bf16[256,256]{1,0:T(8,128)(2,1)S(1)}, u32[]{:S(2)}, u32[]{:S(2)}) %collective-permute-start.5) | collective-permute-done | bytes 131104 | tf_op jit(solution)/shard_map/ppermute | solution.py:19
  48.8 4.3 %collective-permute-start.6 = (bf16[256,512]{1,0:T(8,128)(2,1)S(1)}, bf16[256,512]{1,0:T(8,128)(2,1)S(1)}, u32[]{:S(2)}, u32[]{:S(2)}) collective-permute-start(bf16[256,512]{1,0:T(8,128)(2,1)S(1)} %fusion.4), channel_id=1, source_target_pairs={{0,256},{128,384},{256,0},{384,128},{1,257},{129,385},{257,1},{385... | collective-permute-start | bytes 786440 | tf_op jit(solution)/shard_map/ppermute | solution.py:19
  53.4 7.0 %collective-permute-start.7 = (bf16[256,256]{1,0:T(8,128)(2,1)S(1)}, bf16[256,256]{1,0:T(8,128)(2,1)}, u32[]{:S(2)}, u32[]{:S(2)}) collective-permute-start(bf16[256,256]{1,0:T(8,128)(2,1)S(1)} %convolution_convert_fusion.8), channel_id=1, source_target_pairs={{0,64},{64,0},{1,65},{65,1},{2,66},{66,2},{3,67},{67,3},{4,68},{68... | collective-permute-start | bytes 393224 | tf_op jit(solution)/shard_map/ppermute | solution.py:19
  61.9 8.3 %all-gather = bf16[512,512]{1,0:T(8,128)(2,1)S(1)} all-gather(bf16[256,512]{1,0:T(8,128)(2,1)S(1)} %fusion.5), channel_id=2, replica_groups=mesh['x'=4,'zb'=2,'za'=2,'zl'=2,'y'=8,'c'=2] {'c'}, dimensions={0}, use_global_device_ids=true | all-gather | bytes 786432 | tf_op jit(solution)/shard_map/all_gather | solution.py:133
  70.8 5.1 %collective-permute-start.8 = (bf16[256,256]{1,0:T(8,128)(2,1)S(1)}, bf16[256,256]{1,0:T(8,128)(2,1)}, u32[]{:S(2)}, u32[]{:S(2)}) collective-permute-start(bf16[256,256]{1,0:T(8,128)(2,1)S(1)} %convolution_convert_fusion.9), channel_id=1, source_target_pairs={{0,64},{64,0},{1,65},{65,1},{2,66},{66,2},{3,67},{67,3},{4,68},{68... | collective-permute-start | bytes 393224 | tf_op jit(solution)/shard_map/ppermute | solution.py:19
  76.8 6.9 %all-to-all-start = ((bf16[16,16,256]{2,1,0:T(8,128)(2,1)}), bf16[16,16,256]{2,1,0:T(8,128)(2,1)S(1)}, u32[]{:S(2)}, u32[]{:S(2)}) async-start(bf16[16,16,256]{2,1,0:T(8,128)(2,1)} %bitcast.14), calls=%async_computation | async-start | bytes 262144 | tf_op jit(solution)/shard_map/all_to_all | solution.py:140
  83.7 2.7 %all-gather.1 = bf16[512,512]{1,0:T(8,128)(2,1)S(1)} all-gather(bf16[256,512]{1,0:T(8,128)(2,1)S(1)} %fusion.3), channel_id=3, replica_groups=mesh['x'=4,'zb'=2,'za'=2,'zl'=2,'y'=8,'c'=2] {'c'}, dimensions={0}, use_global_device_ids=true | all-gather | bytes 786432 | tf_op jit(solution)/shard_map/all_gather | solution.py:138
  86.5 5.7 %all-to-all-done = bf16[16,16,256]{2,1,0:T(8,128)(2,1)S(1)} async-done(((bf16[16,16,256]{2,1,0:T(8,128)(2,1)}), bf16[16,16,256]{2,1,0:T(8,128)(2,1)S(1)}, u32[]{:S(2)}, u32[]{:S(2)}) %all-to-all-start) | async-done | bytes 131104 | tf_op jit(solution)/shard_map/all_to_all | solution.py:140
  92.7 1.1 convolution_convert_fusion.6
  94.7 5.5 %all-to-all-start.1 = ((bf16[64,16,256]{2,1,0:T(8,128)(2,1)}), bf16[64,16,256]{2,1,0:T(8,128)(2,1)}, u32[]{:S(2)}, u32[]{:S(2)}) async-start(bf16[64,16,256]{2,1,0:T(8,128)(2,1)} %broadcast_in_dim.9), calls=%async_computation.1 | async-start | bytes 1048576 | tf_op jit(solution)/shard_map/all_to_all | solution.py:51
  100.2 1.1 broadcast_select_fusion.7
  101.4 3.9 %all_gather.46 = bf16[2,512,256]{2,1,0:T(8,128)(2,1)S(1)} all-gather(bf16[1,512,256]{2,1,0:T(8,128)(2,1)S(1)} %bitcast.102), channel_id=1, replica_groups=mesh['x'=4,'zb'=2,'za'=2,'zl'=2,'y'=8,'c'=2] {'c'}, dimensions={0}, use_global_device_ids=true | all-gather | bytes 786432 | tf_op jit(solution)/shard_map/all_gather | solution.py:148
  105.3 2.2 %all_gather.44 = bf16[2,512,256]{2,1,0:T(8,128)(2,1)S(1)} all-gather(bf16[1,512,256]{2,1,0:T(8,128)(2,1)S(1)} %bitcast.103), channel_id=1, replica_groups=mesh['x'=4,'zb'=2,'za'=2,'zl'=2,'y'=8,'c'=2] {'c'}, dimensions={0}, use_global_device_ids=true | all-gather | bytes 786432 | tf_op jit(solution)/shard_map/all_gather | solution.py:148
  107.4 2.2 %all-gather.3 = bf16[512,512]{1,0:T(8,128)(2,1)S(1)} all-gather(bf16[256,512]{1,0:T(8,128)(2,1)S(1)} %pad_maximum_fusion.5), channel_id=5, replica_groups=mesh['x'=4,'zb'=2,'za'=2,'zl'=2,'y'=8,'c'=2] {'c'}, dimensions={0}, use_global_device_ids=true | all-gather | bytes 786432 | tf_op jit(solution)/shard_map/all_gather | solution.py:154
  109.6 2.2 %all-gather.2 = bf16[512,512]{1,0:T(8,128)(2,1)S(1)} all-gather(bf16[256,512]{1,0:T(8,128)(2,1)S(1)} %pad_maximum_fusion.4), channel_id=4, replica_groups=mesh['x'=4,'zb'=2,'za'=2,'zl'=2,'y'=8,'c'=2] {'c'}, dimensions={0}, use_global_device_ids=true | all-gather | bytes 786432 | tf_op jit(solution)/shard_map/all_gather | solution.py:154
  112.0 3.8 %all-to-all-done.1 = bf16[64,16,256]{2,1,0:T(8,128)(2,1)} async-done(((bf16[64,16,256]{2,1,0:T(8,128)(2,1)}), bf16[64,16,256]{2,1,0:T(8,128)(2,1)}, u32[]{:S(2)}, u32[]{:S(2)}) %all-to-all-start.1) | async-done | bytes 524320 | tf_op jit(solution)/shard_map/all_to_all | solution.py:51
  115.8 1.5 fusion.1
  117.7 23.0 %all_to_all.20 = bf16[64,16,256]{2,1,0:T(8,128)(2,1)S(1)} all-to-all(bf16[64,16,256]{2,1,0:T(8,128)(2,1)S(1)} %bitcast.97), channel_id=1, replica_groups=mesh['x'=4,'zb'=2,'za'=2,'zl'=2,'y'=8,'c'=2] {'y','zl','x'}, dimensions={0} | all-to-all | bytes 1048576 | tf_op jit(solution)/shard_map/all_to_all | solution.py:45
  140.9 13.9 %all_to_all.21 = bf16[16,16,256]{2,1,0:T(8,128)(2,1)S(1)} all-to-all(bf16[16,16,256]{2,1,0:T(8,128)(2,1)S(1)} %broadcast_in_dim.10), channel_id=1, replica_groups=mesh['x'=4,'zb'=2,'za'=2,'zl'=2,'y'=8,'c'=2] {'y','zl'}, dimensions={0} | all-to-all | bytes 262144 | tf_op jit(solution)/shard_map/all_to_all | solution.py:51
  154.8 5.7 %all_gather.51.total_hbm = bf16[2,256,256]{2,1,0:T(8,128)(2,1)S(1)} all-gather(bf16[1,256,256]{2,1,0:T(8,128)(2,1)S(1)} %bitcast.104), channel_id=1, replica_groups=mesh['x'=4,'zb'=2,'za'=2,'zl'=2,'y'=8,'c'=2] {'c'}, dimensions={0}, use_global_device_ids=true | all-gather | bytes 393216 | tf_op jit(solution)/shard_map/all_gather | solution.py:161
  160.5 2.6 %shard_map.46 = f32[1024,512]{1,0:T(8,128)} custom-call(bf16[1024,512]{1,0:T(8,128)(2,1)S(1)} %bitcast.95, bf16[1024,256]{1,0:T(8,128)(2,1)S(1)} %bitcast.96, bf16[2,256,256]{2,1,0:T(8,128)(2,1)S(1)} %all_gather.51.total_hbm), custom_call_target="tpu_custom_call" | custom-call | tf_op jit(solution)/shard_map/pallas_call | solution.py:86
  (49 shorter events, 7.2 us)
Async XLA Ops:
  0.0 1.0 copy-start
  0.0 9.4 %copy-start.3 = (bf16[4,1,1,2,256,256]{5,4,3,2,1,0:T(8,128)(2,1)S(1)}, bf16[4,1,1,2,256,256]{5,4,3,2,1,0:T(8,128)(2,1)}, u32[]{:S(2)}) copy-start(bf16[4,1,1,2,256,256]{5,4,3,2,1,0:T(8,128)(2,1)} %param.7) | copy-start | bytes 3145732
  2.7 17.1 %collective-permute-start = (bf16[256,512]{1,0:T(8,128)(2,1)S(1)}, bf16[256,512]{1,0:T(8,128)(2,1)S(1)}, u32[]{:S(2)}, u32[]{:S(2)}) collective-permute-start(bf16[256,512]{1,0:T(8,128)(2,1)S(1)} %convolution_convert_fusion.2), channel_id=1, source_target_pairs={{0,32},{32,0},{1,33},{33,1},{2,34},{34,2},{3,35},{35,3},{4,36},{36... | collective-permute-start | bytes 786440 | tf_op jit(solution)/shard_map/ppermute | solution.py:19
  9.4 10.7 %collective-permute-start.1 = (bf16[256,256]{1,0:T(8,128)(2,1)S(1)}, bf16[256,256]{1,0:T(8,128)(2,1)S(1)}, u32[]{:S(2)}, u32[]{:S(2)}) collective-permute-start(bf16[256,256]{1,0:T(8,128)(2,1)S(1)} %get-tuple-element.54), channel_id=1, source_target_pairs={{0,256},{128,384},{256,0},{384,128},{1,257},{129,385},{257,1},{385... | collective-permute-start | bytes 393224 | tf_op jit(solution)/shard_map/ppermute | solution.py:19
  14.3 27.6 %copy-start.2 = (bf16[1,1024,256]{2,1,0:T(8,128)(2,1)S(1)}, bf16[1,1024,256]{2,1,0:T(8,128)(2,1)}, u32[]{:S(2)}) copy-start(bf16[1,1024,256]{2,1,0:T(8,128)(2,1)} %param.6) | copy-start | bytes 1572868
  20.1 18.1 %collective-permute-start.2 = (bf16[256,512]{1,0:T(8,128)(2,1)S(1)}, bf16[256,512]{1,0:T(8,128)(2,1)S(1)}, u32[]{:S(2)}, u32[]{:S(2)}) collective-permute-start(bf16[256,512]{1,0:T(8,128)(2,1)S(1)} %fusion.2), channel_id=1, source_target_pairs={{0,64},{64,0},{1,65},{65,1},{2,66},{66,2},{3,67},{67,3},{4,68},{68... | collective-permute-start | bytes 786440 | tf_op jit(solution)/shard_map/ppermute | solution.py:19
  30.4 8.3 %collective-permute-start.3 = (bf16[512,256]{1,0:T(8,128)(2,1)S(1)}, bf16[512,256]{1,0:T(8,128)(2,1)S(1)}, u32[]{:S(2)}, u32[]{:S(2)}) collective-permute-start(bf16[512,256]{1,0:T(8,128)(2,1)S(1)} %convolution_convert_fusion.1), channel_id=1, source_target_pairs={{0,128},{128,0},{256,384},{384,256},{1,129},{129,1},{257,385},{385... | collective-permute-start | bytes 786440 | tf_op jit(solution)/shard_map/ppermute | solution.py:19
  38.7 7.1 %collective-permute-start.4 = (bf16[256,512]{1,0:T(8,128)(2,1)S(1)}, bf16[256,512]{1,0:T(8,128)(2,1)S(1)}, u32[]{:S(2)}, u32[]{:S(2)}) collective-permute-start(bf16[256,512]{1,0:T(8,128)(2,1)S(1)} %fusion.3), channel_id=1, source_target_pairs={{0,128},{128,0},{256,384},{384,256},{1,129},{129,1},{257,385},{385... | collective-permute-start | bytes 786440 | tf_op jit(solution)/shard_map/ppermute | solution.py:19
  42.2 6.6 %collective-permute-start.5 = (bf16[256,256]{1,0:T(8,128)(2,1)S(1)}, bf16[256,256]{1,0:T(8,128)(2,1)S(1)}, u32[]{:S(2)}, u32[]{:S(2)}) collective-permute-start(bf16[256,256]{1,0:T(8,128)(2,1)S(1)} %convolution_convert_fusion.3), channel_id=1, source_target_pairs={{0,32},{32,0},{1,33},{33,1},{2,34},{34,2},{3,35},{35,3},{4,36},{36... | collective-permute-start | bytes 393224 | tf_op jit(solution)/shard_map/ppermute | solution.py:19
  48.8 12.5 %collective-permute-start.6 = (bf16[256,512]{1,0:T(8,128)(2,1)S(1)}, bf16[256,512]{1,0:T(8,128)(2,1)S(1)}, u32[]{:S(2)}, u32[]{:S(2)}) collective-permute-start(bf16[256,512]{1,0:T(8,128)(2,1)S(1)} %fusion.4), channel_id=1, source_target_pairs={{0,256},{128,384},{256,0},{384,128},{1,257},{129,385},{257,1},{385... | collective-permute-start | bytes 786440 | tf_op jit(solution)/shard_map/ppermute | solution.py:19
  53.4 38.8 %collective-permute-start.7 = (bf16[256,256]{1,0:T(8,128)(2,1)S(1)}, bf16[256,256]{1,0:T(8,128)(2,1)}, u32[]{:S(2)}, u32[]{:S(2)}) collective-permute-start(bf16[256,256]{1,0:T(8,128)(2,1)S(1)} %convolution_convert_fusion.8), channel_id=1, source_target_pairs={{0,64},{64,0},{1,65},{65,1},{2,66},{66,2},{3,67},{67,3},{4,68},{68... | collective-permute-start | bytes 393224 | tf_op jit(solution)/shard_map/ppermute | solution.py:19
  70.8 21.4 %collective-permute-start.8 = (bf16[256,256]{1,0:T(8,128)(2,1)S(1)}, bf16[256,256]{1,0:T(8,128)(2,1)}, u32[]{:S(2)}, u32[]{:S(2)}) collective-permute-start(bf16[256,256]{1,0:T(8,128)(2,1)S(1)} %convolution_convert_fusion.9), channel_id=1, source_target_pairs={{0,64},{64,0},{1,65},{65,1},{2,66},{66,2},{3,67},{67,3},{4,68},{68... | collective-permute-start | bytes 393224 | tf_op jit(solution)/shard_map/ppermute | solution.py:19
  76.8 15.4 %all-to-all-start = ((bf16[16,16,256]{2,1,0:T(8,128)(2,1)}), bf16[16,16,256]{2,1,0:T(8,128)(2,1)S(1)}, u32[]{:S(2)}, u32[]{:S(2)}) async-start(bf16[16,16,256]{2,1,0:T(8,128)(2,1)} %bitcast.14), calls=%async_computation | async-start | bytes 262144 | tf_op jit(solution)/shard_map/all_to_all | solution.py:140
  92.6 7.6 %copy-start.4 = (bf16[256,256]{1,0:T(8,128)(2,1)S(1)}, bf16[256,256]{1,0:T(8,128)(2,1)}, u32[]{:S(2)}) copy-start(bf16[256,256]{1,0:T(8,128)(2,1)} %convolution_convert_fusion.4) | copy-start | bytes 393220
  92.6 7.6 %copy-start.5 = (bf16[256,256]{1,0:T(8,128)(2,1)S(1)}, bf16[256,256]{1,0:T(8,128)(2,1)}, u32[]{:S(2)}) copy-start(bf16[256,256]{1,0:T(8,128)(2,1)} %convolution_convert_fusion.5) | copy-start | bytes 393220
  94.7 21.1 %all-to-all-start.1 = ((bf16[64,16,256]{2,1,0:T(8,128)(2,1)}), bf16[64,16,256]{2,1,0:T(8,128)(2,1)}, u32[]{:S(2)}, u32[]{:S(2)}) async-start(bf16[64,16,256]{2,1,0:T(8,128)(2,1)} %broadcast_in_dim.9), calls=%async_computation.1 | async-start | bytes 1048576 | tf_op jit(solution)/shard_map/all_to_all | solution.py:51
  117.3 43.2 %copy-start.1 = (bf16[1,1024,512]{2,1,0:T(8,128)(2,1)S(1)}, bf16[1,1024,512]{2,1,0:T(8,128)(2,1)}, u32[]{:S(2)}) copy-start(bf16[1,1024,512]{2,1,0:T(8,128)(2,1)} %param.4) | copy-start | bytes 3145732

commit v6 on v4

--- a/solution.py
+++ b/solution.py
@@ -7,8 +7,8 @@
 
 BF = jnp.bfloat16
 F32 = jnp.float32
-LINE = ("y", "zl")
-GROUP = LINE + ("x",)
+LINE = ("zl", "y")
+GROUP = ("x",) + LINE
 QUAD = ("zb", "za")
 CHUNKS = 4
 
@@ -100,28 +100,28 @@
     rank = basis.shape[1]
     core = lax.axis_index("c")
 
+    tie = lax.optimization_barrier
     start = mm("lk,lr->kr", basis, rhs).astype(BF)
-    start, transfer = lax.optimization_barrier((start, transfer))
+    start, transfer = tie((start, transfer))
     own = transfer[:, 0, 0, 0]
     other = transfer[:, 0, 0, 1]
 
-    kept_part = dot(own[0], start)
-    kept_part, far = lax.optimization_barrier((kept_part, other[3]))
-    far = swap(far, "x", 2)
-    field = (kept_part + dot(other[0], swap(start, "za", 1))).astype(BF)
-    field = (dot(own[1], field) + dot(other[1], swap(field, "zb", 1))).astype(BF)
+    far = swap(other[3], "x", 2)
+    field = (dot(own[0], start) + dot(other[0], swap(start, "za", 1))).astype(BF)
+    field, far = tie((field, far))
+    wide = jnp.concatenate([own[3], far], 0)
+    came = swap(dot(wide, other[2]).astype(BF), "x", 1)
+    kept = lax.all_gather(dot(wide, own[2]).astype(BF), "c")
+    kept, basis = tie((kept, basis))
 
-    wide = jnp.concatenate([own[3], far], 0)
-    kept = dot(wide, own[2]).astype(BF)
-    came = swap(dot(wide, other[2]).astype(BF), "x", 1)
-    tail = in_order([kept[:rank], came[:rank], kept[rank:], came[rank:]], "x")
-    tail = jnp.stack([t.reshape(lax.axis_size(LINE), -1, rank) for t in tail], 1).reshape(4 * rank, rank)
-    tail = [lax.all_gather(tail[i : i + 2 * rank], "c") for i in (0, 2 * rank)]
-    tail = jnp.concatenate(tail, 1)
-
-    tail, basis = lax.optimization_barrier((tail, basis))
     gram = mm("li,lj->ij", basis, out_basis).astype(BF)
     near = swap(gram, "za", 1)
+    field = (dot(own[1], field) + dot(other[1], swap(field, "zb", 1))).astype(BF)
+    field, came, kept = tie((field, came, kept))
+
+    came = lax.all_gather(came, "c")
+    tail = in_order([kept[:, :rank], came[:, :rank], kept[:, rank:], came[:, rank:]], "x")
+    tail = tie(jnp.concatenate(tail, 1))
 
     field = lax.all_gather(field, "c")
     field, near = lax.optimization_barrier((field, near))

time: 153 us -> 149 us (0.974)
  waiting for transfers between devices: 26.2 us -> 21.5 us
  starting transfers between devices: 47.2 us -> 51 us
  blocking collectives: 61.5 us -> 58.8 us
    ppermute x6, waiting for transfers between devices: 11 us -> 6.13 us  [swap(): return lax.ppermute(block, axis, [(i, i ^ bit) for i in range(size)])]
    all_gather x1, blocking collectives: 6.99 us -> 2.18 us  [body(): field = lax.all_gather(field, 'c')]
    all_gather x2, blocking collectives: 5.86 us -> 10.3 us  [the longest x1 6.48 us: body(): came = lax.all_gather(came, 'c')]
    all_to_all x1, starting transfers between devices: 8.41 us -> 10.3 us  [add_up(): pieces = lax.all_to_all(pieces, GROUP, 0, 0, tiled=True)]
    all_to_all x1, blocking collectives: 23.2 us -> 21.4 us  [add_up(): pieces = lax.all_to_all(pieces, GROUP, 0, 0, tiled=True)]
where the time goes in v6:
time: 149 us
  blocking collectives  58.8 us (39%)
  starting transfers between devices  51 us (34%)
  waiting for transfers between devices  21.5 us (14%)
  matrix products  11.4 us (8%)
  Pallas kernels  2.62 us (2%)
  local copies, waits for them, and re-layouts  1.92 us (1%)
    ppermute x6, starting transfers between devices, swap(): return lax.ppermute(block, axis, [(i, i ^ bit) for i in range(size)])  31.2 us
    all_to_all x1, blocking collectives, add_up(): pieces = lax.all_to_all(pieces, GROUP, 0, 0, tiled=True)  21.4 us
    all_to_all x1, blocking collectives, hand_out(): return lax.all_to_all(copies, axes, 0, 0, tiled=True)  12.8 us
    all_to_all x1, starting transfers between devices, add_up(): pieces = lax.all_to_all(pieces, GROUP, 0, 0, tiled=True)  10.3 us
    all_to_all x1, starting transfers between devices, hand_out(): return lax.all_to_all(copies, axes, 0, 0, tiled=True)  9.52 us
    all_to_all x1, waiting for transfers between devices, add_up(): pieces = lax.all_to_all(pieces, GROUP, 0, 0, tiled=True)  8.29 us
    all_to_all x1, waiting for transfers between devices, hand_out(): return lax.all_to_all(copies, axes, 0, 0, tiled=True)  7.1 us
    all_gather x1, blocking collectives, body(): came = lax.all_gather(came, 'c')  6.48 us
  transfers between devices with their start and end apart: 8, of which 4 were waited for; matrix products, arithmetic and copies ran while one was open for 5% of the time, Pallas kernels for 0%

profile of v6, /device:TPU:1, one launch (start us, length us, event | category | flops | bytes accessed | tf_op | source)
XLA Modules:
  0.0 148.6 jit_solution(13207462927075780074)
XLA Ops:
  0.0 1.0 copy-done
  1.0 1.7 %convolution_convert_fusion.4 = bf16[256,512]{1,0:T(8,128)(2,1)S(1)} fusion(bf16[1,1024,256]{2,1,0:T(8,128)(2,1)S(1)} %copy-done, bf16[1,1024,512]{2,1,0:T(8,128)(2,1)} %param.4), kind=kOutput, calls=%fused_computation.10 | convolution fusion | flops 268566528 | bytes 1835008 | tf_op jit(solution)/shard_map/lk,lr->kr/dot_general | solution.py:22
  2.7 6.6 %collective-permute-start = (bf16[256,512]{1,0:T(8,128)(2,1)S(1)}, bf16[256,512]{1,0:T(8,128)(2,1)S(1)}, u32[]{:S(2)}, u32[]{:S(2)}) collective-permute-start(bf16[256,512]{1,0:T(8,128)(2,1)S(1)} %convolution_convert_fusion.4), channel_id=1, source_target_pairs={{0,32},{32,0},{1,33},{33,1},{2,34},{34,2},{3,35},{35,3},{4,36},{36... | collective-permute-start | bytes 786440 | tf_op jit(solution)/shard_map/ppermute | solution.py:18
  9.4 4.7 %collective-permute-start.1 = (bf16[256,256]{1,0:T(8,128)(2,1)S(1)}, bf16[256,256]{1,0:T(8,128)(2,1)S(1)}, u32[]{:S(2)}, u32[]{:S(2)}) collective-permute-start(bf16[256,256]{1,0:T(8,128)(2,1)S(1)} %get-tuple-element.32), channel_id=1, source_target_pairs={{0,256},{128,384},{256,0},{384,128},{1,257},{129,385},{257,1},{385... | collective-permute-start | bytes 393224 | tf_op jit(solution)/shard_map/ppermute | solution.py:18
  14.3 5.5 %collective-permute-done = bf16[256,512]{1,0:T(8,128)(2,1)S(1)} collective-permute-done((bf16[256,512]{1,0:T(8,128)(2,1)S(1)}, bf16[256,512]{1,0:T(8,128)(2,1)S(1)}, u32[]{:S(2)}, u32[]{:S(2)}) %collective-permute-start) | collective-permute-done | bytes 262176 | tf_op jit(solution)/shard_map/ppermute | solution.py:18
  20.6 10.0 %collective-permute-start.2 = (bf16[256,512]{1,0:T(8,128)(2,1)S(1)}, bf16[256,512]{1,0:T(8,128)(2,1)S(1)}, u32[]{:S(2)}, u32[]{:S(2)}) collective-permute-start(bf16[256,512]{1,0:T(8,128)(2,1)S(1)} %fusion.2), channel_id=1, source_target_pairs={{0,64},{64,0},{1,65},{65,1},{2,66},{66,2},{3,67},{67,3},{4,68},{68... | collective-permute-start | bytes 786440 | tf_op jit(solution)/shard_map/ppermute | solution.py:18
  30.6 3.1 %collective-permute-start.3 = (bf16[512,256]{1,0:T(8,128)(2,1)S(1)}, bf16[512,256]{1,0:T(8,128)(2,1)S(1)}, u32[]{:S(2)}, u32[]{:S(2)}) collective-permute-start(bf16[512,256]{1,0:T(8,128)(2,1)S(1)} %convolution_convert_fusion.3), channel_id=1, source_target_pairs={{0,128},{128,0},{256,384},{384,256},{1,129},{129,1},{257,385},{385... | collective-permute-start | bytes 786440 | tf_op jit(solution)/shard_map/ppermute | solution.py:18
  33.7 3.8 %all-gather = bf16[1024,256]{1,0:T(8,128)(2,1)S(1)} all-gather(bf16[512,256]{1,0:T(8,128)(2,1)S(1)} %convolution_convert_fusion.2), channel_id=2, replica_groups=mesh['x'=4,'zb'=2,'za'=2,'zl'=2,'y'=8,'c'=2] {'c'}, dimensions={0}, use_global_device_ids=true | all-gather | bytes 786432 | tf_op jit(solution)/shard_map/all_gather | solution.py:114
  37.9 1.9 %collective-permute-start.4 = (bf16[256,256]{1,0:T(8,128)(2,1)S(1)}, bf16[256,256]{1,0:T(8,128)(2,1)S(1)}, u32[]{:S(2)}, u32[]{:S(2)}) collective-permute-start(bf16[256,256]{1,0:T(8,128)(2,1)S(1)} %convolution_convert_fusion.5), channel_id=1, source_target_pairs={{0,32},{32,0},{1,33},{33,1},{2,34},{34,2},{3,35},{35,3},{4,36},{36... | collective-permute-start | bytes 393224 | tf_op jit(solution)/shard_map/ppermute | solution.py:18
  40.3 6.5 %all-gather.1 = bf16[1024,256]{1,0:T(8,128)(2,1)S(1)} all-gather(bf16[512,256]{1,0:T(8,128)(2,1)S(1)} %collective-permute-done.3), channel_id=3, replica_groups=mesh['x'=4,'zb'=2,'za'=2,'zl'=2,'y'=8,'c'=2] {'c'}, dimensions={0}, use_global_device_ids=true | all-gather | bytes 786432 | tf_op jit(solution)/shard_map/all_gather | solution.py:122
  46.9 2.2 %all-gather.2 = bf16[512,512]{1,0:T(8,128)(2,1)S(1)} all-gather(bf16[256,512]{1,0:T(8,128)(2,1)S(1)} %fusion.3), channel_id=4, replica_groups=mesh['x'=4,'zb'=2,'za'=2,'zl'=2,'y'=8,'c'=2] {'c'}, dimensions={0}, use_global_device_ids=true | all-gather | bytes 786432 | tf_op jit(solution)/shard_map/all_gather | solution.py:126
  49.1 0.6 collective-permute-done.4
  49.7 1.2 fusion
  50.9 10.3 %all-to-all-start = ((bf16[64,16,256]{2,1,0:T(8,128)(2,1)}), bf16[64,16,256]{2,1,0:T(8,128)(2,1)S(1)}, u32[]{:S(2)}, u32[]{:S(2)}) async-start(bf16[64,16,256]{2,1,0:T(8,128)(2,1)} %bitcast.17), calls=%async_computation | async-start | bytes 1048576 | tf_op jit(solution)/shard_map/all_to_all | solution.py:40
  61.2 1.1 convolution_convert_fusion.7
  62.4 1.1 convolution_convert_fusion.6
  63.5 0.7 pad_maximum_fusion.2
  64.2 4.8 %collective-permute-start.5 = (bf16[256,512]{0,1:T(8,128)(2,1)}, bf16[256,512]{0,1:T(8,128)(2,1)}, u32[]{:S(2)}, u32[]{:S(2)}) collective-permute-start(bf16[256,512]{0,1:T(8,128)(2,1)} %pad_maximum_fusion.2), channel_id=1, source_target_pairs={{0,64},{64,0},{1,65},{65,1},{2,66},{66,2},{3,67},{67,3},{4,68},{68... | collective-permute-start | bytes 786440 | tf_op jit(solution)/shard_map/ppermute | solution.py:18
  69.0 8.3 %all-to-all-done = bf16[64,16,256]{2,1,0:T(8,128)(2,1)S(1)} async-done(((bf16[64,16,256]{2,1,0:T(8,128)(2,1)}), bf16[64,16,256]{2,1,0:T(8,128)(2,1)S(1)}, u32[]{:S(2)}, u32[]{:S(2)}) %all-to-all-start) | async-done | bytes 524320 | tf_op jit(solution)/shard_map/all_to_all | solution.py:40
  77.4 0.8 broadcast_in_dim.9
  78.3 9.5 %all-to-all-start.1 = ((bf16[64,16,256]{2,1,0:T(8,128)(2,1)}), bf16[64,16,256]{2,1,0:T(8,128)(2,1)}, u32[]{:S(2)}, u32[]{:S(2)}) async-start(bf16[64,16,256]{2,1,0:T(8,128)(2,1)} %broadcast_in_dim.9), calls=%async_computation.1 | async-start | bytes 1048576 | tf_op jit(solution)/shard_map/all_to_all | solution.py:46
  87.8 1.2 convolution_convert_fusion
  89.0 1.3 convolution_convert_fusion.1
  90.4 3.7 %all-gather.4 = bf16[512,512]{1,0:T(8,128)(2,1)S(1)} all-gather(bf16[256,512]{1,0:T(8,128)(2,1)S(1)} %pad_maximum_fusion.4), channel_id=6, replica_groups=mesh['x'=4,'zb'=2,'za'=2,'zl'=2,'y'=8,'c'=2] {'c'}, dimensions={0}, use_global_device_ids=true | all-gather | bytes 786432 | tf_op jit(solution)/shard_map/all_gather | solution.py:137
  94.1 2.3 %all-gather.3 = bf16[512,512]{1,0:T(8,128)(2,1)} all-gather(bf16[256,512]{1,0:T(8,128)(2,1)S(1)} %pad_maximum_fusion.3), channel_id=5, replica_groups=mesh['x'=4,'zb'=2,'za'=2,'zl'=2,'y'=8,'c'=2] {'c'}, dimensions={0}, use_global_device_ids=true | all-gather | bytes 786432 | tf_op jit(solution)/shard_map/all_gather | solution.py:137
  96.4 7.1 %all-to-all-done.1 = bf16[64,16,256]{2,1,0:T(8,128)(2,1)} async-done(((bf16[64,16,256]{2,1,0:T(8,128)(2,1)}), bf16[64,16,256]{2,1,0:T(8,128)(2,1)}, u32[]{:S(2)}, u32[]{:S(2)}) %all-to-all-start.1) | async-done | bytes 524320 | tf_op jit(solution)/shard_map/all_to_all | solution.py:46
  103.5 1.6 %subtract_convert_fusion = bf16[2,256,256]{2,1,0:T(8,128)(2,1)S(1)} fusion(bf16[2,256,512]{2,1,0:T(8,128)(2,1)S(1)} %bitcast.78, s32[]{:T(128)S(6)} %select_n.89, bf16[1024,256,1]{1,0,2:T(8,128)(2,1)} %bitcast.19, bf16[2,256,512]{2,1,0:T(8,128)(2,1)S(1)} %bitcast.80, bf16[2,256,512]{2,1,0:T(8,128)(2,1)} %bitcast.81), kind=kOutput, calls=%fused_computation.21 | convolution fusion | flops 270925824 | bytes 2097156 | tf_op jit(solution)/shard_map/cij,jr->cir/dot_general | solution.py:22
  105.2 0.4 fusion.1
  105.6 21.4 %all_to_all.20 = bf16[64,16,256]{2,1,0:T(8,128)(2,1)S(1)} all-to-all(bf16[64,16,256]{2,1,0:T(8,128)(2,1)S(1)} %bitcast.74), channel_id=1, replica_groups=mesh['x'=4,'zb'=2,'za'=2,'zl'=2,'y'=8,'c'=2] {'x','zl','y'}, dimensions={0} | all-to-all | bytes 1048576 | tf_op jit(solution)/shard_map/all_to_all | solution.py:40
  127.1 12.8 %all_to_all.21 = bf16[16,16,256]{2,1,0:T(8,128)(2,1)S(1)} all-to-all(bf16[16,16,256]{2,1,0:T(8,128)(2,1)S(1)} %broadcast_in_dim.10), channel_id=1, replica_groups=mesh['x'=4,'zb'=2,'za'=2,'zl'=2,'y'=8,'c'=2] {'zl','y'}, dimensions={0} | all-to-all | bytes 262144 | tf_op jit(solution)/shard_map/all_to_all | solution.py:46
  139.9 6.1 %all_gather.43.total_hbm = bf16[2,256,256]{2,1,0:T(8,128)(2,1)S(1)} all-gather(bf16[1,256,256]{2,1,0:T(8,128)(2,1)S(1)} %bitcast.79), channel_id=1, replica_groups=mesh['x'=4,'zb'=2,'za'=2,'zl'=2,'y'=8,'c'=2] {'c'}, dimensions={0}, use_global_device_ids=true | all-gather | bytes 393216 | tf_op jit(solution)/shard_map/all_gather | solution.py:143
  146.0 2.6 %shard_map.46 = f32[1024,512]{1,0:T(8,128)} custom-call(bf16[1024,512]{1,0:T(8,128)(2,1)S(1)} %bitcast.72, bf16[1024,256]{1,0:T(8,128)(2,1)S(1)} %bitcast.73, bf16[2,256,256]{2,1,0:T(8,128)(2,1)S(1)} %all_gather.43.total_hbm), custom_call_target="tpu_custom_call" | custom-call | tf_op jit(solution)/shard_map/pallas_call | solution.py:81
  (27 shorter events, 2.2 us)
Async XLA Ops:
  0.0 1.0 copy-start
  0.0 9.4 %copy-start.3 = (bf16[4,1,1,2,256,256]{5,4,3,2,1,0:T(8,128)(2,1)S(1)}, bf16[4,1,1,2,256,256]{5,4,3,2,1,0:T(8,128)(2,1)}, u32[]{:S(2)}) copy-start(bf16[4,1,1,2,256,256]{5,4,3,2,1,0:T(8,128)(2,1)} %param.7) | copy-start | bytes 3145732
  2.7 17.1 %collective-permute-start = (bf16[256,512]{1,0:T(8,128)(2,1)S(1)}, bf16[256,512]{1,0:T(8,128)(2,1)S(1)}, u32[]{:S(2)}, u32[]{:S(2)}) collective-permute-start(bf16[256,512]{1,0:T(8,128)(2,1)S(1)} %convolution_convert_fusion.4), channel_id=1, source_target_pairs={{0,32},{32,0},{1,33},{33,1},{2,34},{34,2},{3,35},{35,3},{4,36},{36... | collective-permute-start | bytes 786440 | tf_op jit(solution)/shard_map/ppermute | solution.py:18
  9.4 10.7 %collective-permute-start.1 = (bf16[256,256]{1,0:T(8,128)(2,1)S(1)}, bf16[256,256]{1,0:T(8,128)(2,1)S(1)}, u32[]{:S(2)}, u32[]{:S(2)}) collective-permute-start(bf16[256,256]{1,0:T(8,128)(2,1)S(1)} %get-tuple-element.32), channel_id=1, source_target_pairs={{0,256},{128,384},{256,0},{384,128},{1,257},{129,385},{257,1},{385... | collective-permute-start | bytes 393224 | tf_op jit(solution)/shard_map/ppermute | solution.py:18
  14.1 23.5 %copy-start.2 = (bf16[1,1024,256]{2,1,0:T(8,128)(2,1)S(1)}, bf16[1,1024,256]{2,1,0:T(8,128)(2,1)}, u32[]{:S(2)}) copy-start(bf16[1,1024,256]{2,1,0:T(8,128)(2,1)} %param.6) | copy-start | bytes 1572868
  20.6 19.2 %collective-permute-start.2 = (bf16[256,512]{1,0:T(8,128)(2,1)S(1)}, bf16[256,512]{1,0:T(8,128)(2,1)S(1)}, u32[]{:S(2)}, u32[]{:S(2)}) collective-permute-start(bf16[256,512]{1,0:T(8,128)(2,1)S(1)} %fusion.2), channel_id=1, source_target_pairs={{0,64},{64,0},{1,65},{65,1},{2,66},{66,2},{3,67},{67,3},{4,68},{68... | collective-permute-start | bytes 786440 | tf_op jit(solution)/shard_map/ppermute | solution.py:18
  30.6 9.7 %collective-permute-start.3 = (bf16[512,256]{1,0:T(8,128)(2,1)S(1)}, bf16[512,256]{1,0:T(8,128)(2,1)S(1)}, u32[]{:S(2)}, u32[]{:S(2)}) collective-permute-start(bf16[512,256]{1,0:T(8,128)(2,1)S(1)} %convolution_convert_fusion.3), channel_id=1, source_target_pairs={{0,128},{128,0},{256,384},{384,256},{1,129},{129,1},{257,385},{385... | collective-permute-start | bytes 786440 | tf_op jit(solution)/shard_map/ppermute | solution.py:18
  37.9 11.8 %collective-permute-start.4 = (bf16[256,256]{1,0:T(8,128)(2,1)S(1)}, bf16[256,256]{1,0:T(8,128)(2,1)S(1)}, u32[]{:S(2)}, u32[]{:S(2)}) collective-permute-start(bf16[256,256]{1,0:T(8,128)(2,1)S(1)} %convolution_convert_fusion.5), channel_id=1, source_target_pairs={{0,32},{32,0},{1,33},{33,1},{2,34},{34,2},{3,35},{35,3},{4,36},{36... | collective-permute-start | bytes 393224 | tf_op jit(solution)/shard_map/ppermute | solution.py:18
  50.9 26.4 %all-to-all-start = ((bf16[64,16,256]{2,1,0:T(8,128)(2,1)}), bf16[64,16,256]{2,1,0:T(8,128)(2,1)S(1)}, u32[]{:S(2)}, u32[]{:S(2)}) async-start(bf16[64,16,256]{2,1,0:T(8,128)(2,1)} %bitcast.17), calls=%async_computation | async-start | bytes 1048576 | tf_op jit(solution)/shard_map/all_to_all | solution.py:40
  64.2 24.8 %collective-permute-start.5 = (bf16[256,512]{0,1:T(8,128)(2,1)}, bf16[256,512]{0,1:T(8,128)(2,1)}, u32[]{:S(2)}, u32[]{:S(2)}) collective-permute-start(bf16[256,512]{0,1:T(8,128)(2,1)} %pad_maximum_fusion.2), channel_id=1, source_target_pairs={{0,64},{64,0},{1,65},{65,1},{2,66},{66,2},{3,67},{67,3},{4,68},{68... | collective-permute-start | bytes 786440 | tf_op jit(solution)/shard_map/ppermute | solution.py:18
  78.3 25.2 %all-to-all-start.1 = ((bf16[64,16,256]{2,1,0:T(8,128)(2,1)}), bf16[64,16,256]{2,1,0:T(8,128)(2,1)}, u32[]{:S(2)}, u32[]{:S(2)}) async-start(bf16[64,16,256]{2,1,0:T(8,128)(2,1)} %broadcast_in_dim.9), calls=%async_computation.1 | async-start | bytes 1048576 | tf_op jit(solution)/shard_map/all_to_all | solution.py:46
  105.1 40.9 %copy-start.1 = (bf16[1,1024,512]{2,1,0:T(8,128)(2,1)S(1)}, bf16[1,1024,512]{2,1,0:T(8,128)(2,1)}, u32[]{:S(2)}) copy-start(bf16[1,1024,512]{2,1,0:T(8,128)(2,1)} %param.4) | copy-start | bytes 3145732

commit v7 on v6

--- a/solution.py
+++ b/solution.py
@@ -101,14 +101,16 @@
     core = lax.axis_index("c")
 
     tie = lax.optimization_barrier
-    start = mm("lk,lr->kr", basis, rhs).astype(BF)
-    start, transfer = tie((start, transfer))
+    parts = [mm("lk,lr->kr", basis, rhs[:, :half]).astype(BF)]
+    parts[0], basis = tie((parts[0], basis))
+    parts.append(mm("lk,lr->kr", basis, rhs[:, half:]).astype(BF))
+    parts[1], transfer = tie((parts[1], transfer))
     own = transfer[:, 0, 0, 0]
     other = transfer[:, 0, 0, 1]
 
     far = swap(other[3], "x", 2)
-    field = (dot(own[0], start) + dot(other[0], swap(start, "za", 1))).astype(BF)
-    field, far = tie((field, far))
+    parts = [(dot(own[0], p) + dot(other[0], swap(p, "za", 1))).astype(BF) for p in parts]
+    *_, far = tie((*parts, far))
     wide = jnp.concatenate([own[3], far], 0)
     came = swap(dot(wide, other[2]).astype(BF), "x", 1)
     kept = lax.all_gather(dot(wide, own[2]).astype(BF), "c")
@@ -116,17 +118,17 @@
 
     gram = mm("li,lj->ij", basis, out_basis).astype(BF)
     near = swap(gram, "za", 1)
-    field = (dot(own[1], field) + dot(other[1], swap(field, "zb", 1))).astype(BF)
-    field, came, kept = tie((field, came, kept))
+    parts = [(dot(own[1], p) + dot(other[1], swap(p, "zb", 1))).astype(BF) for p in parts]
+    *_, came, kept = tie((*parts, came, kept))
 
     came = lax.all_gather(came, "c")
     tail = in_order([kept[:, :rank], came[:, :rank], kept[:, rank:], came[:, rank:]], "x")
     tail = tie(jnp.concatenate(tail, 1))
 
-    field = lax.all_gather(field, "c")
+    parts = [lax.all_gather(p, "c") for p in parts]
+    field = jnp.where(core == 0, parts[0], parts[1])
     field, near = lax.optimization_barrier((field, near))
     chain = jnp.concatenate([dot(own[0], gram).astype(BF), dot(other[0], near).astype(BF)], 1)
-    field = lax.dynamic_slice_in_dim(field, core * half, half, 2)
     share = add_up(tail, field)
     totals = hand_out(share, QUAD + LINE).reshape(4 * rank, half)
 

time: 149 us -> 153 us (1.027)
  starting transfers between devices: 51 us -> 58.9 us
  waiting for transfers between devices: 21.5 us -> 14.6 us
  matrix products: 11.4 us -> 13 us
    ppermute x6 -> x8, waiting for transfers between devices: 6.13 us -> 0.26 us  [swap(): return lax.ppermute(block, axis, [(i, i ^ bit) for i in range(size)])]
    ppermute x6 -> x8, starting transfers between devices: 31.2 us -> 35.6 us  [swap(): return lax.ppermute(block, axis, [(i, i ^ bit) for i in range(size)])]
    all_to_all x1, starting transfers between devices: 10.3 us -> 14.7 us  [add_up(): pieces = lax.all_to_all(pieces, GROUP, 0, 0, tiled=True)]
    all_gather x1, blocking collectives: 6.48 us -> 3 us  [body(): came = lax.all_gather(came, 'c')]
    all_gather x1 -> x2, blocking collectives: 2.18 us -> 4.28 us  [body(): parts = [lax.all_gather(p, 'c') for p in parts]]
    dot_general x5 -> x6, matrix products: 5.31 us -> 6.42 us  [mm(): return jnp.einsum(spec, a, b, preferred_element_type=F32)]
    dot_general x10 -> x14, matrix products: 6.05 us -> 6.56 us  [dot(): return jnp.dot(a, b, preferred_element_type=F32)]
  transfers between devices with their start and end apart: 8 -> 10, of which waited for: 4 -> 3; matrix products, arithmetic and copies ran while one was open for 5% -> 7% of each run, Pallas kernels for 0% -> 0%
where the time goes in v7:
time: 153 us; the launch traced here: 152 us
  starting transfers between devices  58.9 us (38%)
  blocking collectives  57.9 us (38%)
  waiting for transfers between devices  14.6 us (10%)
  matrix products  13 us (8%)
  Pallas kernels  2.63 us (2%)
  local copies, waits for them, and re-layouts  2.58 us (2%)
  other arithmetic  2.25 us (1%)
    ppermute x8, starting transfers between devices, swap(): return lax.ppermute(block, axis, [(i, i ^ bit) for i in range(size)])  35.6 us
    all_to_all x1, blocking collectives, add_up(): pieces = lax.all_to_all(pieces, GROUP, 0, 0, tiled=True)  22 us
    all_to_all x1, starting transfers between devices, add_up(): pieces = lax.all_to_all(pieces, GROUP, 0, 0, tiled=True)  14.7 us
    all_to_all x1, blocking collectives, hand_out(): return lax.all_to_all(copies, axes, 0, 0, tiled=True)  12.8 us
    all_to_all x1, starting transfers between devices, hand_out(): return lax.all_to_all(copies, axes, 0, 0, tiled=True)  8.59 us
    all_to_all x1, waiting for transfers between devices, add_up(): pieces = lax.all_to_all(pieces, GROUP, 0, 0, tiled=True)  7.46 us
    all_to_all x1, waiting for transfers between devices, hand_out(): return lax.all_to_all(copies, axes, 0, 0, tiled=True)  6.93 us
    dot_general x14, matrix products, dot(): return jnp.dot(a, b, preferred_element_type=F32)  6.56 us
  transfers between devices with their start and end apart: 10, of which 3 were waited for; matrix products, arithmetic and copies ran while one was open for 7% of the time, Pallas kernels for 0%

profile of v7, /device:TPU:1, one launch (start us, length us, event | category | flops | bytes accessed | tf_op | source)
XLA Modules:
  0.0 152.3 jit_solution(7356231980012124466)
XLA Ops:
  0.0 1.0 copy-done
  1.0 1.4 convolution_convert_fusion.6
  2.4 6.6 %collective-permute-start = (bf16[256,256]{1,0:T(8,128)(2,1)S(1)}, bf16[256,256]{1,0:T(8,128)(2,1)S(1)}, u32[]{:S(2)}, u32[]{:S(2)}) collective-permute-start(bf16[256,256]{1,0:T(8,128)(2,1)S(1)} %convolution_convert_fusion.6), channel_id=1, source_target_pairs={{0,32},{32,0},{1,33},{33,1},{2,34},{34,2},{3,35},{35,3},{4,36},{36... | collective-permute-start | bytes 393224 | tf_op jit(solution)/shard_map/ppermute | solution.py:18
  9.1 1.4 convolution_convert_fusion.5
  10.5 1.9 %collective-permute-start.2 = (bf16[256,256]{1,0:T(8,128)(2,1)S(1)}, bf16[256,256]{1,0:T(8,128)(2,1)S(1)}, u32[]{:S(2)}, u32[]{:S(2)}) collective-permute-start(bf16[256,256]{1,0:T(8,128)(2,1)S(1)} %convolution_convert_fusion.5), channel_id=1, source_target_pairs={{0,32},{32,0},{1,33},{33,1},{2,34},{34,2},{3,35},{35,3},{4,36},{36... | collective-permute-start | bytes 393224 | tf_op jit(solution)/shard_map/ppermute | solution.py:18
  12.4 4.7 %collective-permute-start.4 = (bf16[256,256]{1,0:T(8,128)(2,1)S(1)}, bf16[256,256]{1,0:T(8,128)(2,1)S(1)}, u32[]{:S(2)}, u32[]{:S(2)}) collective-permute-start(bf16[256,256]{1,0:T(8,128)(2,1)S(1)} %get-tuple-element.32), channel_id=1, source_target_pairs={{0,256},{128,384},{256,0},{384,128},{1,257},{129,385},{257,1},{385... | collective-permute-start | bytes 393224 | tf_op jit(solution)/shard_map/ppermute | solution.py:18
  17.7 9.1 %collective-permute-start.1 = (bf16[256,256]{1,0:T(8,128)(2,1)S(1)}, bf16[256,256]{1,0:T(8,128)(2,1)S(1)}, u32[]{:S(2)}, u32[]{:S(2)}) collective-permute-start(bf16[256,256]{1,0:T(8,128)(2,1)S(1)} %fusion.2), channel_id=1, source_target_pairs={{0,64},{64,0},{1,65},{65,1},{2,66},{66,2},{3,67},{67,3},{4,68},{68... | collective-permute-start | bytes 393224 | tf_op jit(solution)/shard_map/ppermute | solution.py:18
  27.0 3.0 %collective-permute-start.3 = (bf16[256,256]{1,0:T(8,128)(2,1)S(1)}, bf16[256,256]{1,0:T(8,128)(2,1)S(1)}, u32[]{:S(2)}, u32[]{:S(2)}) collective-permute-start(bf16[256,256]{1,0:T(8,128)(2,1)S(1)} %fusion.4), channel_id=1, source_target_pairs={{0,64},{64,0},{1,65},{65,1},{2,66},{66,2},{3,67},{67,3},{4,68},{68... | collective-permute-start | bytes 393224 | tf_op jit(solution)/shard_map/ppermute | solution.py:18
  30.6 3.1 %collective-permute-start.5 = (bf16[512,256]{1,0:T(8,128)(2,1)S(1)}, bf16[512,256]{1,0:T(8,128)(2,1)S(1)}, u32[]{:S(2)}, u32[]{:S(2)}) collective-permute-start(bf16[512,256]{1,0:T(8,128)(2,1)S(1)} %convolution_convert_fusion.3), channel_id=1, source_target_pairs={{0,128},{128,0},{256,384},{384,256},{1,129},{129,1},{257,385},{385... | collective-permute-start | bytes 786440 | tf_op jit(solution)/shard_map/ppermute | solution.py:18
  33.8 3.6 %all-gather = bf16[1024,256]{1,0:T(8,128)(2,1)S(1)} all-gather(bf16[512,256]{1,0:T(8,128)(2,1)S(1)} %convolution_convert_fusion.2), channel_id=2, replica_groups=mesh['x'=4,'zb'=2,'za'=2,'zl'=2,'y'=8,'c'=2] {'c'}, dimensions={0}, use_global_device_ids=true | all-gather | bytes 786432 | tf_op jit(solution)/shard_map/all_gather | solution.py:116
  37.8 2.3 %collective-permute-start.6 = (bf16[256,256]{1,0:T(8,128)(2,1)S(1)}, bf16[256,256]{1,0:T(8,128)(2,1)S(1)}, u32[]{:S(2)}, u32[]{:S(2)}) collective-permute-start(bf16[256,256]{1,0:T(8,128)(2,1)S(1)} %convolution_convert_fusion.4), channel_id=1, source_target_pairs={{0,32},{32,0},{1,33},{33,1},{2,34},{34,2},{3,35},{35,3},{4,36},{36... | collective-permute-start | bytes 393224 | tf_op jit(solution)/shard_map/ppermute | solution.py:18
  40.5 2.3 %all-gather.2 = bf16[512,256]{1,0:T(8,128)(2,1)S(1)} all-gather(bf16[256,256]{1,0:T(8,128)(2,1)S(1)} %fusion.3), channel_id=4, replica_groups=mesh['x'=4,'zb'=2,'za'=2,'zl'=2,'y'=8,'c'=2] {'c'}, dimensions={0}, use_global_device_ids=true | all-gather | bytes 393216 | tf_op jit(solution)/shard_map/all_gather | solution.py:128
  43.0 2.0 %all-gather.3 = bf16[512,256]{1,0:T(8,128)(2,1)S(1)} all-gather(bf16[256,256]{1,0:T(8,128)(2,1)S(1)} %fusion.5), channel_id=5, replica_groups=mesh['x'=4,'zb'=2,'za'=2,'zl'=2,'y'=8,'c'=2] {'c'}, dimensions={0}, use_global_device_ids=true | all-gather | bytes 393216 | tf_op jit(solution)/shard_map/all_gather | solution.py:128
  45.3 3.0 %all-gather.1 = bf16[1024,256]{1,0:T(8,128)(2,1)S(1)} all-gather(bf16[512,256]{1,0:T(8,128)(2,1)S(1)} %collective-permute-done.5), channel_id=3, replica_groups=mesh['x'=4,'zb'=2,'za'=2,'zl'=2,'y'=8,'c'=2] {'c'}, dimensions={0}, use_global_device_ids=true | all-gather | bytes 786432 | tf_op jit(solution)/shard_map/all_gather | solution.py:124
  48.4 1.2 fusion
  49.7 14.7 %all-to-all-start = ((bf16[64,16,256]{2,1,0:T(8,128)(2,1)}), bf16[64,16,256]{2,1,0:T(8,128)(2,1)}, u32[]{:S(2)}, u32[]{:S(2)}) async-start(bf16[64,16,256]{2,1,0:T(8,128)(2,1)} %bitcast.89), calls=%async_computation | async-start | bytes 1048576 | tf_op jit(solution)/shard_map/all_to_all | solution.py:40
  64.4 1.1 convolution_convert_fusion.8
  65.5 1.1 convolution_convert_fusion.7
  68.0 4.9 %collective-permute-start.7 = (bf16[256,512]{0,1:T(8,128)(2,1)}, bf16[256,512]{0,1:T(8,128)(2,1)}, u32[]{:S(2)}, u32[]{:S(2)}) collective-permute-start(bf16[256,512]{0,1:T(8,128)(2,1)} %pad_maximum_fusion.2), channel_id=1, source_target_pairs={{0,64},{64,0},{1,65},{65,1},{2,66},{66,2},{3,67},{67,3},{4,68},{68... | collective-permute-start | bytes 786440 | tf_op jit(solution)/shard_map/ppermute | solution.py:18
  73.0 7.5 %all-to-all-done = bf16[64,16,256]{2,1,0:T(8,128)(2,1)} async-done(((bf16[64,16,256]{2,1,0:T(8,128)(2,1)}), bf16[64,16,256]{2,1,0:T(8,128)(2,1)}, u32[]{:S(2)}, u32[]{:S(2)}) %all-to-all-start) | async-done | bytes 524320 | tf_op jit(solution)/shard_map/all_to_all | solution.py:40
  80.4 1.1 reduce_sum.24
  82.4 8.6 %all-to-all-start.1 = ((bf16[64,16,256]{2,1,0:T(8,128)(2,1)}), bf16[64,16,256]{2,1,0:T(8,128)(2,1)}, u32[]{:S(2)}, u32[]{:S(2)}) async-start(bf16[64,16,256]{2,1,0:T(8,128)(2,1)} %broadcast_in_dim.9), calls=%async_computation.1 | async-start | bytes 1048576 | tf_op jit(solution)/shard_map/all_to_all | solution.py:46
  91.0 1.2 convolution_convert_fusion
  92.2 1.2 convolution_convert_fusion.1
  93.5 3.8 %all-gather.5 = bf16[512,512]{1,0:T(8,128)(2,1)S(1)} all-gather(bf16[256,512]{1,0:T(8,128)(2,1)S(1)} %pad_maximum_fusion.4), channel_id=7, replica_groups=mesh['x'=4,'zb'=2,'za'=2,'zl'=2,'y'=8,'c'=2] {'c'}, dimensions={0}, use_global_device_ids=true | all-gather | bytes 786432 | tf_op jit(solution)/shard_map/all_gather | solution.py:139
  97.3 2.3 %all-gather.4 = bf16[512,512]{1,0:T(8,128)(2,1)} all-gather(bf16[256,512]{1,0:T(8,128)(2,1)S(1)} %pad_maximum_fusion.3), channel_id=6, replica_groups=mesh['x'=4,'zb'=2,'za'=2,'zl'=2,'y'=8,'c'=2] {'c'}, dimensions={0}, use_global_device_ids=true | all-gather | bytes 786432 | tf_op jit(solution)/shard_map/all_gather | solution.py:139
  99.6 6.9 %all-to-all-done.1 = bf16[64,16,256]{2,1,0:T(8,128)(2,1)} async-done(((bf16[64,16,256]{2,1,0:T(8,128)(2,1)}), bf16[64,16,256]{2,1,0:T(8,128)(2,1)}, u32[]{:S(2)}, u32[]{:S(2)}) %all-to-all-start.1) | async-done | bytes 524320 | tf_op jit(solution)/shard_map/all_to_all | solution.py:46
  106.6 1.6 %subtract_convert_fusion = bf16[2,256,256]{2,1,0:T(8,128)(2,1)S(1)} fusion(bf16[2,256,256]{2,1,0:T(8,128)(2,1)S(1)} %bitcast.94, bf16[1024,256,1]{1,0,2:T(8,128)(2,1)} %bitcast.19, bf16[2,256,512]{2,1,0:T(8,128)(2,1)S(1)} %bitcast.96, bf16[2,256,512]{2,1,0:T(8,128)(2,1)} %bitcast.97), kind=kOutput, calls=%fused_computation.28 | convolution fusion | flops 270925824 | bytes 2097152 | tf_op jit(solution)/shard_map/cij,jr->cir/dot_general | solution.py:22
  108.6 22.0 %all_to_all.20 = bf16[64,16,256]{2,1,0:T(8,128)(2,1)S(1)} all-to-all(bf16[64,16,256]{2,1,0:T(8,128)(2,1)S(1)} %bitcast.90), channel_id=1, replica_groups=mesh['x'=4,'zb'=2,'za'=2,'zl'=2,'y'=8,'c'=2] {'x','zl','y'}, dimensions={0} | all-to-all | bytes 1048576 | tf_op jit(solution)/shard_map/all_to_all | solution.py:40
  130.7 12.8 %all_to_all.21 = bf16[16,16,256]{2,1,0:T(8,128)(2,1)S(1)} all-to-all(bf16[16,16,256]{2,1,0:T(8,128)(2,1)S(1)} %broadcast_in_dim.10), channel_id=1, replica_groups=mesh['x'=4,'zb'=2,'za'=2,'zl'=2,'y'=8,'c'=2] {'zl','y'}, dimensions={0} | all-to-all | bytes 262144 | tf_op jit(solution)/shard_map/all_to_all | solution.py:46
  143.6 6.1 %all_gather.51.total_hbm = bf16[2,256,256]{2,1,0:T(8,128)(2,1)S(1)} all-gather(bf16[1,256,256]{2,1,0:T(8,128)(2,1)S(1)} %bitcast.95), channel_id=1, replica_groups=mesh['x'=4,'zb'=2,'za'=2,'zl'=2,'y'=8,'c'=2] {'c'}, dimensions={0}, use_global_device_ids=true | all-gather | bytes 393216 | tf_op jit(solution)/shard_map/all_gather | solution.py:145
  149.7 2.6 %shard_map.46 = f32[1024,512]{1,0:T(8,128)} custom-call(bf16[1024,512]{1,0:T(8,128)(2,1)S(1)} %bitcast.87, bf16[1024,256]{1,0:T(8,128)(2,1)S(1)} %bitcast.88, bf16[2,256,256]{2,1,0:T(8,128)(2,1)S(1)} %all_gather.51.total_hbm), custom_call_target="tpu_custom_call" | custom-call | tf_op jit(solution)/shard_map/pallas_call | solution.py:81
  (44 shorter events, 5.6 us)
Async XLA Ops:
  0.0 1.0 copy-start
  0.0 12.4 %copy-start.3 = (bf16[4,1,1,2,256,256]{5,4,3,2,1,0:T(8,128)(2,1)S(1)}, bf16[4,1,1,2,256,256]{5,4,3,2,1,0:T(8,128)(2,1)}, u32[]{:S(2)}) copy-start(bf16[4,1,1,2,256,256]{5,4,3,2,1,0:T(8,128)(2,1)} %param.7) | copy-start | bytes 3145732
  2.4 15.1 %collective-permute-start = (bf16[256,256]{1,0:T(8,128)(2,1)S(1)}, bf16[256,256]{1,0:T(8,128)(2,1)S(1)}, u32[]{:S(2)}, u32[]{:S(2)}) collective-permute-start(bf16[256,256]{1,0:T(8,128)(2,1)S(1)} %convolution_convert_fusion.6), channel_id=1, source_target_pairs={{0,32},{32,0},{1,33},{33,1},{2,34},{34,2},{3,35},{35,3},{4,36},{36... | collective-permute-start | bytes 393224 | tf_op jit(solution)/shard_map/ppermute | solution.py:18
  10.5 16.3 %collective-permute-start.2 = (bf16[256,256]{1,0:T(8,128)(2,1)S(1)}, bf16[256,256]{1,0:T(8,128)(2,1)S(1)}, u32[]{:S(2)}, u32[]{:S(2)}) collective-permute-start(bf16[256,256]{1,0:T(8,128)(2,1)S(1)} %convolution_convert_fusion.5), channel_id=1, source_target_pairs={{0,32},{32,0},{1,33},{33,1},{2,34},{34,2},{3,35},{35,3},{4,36},{36... | collective-permute-start | bytes 393224 | tf_op jit(solution)/shard_map/ppermute | solution.py:18
  12.4 17.7 %collective-permute-start.4 = (bf16[256,256]{1,0:T(8,128)(2,1)S(1)}, bf16[256,256]{1,0:T(8,128)(2,1)S(1)}, u32[]{:S(2)}, u32[]{:S(2)}) collective-permute-start(bf16[256,256]{1,0:T(8,128)(2,1)S(1)} %get-tuple-element.32), channel_id=1, source_target_pairs={{0,256},{128,384},{256,0},{384,128},{1,257},{129,385},{257,1},{385... | collective-permute-start | bytes 393224 | tf_op jit(solution)/shard_map/ppermute | solution.py:18
  17.5 19.9 %copy-start.2 = (bf16[1,1024,256]{2,1,0:T(8,128)(2,1)S(1)}, bf16[1,1024,256]{2,1,0:T(8,128)(2,1)}, u32[]{:S(2)}) copy-start(bf16[1,1024,256]{2,1,0:T(8,128)(2,1)} %param.6) | copy-start | bytes 1572868
  17.7 22.6 %collective-permute-start.1 = (bf16[256,256]{1,0:T(8,128)(2,1)S(1)}, bf16[256,256]{1,0:T(8,128)(2,1)S(1)}, u32[]{:S(2)}, u32[]{:S(2)}) collective-permute-start(bf16[256,256]{1,0:T(8,128)(2,1)S(1)} %fusion.2), channel_id=1, source_target_pairs={{0,64},{64,0},{1,65},{65,1},{2,66},{66,2},{3,67},{67,3},{4,68},{68... | collective-permute-start | bytes 393224 | tf_op jit(solution)/shard_map/ppermute | solution.py:18
  27.0 15.8 %collective-permute-start.3 = (bf16[256,256]{1,0:T(8,128)(2,1)S(1)}, bf16[256,256]{1,0:T(8,128)(2,1)S(1)}, u32[]{:S(2)}, u32[]{:S(2)}) collective-permute-start(bf16[256,256]{1,0:T(8,128)(2,1)S(1)} %fusion.4), channel_id=1, source_target_pairs={{0,64},{64,0},{1,65},{65,1},{2,66},{66,2},{3,67},{67,3},{4,68},{68... | collective-permute-start | bytes 393224 | tf_op jit(solution)/shard_map/ppermute | solution.py:18
  30.6 14.6 %collective-permute-start.5 = (bf16[512,256]{1,0:T(8,128)(2,1)S(1)}, bf16[512,256]{1,0:T(8,128)(2,1)S(1)}, u32[]{:S(2)}, u32[]{:S(2)}) collective-permute-start(bf16[512,256]{1,0:T(8,128)(2,1)S(1)} %convolution_convert_fusion.3), channel_id=1, source_target_pairs={{0,128},{128,0},{256,384},{384,256},{1,129},{129,1},{257,385},{385... | collective-permute-start | bytes 786440 | tf_op jit(solution)/shard_map/ppermute | solution.py:18
  37.7 10.5 %copy-start.5 = (bf16[256,256]{1,0:T(8,128)(2,1)}, bf16[256,256]{1,0:T(8,128)(2,1)S(1)}, u32[]{:S(2)}) copy-start(bf16[256,256]{1,0:T(8,128)(2,1)S(1)} %convolution_convert_fusion.4) | copy-start | bytes 393220
  37.8 7.5 %collective-permute-start.6 = (bf16[256,256]{1,0:T(8,128)(2,1)S(1)}, bf16[256,256]{1,0:T(8,128)(2,1)S(1)}, u32[]{:S(2)}, u32[]{:S(2)}) collective-permute-start(bf16[256,256]{1,0:T(8,128)(2,1)S(1)} %convolution_convert_fusion.4), channel_id=1, source_target_pairs={{0,32},{32,0},{1,33},{33,1},{2,34},{34,2},{3,35},{35,3},{4,36},{36... | collective-permute-start | bytes 393224 | tf_op jit(solution)/shard_map/ppermute | solution.py:18
  45.3 3.0 %copy-start.6 = (bf16[256,256]{1,0:T(8,128)(2,1)}, bf16[256,256]{1,0:T(8,128)(2,1)S(1)}, u32[]{:S(2)}) copy-start(bf16[256,256]{1,0:T(8,128)(2,1)S(1)} %collective-permute-done.6) | copy-start | bytes 393220
  49.7 30.8 %all-to-all-start = ((bf16[64,16,256]{2,1,0:T(8,128)(2,1)}), bf16[64,16,256]{2,1,0:T(8,128)(2,1)}, u32[]{:S(2)}, u32[]{:S(2)}) async-start(bf16[64,16,256]{2,1,0:T(8,128)(2,1)} %bitcast.89), calls=%async_computation | async-start | bytes 1048576 | tf_op jit(solution)/shard_map/all_to_all | solution.py:40
  66.7 0.7 copy-start.4
  68.0 24.2 %collective-permute-start.7 = (bf16[256,512]{0,1:T(8,128)(2,1)}, bf16[256,512]{0,1:T(8,128)(2,1)}, u32[]{:S(2)}, u32[]{:S(2)}) collective-permute-start(bf16[256,512]{0,1:T(8,128)(2,1)} %pad_maximum_fusion.2), channel_id=1, source_target_pairs={{0,64},{64,0},{1,65},{65,1},{2,66},{66,2},{3,67},{67,3},{4,68},{68... | collective-permute-start | bytes 786440 | tf_op jit(solution)/shard_map/ppermute | solution.py:18
  82.4 24.1 %all-to-all-start.1 = ((bf16[64,16,256]{2,1,0:T(8,128)(2,1)}), bf16[64,16,256]{2,1,0:T(8,128)(2,1)}, u32[]{:S(2)}, u32[]{:S(2)}) async-start(bf16[64,16,256]{2,1,0:T(8,128)(2,1)} %broadcast_in_dim.9), calls=%async_computation.1 | async-start | bytes 1048576 | tf_op jit(solution)/shard_map/all_to_all | solution.py:46
  108.2 41.5 %copy-start.1 = (bf16[1,1024,512]{2,1,0:T(8,128)(2,1)S(1)}, bf16[1,1024,512]{2,1,0:T(8,128)(2,1)}, u32[]{:S(2)}) copy-start(bf16[1,1024,512]{2,1,0:T(8,128)(2,1)} %param.4) | copy-start | bytes 3145732

commit v8 on v6

--- a/solution.py
+++ b/solution.py
@@ -38,6 +38,12 @@
     spread = mm("cij,cjr->ir", tail, coefficient).astype(BF)
     pieces = spread.reshape(lax.axis_size(GROUP), -1, coefficient.shape[2])
     pieces = lax.all_to_all(pieces, GROUP, 0, 0, tiled=True)
+    return jnp.sum(pieces.astype(F32), axis=0).astype(BF)
+
+
+def add_over(share, axes):
+    pieces = share.reshape(lax.axis_size(axes), -1, share.shape[1])
+    pieces = lax.all_to_all(pieces, axes, 0, 0, tiled=True)
     return jnp.sum(pieces.astype(F32), axis=0).astype(BF)
 
 
@@ -119,18 +125,22 @@
     field = (dot(own[1], field) + dot(other[1], swap(field, "zb", 1))).astype(BF)
     field, came, kept = tie((field, came, kept))
 
-    came = lax.all_gather(came, "c")
+    keep = lax.dynamic_slice_in_dim(field, core * half, half, 1)
+    give = lax.dynamic_slice_in_dim(field, (1 - core) * half, half, 1)
+    both = lax.all_gather(jnp.concatenate([came, give], 0), "c")
+    came = both[:, : 2 * rank]
+    field = jnp.where(lax.broadcasted_iota(jnp.int32, (2, 1, 1), 0) == core, keep, both[:, 2 * rank :])
     tail = in_order([kept[:, :rank], came[:, :rank], kept[:, rank:], came[:, rank:]], "x")
     tail = tie(jnp.concatenate(tail, 1))
 
-    field = lax.all_gather(field, "c")
     field, near = lax.optimization_barrier((field, near))
     chain = jnp.concatenate([dot(own[0], gram).astype(BF), dot(other[0], near).astype(BF)], 1)
-    field = lax.dynamic_slice_in_dim(field, core * half, half, 2)
-    share = add_up(tail, field)
+    share = add_over(mm("cij,cjr->ir", tail, field).astype(BF), "x")
+    share, chain = tie((share, chain))
+    chain_far = swap(chain, "zb", 1)
+    share = add_over(share, LINE)
     totals = hand_out(share, QUAD + LINE).reshape(4 * rank, half)
 
-    chain_far = swap(chain, "zb", 1)
     mine = dot(own[1], chain).astype(BF)
     theirs = dot(other[1], chain_far).astype(BF)
     back = in_order([mine[:, :rank], mine[:, rank:], theirs[:, :rank], theirs[:, rank:]], QUAD)

time: 149 us -> 150 us (level)
  starting transfers between devices: 51 us -> 49.4 us
  waiting for transfers between devices: 21.5 us -> 23.1 us
    all_to_all x1, blocking collectives: 21.4 us -> 25.3 us  [add_up(): pieces = lax.all_to_all(pieces, GROUP, 0, 0, tiled=True)]
    all_to_all x1, starting transfers between devices: 9.52 us -> 7.33 us  [hand_out(): return lax.all_to_all(copies, axes, 0, 0, tiled=True)]
    all_gather x2 -> x1, blocking collectives: 8.66 us -> 6.62 us  [body(): both = lax.all_gather(jnp.concatenate([came, give], 0), 'c')]
    ppermute x6, waiting for transfers between devices: 6.13 us -> 7.96 us  [swap(): return lax.ppermute(block, axis, [(i, i ^ bit) for i in range(size)])]
    all_gather x1, blocking collectives: 6.09 us -> 4.5 us  [body(): return finish(rhs, out_basis, lax.all_gather(total, 'c'))[None]]
    all_to_all x1 -> x2, waiting for transfers between devices: 8.29 us -> 9.15 us  [add_over(): pieces = lax.all_to_all(pieces, axes, 0, 0, tiled=True)]
    all_to_all x1 -> x2, starting transfers between devices: 10.3 us -> 10.9 us  [add_over(): pieces = lax.all_to_all(pieces, axes, 0, 0, tiled=True)]
  transfers between devices with their start and end apart: 8 -> 9, of which waited for: 4 -> 5; matrix products, arithmetic and copies ran while one was open for 5% -> 5% of each run, Pallas kernels for 0% -> 0%
where the time goes in v8:
time: 150 us; the launch traced here: 149 us
  blocking collectives  59.5 us (40%)
  starting transfers between devices  49.4 us (33%)
  waiting for transfers between devices  23.1 us (15%)
  matrix products  11.1 us (7%)
  Pallas kernels  2.62 us (2%)
  local copies, waits for them, and re-layouts  1.95 us (1%)
    ppermute x6, starting transfers between devices, swap(): return lax.ppermute(block, axis, [(i, i ^ bit) for i in range(size)])  31.2 us
    all_to_all x1, blocking collectives, add_up(): pieces = lax.all_to_all(pieces, GROUP, 0, 0, tiled=True)  25.3 us
    all_to_all x1, blocking collectives, hand_out(): return lax.all_to_all(copies, axes, 0, 0, tiled=True)  12.5 us
    all_to_all x2, starting transfers between devices, add_over(): pieces = lax.all_to_all(pieces, axes, 0, 0, tiled=True)  10.9 us
    all_to_all x2, waiting for transfers between devices, add_over(): pieces = lax.all_to_all(pieces, axes, 0, 0, tiled=True)  9.15 us
    ppermute x6, waiting for transfers between devices, swap(): return lax.ppermute(block, axis, [(i, i ^ bit) for i in range(size)])  7.96 us
    all_to_all x1, starting transfers between devices, hand_out(): return lax.all_to_all(copies, axes, 0, 0, tiled=True)  7.33 us
    all_gather x2, blocking collectives, body(): lax.all_gather(jnp.concatenate(back[i:i + 2], 1), 'c')  6.74 us
  transfers between devices with their start and end apart: 9, of which 5 were waited for; matrix products, arithmetic and copies ran while one was open for 5% of the time, Pallas kernels for 0%

profile of v8, /device:TPU:1, one launch (start us, length us, event | category | flops | bytes accessed | tf_op | source)
XLA Modules:
  0.0 149.4 jit_solution(3279582208800792150)
XLA Ops:
  0.0 1.0 copy-done
  1.0 1.7 %convolution_convert_fusion.4 = bf16[256,512]{1,0:T(8,128)(2,1)S(1)} fusion(bf16[1,1024,256]{2,1,0:T(8,128)(2,1)S(1)} %copy-done, bf16[1,1024,512]{2,1,0:T(8,128)(2,1)} %param.4), kind=kOutput, calls=%fused_computation.10 | convolution fusion | flops 268566528 | bytes 1835008 | tf_op jit(solution)/shard_map/lk,lr->kr/dot_general | solution.py:22
  2.7 6.6 %collective-permute-start = (bf16[256,512]{1,0:T(8,128)(2,1)S(1)}, bf16[256,512]{1,0:T(8,128)(2,1)S(1)}, u32[]{:S(2)}, u32[]{:S(2)}) collective-permute-start(bf16[256,512]{1,0:T(8,128)(2,1)S(1)} %convolution_convert_fusion.4), channel_id=1, source_target_pairs={{0,32},{32,0},{1,33},{33,1},{2,34},{34,2},{3,35},{35,3},{4,36},{36... | collective-permute-start | bytes 786440 | tf_op jit(solution)/shard_map/ppermute | solution.py:18
  9.4 4.7 %collective-permute-start.1 = (bf16[256,256]{1,0:T(8,128)(2,1)S(1)}, bf16[256,256]{1,0:T(8,128)(2,1)S(1)}, u32[]{:S(2)}, u32[]{:S(2)}) collective-permute-start(bf16[256,256]{1,0:T(8,128)(2,1)S(1)} %get-tuple-element.36), channel_id=1, source_target_pairs={{0,256},{128,384},{256,0},{384,128},{1,257},{129,385},{257,1},{385... | collective-permute-start | bytes 393224 | tf_op jit(solution)/shard_map/ppermute | solution.py:18
  14.3 5.5 %collective-permute-done = bf16[256,512]{1,0:T(8,128)(2,1)S(1)} collective-permute-done((bf16[256,512]{1,0:T(8,128)(2,1)S(1)}, bf16[256,512]{1,0:T(8,128)(2,1)S(1)}, u32[]{:S(2)}, u32[]{:S(2)}) %collective-permute-start) | collective-permute-done | bytes 262176 | tf_op jit(solution)/shard_map/ppermute | solution.py:18
  20.6 10.0 %collective-permute-start.2 = (bf16[256,512]{1,0:T(8,128)(2,1)S(1)}, bf16[256,512]{1,0:T(8,128)(2,1)S(1)}, u32[]{:S(2)}, u32[]{:S(2)}) collective-permute-start(bf16[256,512]{1,0:T(8,128)(2,1)S(1)} %fusion.2), channel_id=1, source_target_pairs={{0,64},{64,0},{1,65},{65,1},{2,66},{66,2},{3,67},{67,3},{4,68},{68... | collective-permute-start | bytes 786440 | tf_op jit(solution)/shard_map/ppermute | solution.py:18
  30.6 3.1 %collective-permute-start.3 = (bf16[512,256]{1,0:T(8,128)(2,1)S(1)}, bf16[512,256]{1,0:T(8,128)(2,1)S(1)}, u32[]{:S(2)}, u32[]{:S(2)}) collective-permute-start(bf16[512,256]{1,0:T(8,128)(2,1)S(1)} %convolution_convert_fusion.3), channel_id=1, source_target_pairs={{0,128},{128,0},{256,384},{384,256},{1,129},{129,1},{257,385},{385... | collective-permute-start | bytes 786440 | tf_op jit(solution)/shard_map/ppermute | solution.py:18
  33.8 3.8 %all-gather = bf16[1024,256]{1,0:T(8,128)(2,1)S(1)} all-gather(bf16[512,256]{1,0:T(8,128)(2,1)S(1)} %convolution_convert_fusion.2), channel_id=2, replica_groups=mesh['x'=4,'zb'=2,'za'=2,'zl'=2,'y'=8,'c'=2] {'c'}, dimensions={0}, use_global_device_ids=true | all-gather | bytes 786432 | tf_op jit(solution)/shard_map/all_gather | solution.py:120
  37.9 1.9 %collective-permute-start.4 = (bf16[256,256]{1,0:T(8,128)(2,1)S(1)}, bf16[256,256]{1,0:T(8,128)(2,1)S(1)}, u32[]{:S(2)}, u32[]{:S(2)}) collective-permute-start(bf16[256,256]{1,0:T(8,128)(2,1)S(1)} %convolution_convert_fusion.5), channel_id=1, source_target_pairs={{0,32},{32,0},{1,33},{33,1},{2,34},{34,2},{3,35},{35,3},{4,36},{36... | collective-permute-start | bytes 393224 | tf_op jit(solution)/shard_map/ppermute | solution.py:18
  40.4 6.6 %all-gather.1 = bf16[1536,256]{1,0:T(8,128)(2,1)S(1)} all-gather(bf16[768,256]{1,0:T(8,128)(2,1)S(1)} %pad_maximum_fusion.1), channel_id=3, replica_groups=mesh['x'=4,'zb'=2,'za'=2,'zl'=2,'y'=8,'c'=2] {'c'}, dimensions={0}, use_global_device_ids=true | all-gather | bytes 1179648 | tf_op jit(solution)/shard_map/all_gather | solution.py:130
  47.3 2.4 %collective-permute-done.4 = bf16[256,256]{1,0:T(8,128)(2,1)S(1)} collective-permute-done((bf16[256,256]{1,0:T(8,128)(2,1)S(1)}, bf16[256,256]{1,0:T(8,128)(2,1)S(1)}, u32[]{:S(2)}, u32[]{:S(2)}) %collective-permute-start.4) | collective-permute-done | bytes 131104 | tf_op jit(solution)/shard_map/ppermute | solution.py:18
  49.7 1.2 fusion
  50.9 4.0 %all-to-all-start = ((bf16[4,256,256]{2,1,0:T(8,128)(2,1)}), bf16[4,256,256]{2,1,0:T(8,128)(2,1)S(1)}, u32[]{:S(2)}, u32[]{:S(2)}) async-start(bf16[4,256,256]{2,1,0:T(8,128)(2,1)} %bitcast.14), calls=%async_computation | async-start | bytes 1048576 | tf_op jit(solution)/shard_map/all_to_all | solution.py:46
  55.0 1.1 convolution_convert_fusion.7
  56.1 1.1 convolution_convert_fusion.6
  57.3 6.5 %all-to-all-done = bf16[4,256,256]{2,1,0:T(8,128)(2,1)S(1)} async-done(((bf16[4,256,256]{2,1,0:T(8,128)(2,1)}), bf16[4,256,256]{2,1,0:T(8,128)(2,1)S(1)}, u32[]{:S(2)}, u32[]{:S(2)}) %all-to-all-start) | async-done | bytes 524320 | tf_op jit(solution)/shard_map/all_to_all | solution.py:46
  63.7 0.7 reduce_sum.36
  64.5 6.9 %all-to-all-start.1 = ((bf16[16,16,256]{2,1,0:T(8,128)(2,1)}), bf16[16,16,256]{2,1,0:T(8,128)(2,1)S(1)}, u32[]{:S(2)}, u32[]{:S(2)}) async-start(bf16[16,16,256]{2,1,0:T(8,128)(2,1)} %bitcast.17), calls=%async_computation.1 | async-start | bytes 262144 | tf_op jit(solution)/shard_map/all_to_all | solution.py:46
  71.4 4.8 %collective-permute-start.5 = (bf16[256,512]{0,1:T(8,128)(2,1)S(1)}, bf16[256,512]{0,1:T(8,128)(2,1)S(1)}, u32[]{:S(2)}, u32[]{:S(2)}) collective-permute-start(bf16[256,512]{0,1:T(8,128)(2,1)S(1)} %pad_maximum_fusion.3), channel_id=1, source_target_pairs={{0,64},{64,0},{1,65},{65,1},{2,66},{66,2},{3,67},{67,3},{4,68},{68... | collective-permute-start | bytes 786440 | tf_op jit(solution)/shard_map/ppermute | solution.py:18
  76.2 2.7 %all-to-all-done.1 = bf16[16,16,256]{2,1,0:T(8,128)(2,1)S(1)} async-done(((bf16[16,16,256]{2,1,0:T(8,128)(2,1)}), bf16[16,16,256]{2,1,0:T(8,128)(2,1)S(1)}, u32[]{:S(2)}, u32[]{:S(2)}) %all-to-all-start.1) | async-done | bytes 131104 | tf_op jit(solution)/shard_map/all_to_all | solution.py:46
  78.9 0.8 broadcast_in_dim.23
  79.8 7.3 %all-to-all-start.2 = ((bf16[64,16,256]{2,1,0:T(8,128)(2,1)}), bf16[64,16,256]{2,1,0:T(8,128)(2,1)}, u32[]{:S(2)}, u32[]{:S(2)}) async-start(bf16[64,16,256]{2,1,0:T(8,128)(2,1)} %broadcast_in_dim.23), calls=%async_computation.2 | async-start | bytes 1048576 | tf_op jit(solution)/shard_map/all_to_all | solution.py:52
  87.1 1.2 convolution_convert_fusion
  88.3 1.2 convolution_convert_fusion.1
  89.6 4.6 %all-gather.3 = bf16[512,512]{1,0:T(8,128)(2,1)S(1)} all-gather(bf16[256,512]{1,0:T(8,128)(2,1)S(1)} %pad_maximum_fusion.5), channel_id=5, replica_groups=mesh['x'=4,'zb'=2,'za'=2,'zl'=2,'y'=8,'c'=2] {'c'}, dimensions={0}, use_global_device_ids=true | all-gather | bytes 786432 | tf_op jit(solution)/shard_map/all_gather | solution.py:147
  94.2 2.2 %all-gather.2 = bf16[512,512]{1,0:T(8,128)(2,1)S(1)} all-gather(bf16[256,512]{1,0:T(8,128)(2,1)S(1)} %pad_maximum_fusion.4), channel_id=4, replica_groups=mesh['x'=4,'zb'=2,'za'=2,'zl'=2,'y'=8,'c'=2] {'c'}, dimensions={0}, use_global_device_ids=true | all-gather | bytes 786432 | tf_op jit(solution)/shard_map/all_gather | solution.py:147
  96.3 6.0 %all-to-all-done.2 = bf16[64,16,256]{2,1,0:T(8,128)(2,1)} async-done(((bf16[64,16,256]{2,1,0:T(8,128)(2,1)}), bf16[64,16,256]{2,1,0:T(8,128)(2,1)}, u32[]{:S(2)}, u32[]{:S(2)}) %all-to-all-start.2) | async-done | bytes 524320 | tf_op jit(solution)/shard_map/all_to_all | solution.py:52
  102.3 1.5 subtract_convert_fusion
  104.2 25.3 %all_to_all.25 = bf16[64,16,256]{2,1,0:T(8,128)(2,1)S(1)} all-to-all(bf16[64,16,256]{2,1,0:T(8,128)(2,1)S(1)} %bitcast.78), channel_id=1, replica_groups=mesh['x'=4,'zb'=2,'za'=2,'zl'=2,'y'=8,'c'=2] {'x','zl','y'}, dimensions={0} | all-to-all | bytes 1048576 | tf_op jit(solution)/shard_map/all_to_all | solution.py:40
  129.7 12.5 %all_to_all.26 = bf16[16,16,256]{2,1,0:T(8,128)(2,1)S(1)} all-to-all(bf16[16,16,256]{2,1,0:T(8,128)(2,1)S(1)} %broadcast_in_dim.24), channel_id=1, replica_groups=mesh['x'=4,'zb'=2,'za'=2,'zl'=2,'y'=8,'c'=2] {'zl','y'}, dimensions={0} | all-to-all | bytes 262144 | tf_op jit(solution)/shard_map/all_to_all | solution.py:52
  142.2 4.5 %all_gather.35.total_hbm = bf16[2,256,256]{2,1,0:T(8,128)(2,1)S(1)} all-gather(bf16[1,256,256]{2,1,0:T(8,128)(2,1)S(1)} %bitcast.80), channel_id=1, replica_groups=mesh['x'=4,'zb'=2,'za'=2,'zl'=2,'y'=8,'c'=2] {'c'}, dimensions={0}, use_global_device_ids=true | all-gather | bytes 393216 | tf_op jit(solution)/shard_map/all_gather | solution.py:153
  146.7 2.6 %shard_map.46 = f32[1024,512]{1,0:T(8,128)} custom-call(bf16[1024,512]{1,0:T(8,128)(2,1)S(1)} %bitcast.74, bf16[1024,256]{1,0:T(8,128)(2,1)S(1)} %bitcast.75, bf16[2,256,256]{2,1,0:T(8,128)(2,1)S(1)} %all_gather.35.total_hbm), custom_call_target="tpu_custom_call" | custom-call | tf_op jit(solution)/shard_map/pallas_call | solution.py:87
  (33 shorter events, 2.8 us)
Async XLA Ops:
  0.0 1.0 copy-start
  0.0 9.4 %copy-start.3 = (bf16[4,1,1,2,256,256]{5,4,3,2,1,0:T(8,128)(2,1)S(1)}, bf16[4,1,1,2,256,256]{5,4,3,2,1,0:T(8,128)(2,1)}, u32[]{:S(2)}) copy-start(bf16[4,1,1,2,256,256]{5,4,3,2,1,0:T(8,128)(2,1)} %param.7) | copy-start | bytes 3145732
  2.7 17.1 %collective-permute-start = (bf16[256,512]{1,0:T(8,128)(2,1)S(1)}, bf16[256,512]{1,0:T(8,128)(2,1)S(1)}, u32[]{:S(2)}, u32[]{:S(2)}) collective-permute-start(bf16[256,512]{1,0:T(8,128)(2,1)S(1)} %convolution_convert_fusion.4), channel_id=1, source_target_pairs={{0,32},{32,0},{1,33},{33,1},{2,34},{34,2},{3,35},{35,3},{4,36},{36... | collective-permute-start | bytes 786440 | tf_op jit(solution)/shard_map/ppermute | solution.py:18
  9.4 10.7 %collective-permute-start.1 = (bf16[256,256]{1,0:T(8,128)(2,1)S(1)}, bf16[256,256]{1,0:T(8,128)(2,1)S(1)}, u32[]{:S(2)}, u32[]{:S(2)}) collective-permute-start(bf16[256,256]{1,0:T(8,128)(2,1)S(1)} %get-tuple-element.36), channel_id=1, source_target_pairs={{0,256},{128,384},{256,0},{384,128},{1,257},{129,385},{257,1},{385... | collective-permute-start | bytes 393224 | tf_op jit(solution)/shard_map/ppermute | solution.py:18
  14.1 23.4 %copy-start.2 = (bf16[1,1024,256]{2,1,0:T(8,128)(2,1)S(1)}, bf16[1,1024,256]{2,1,0:T(8,128)(2,1)}, u32[]{:S(2)}) copy-start(bf16[1,1024,256]{2,1,0:T(8,128)(2,1)} %param.6) | copy-start | bytes 1572868
  20.6 19.2 %collective-permute-start.2 = (bf16[256,512]{1,0:T(8,128)(2,1)S(1)}, bf16[256,512]{1,0:T(8,128)(2,1)S(1)}, u32[]{:S(2)}, u32[]{:S(2)}) collective-permute-start(bf16[256,512]{1,0:T(8,128)(2,1)S(1)} %fusion.2), channel_id=1, source_target_pairs={{0,64},{64,0},{1,65},{65,1},{2,66},{66,2},{3,67},{67,3},{4,68},{68... | collective-permute-start | bytes 786440 | tf_op jit(solution)/shard_map/ppermute | solution.py:18
  30.6 9.7 %collective-permute-start.3 = (bf16[512,256]{1,0:T(8,128)(2,1)S(1)}, bf16[512,256]{1,0:T(8,128)(2,1)S(1)}, u32[]{:S(2)}, u32[]{:S(2)}) collective-permute-start(bf16[512,256]{1,0:T(8,128)(2,1)S(1)} %convolution_convert_fusion.3), channel_id=1, source_target_pairs={{0,128},{128,0},{256,384},{384,256},{1,129},{129,1},{257,385},{385... | collective-permute-start | bytes 786440 | tf_op jit(solution)/shard_map/ppermute | solution.py:18
  37.9 11.8 %collective-permute-start.4 = (bf16[256,256]{1,0:T(8,128)(2,1)S(1)}, bf16[256,256]{1,0:T(8,128)(2,1)S(1)}, u32[]{:S(2)}, u32[]{:S(2)}) collective-permute-start(bf16[256,256]{1,0:T(8,128)(2,1)S(1)} %convolution_convert_fusion.5), channel_id=1, source_target_pairs={{0,32},{32,0},{1,33},{33,1},{2,34},{34,2},{3,35},{35,3},{4,36},{36... | collective-permute-start | bytes 393224 | tf_op jit(solution)/shard_map/ppermute | solution.py:18
  50.9 12.8 %all-to-all-start = ((bf16[4,256,256]{2,1,0:T(8,128)(2,1)}), bf16[4,256,256]{2,1,0:T(8,128)(2,1)S(1)}, u32[]{:S(2)}, u32[]{:S(2)}) async-start(bf16[4,256,256]{2,1,0:T(8,128)(2,1)} %bitcast.14), calls=%async_computation | async-start | bytes 1048576 | tf_op jit(solution)/shard_map/all_to_all | solution.py:46
  64.5 14.4 %all-to-all-start.1 = ((bf16[16,16,256]{2,1,0:T(8,128)(2,1)}), bf16[16,16,256]{2,1,0:T(8,128)(2,1)S(1)}, u32[]{:S(2)}, u32[]{:S(2)}) async-start(bf16[16,16,256]{2,1,0:T(8,128)(2,1)} %bitcast.17), calls=%async_computation.1 | async-start | bytes 262144 | tf_op jit(solution)/shard_map/all_to_all | solution.py:46
  71.4 16.9 %collective-permute-start.5 = (bf16[256,512]{0,1:T(8,128)(2,1)S(1)}, bf16[256,512]{0,1:T(8,128)(2,1)S(1)}, u32[]{:S(2)}, u32[]{:S(2)}) collective-permute-start(bf16[256,512]{0,1:T(8,128)(2,1)S(1)} %pad_maximum_fusion.3), channel_id=1, source_target_pairs={{0,64},{64,0},{1,65},{65,1},{2,66},{66,2},{3,67},{67,3},{4,68},{68... | collective-permute-start | bytes 786440 | tf_op jit(solution)/shard_map/ppermute | solution.py:18
  79.8 22.5 %all-to-all-start.2 = ((bf16[64,16,256]{2,1,0:T(8,128)(2,1)}), bf16[64,16,256]{2,1,0:T(8,128)(2,1)}, u32[]{:S(2)}, u32[]{:S(2)}) async-start(bf16[64,16,256]{2,1,0:T(8,128)(2,1)} %broadcast_in_dim.23), calls=%async_computation.2 | async-start | bytes 1048576 | tf_op jit(solution)/shard_map/all_to_all | solution.py:52
  103.8 43.0 %copy-start.1 = (bf16[1,1024,512]{2,1,0:T(8,128)(2,1)S(1)}, bf16[1,1024,512]{2,1,0:T(8,128)(2,1)}, u32[]{:S(2)}) copy-start(bf16[1,1024,512]{2,1,0:T(8,128)(2,1)} %param.4) | copy-start | bytes 3145732

commit v9 on v6

--- a/solution.py
+++ b/solution.py
@@ -119,14 +119,17 @@
     field = (dot(own[1], field) + dot(other[1], swap(field, "zb", 1))).astype(BF)
     field, came, kept = tie((field, came, kept))
 
-    came = lax.all_gather(came, "c")
+    keep = lax.dynamic_slice_in_dim(field, core * half, half, 1)
+    give = lax.dynamic_slice_in_dim(field, (1 - core) * half, half, 1)
+    both = lax.all_gather(jnp.concatenate([came, give], 0), "c")
+    came = both[:, : 2 * rank]
+    field = jnp.where(lax.broadcasted_iota(jnp.int32, (2, 1, 1), 0) == core, keep, both[:, 2 * rank :])
     tail = in_order([kept[:, :rank], came[:, :rank], kept[:, rank:], came[:, rank:]], "x")
     tail = tie(jnp.concatenate(tail, 1))
 
-    field = lax.all_gather(field, "c")
     field, near = lax.optimization_barrier((field, near))
     chain = jnp.concatenate([dot(own[0], gram).astype(BF), dot(other[0], near).astype(BF)], 1)
-    field = lax.dynamic_slice_in_dim(field, core * half, half, 2)
+    field = tie(field)
     share = add_up(tail, field)
     totals = hand_out(share, QUAD + LINE).reshape(4 * rank, half)
 

time: 149 us -> 149 us (level)
    all_gather x2 -> x1, blocking collectives: 8.66 us -> 6.62 us  [body(): both = lax.all_gather(jnp.concatenate([came, give], 0), 'c')]
    ppermute x6, waiting for transfers between devices: 6.13 us -> 7.96 us  [swap(): return lax.ppermute(block, axis, [(i, i ^ bit) for i in range(size)])]
where the time goes in v9:
time: 149 us; the launch traced here: 148 us
  blocking collectives  57.9 us (39%)
  starting transfers between devices  49.8 us (33%)
  waiting for transfers between devices  22.9 us (15%)
  matrix products  11.1 us (7%)
  Pallas kernels  2.62 us (2%)
  local copies, waits for them, and re-layouts  1.95 us (1%)
    ppermute x6, starting transfers between devices, swap(): return lax.ppermute(block, axis, [(i, i ^ bit) for i in range(size)])  31.2 us
    all_to_all x1, blocking collectives, add_up(): pieces = lax.all_to_all(pieces, GROUP, 0, 0, tiled=True)  22.4 us
    all_to_all x1, blocking collectives, hand_out(): return lax.all_to_all(copies, axes, 0, 0, tiled=True)  12.9 us
    all_to_all x1, starting transfers between devices, add_up(): pieces = lax.all_to_all(pieces, GROUP, 0, 0, tiled=True)  10.3 us
    all_to_all x1, waiting for transfers between devices, add_up(): pieces = lax.all_to_all(pieces, GROUP, 0, 0, tiled=True)  8.38 us
    all_to_all x1, starting transfers between devices, hand_out(): return lax.all_to_all(copies, axes, 0, 0, tiled=True)  8.31 us
    ppermute x6, waiting for transfers between devices, swap(): return lax.ppermute(block, axis, [(i, i ^ bit) for i in range(size)])  7.96 us
    all_gather x1, blocking collectives, body(): both = lax.all_gather(jnp.concatenate([came, give], 0), 'c')  6.62 us
  transfers between devices with their start and end apart: 8, of which 4 were waited for; matrix products, arithmetic and copies ran while one was open for 5% of the time, Pallas kernels for 0%

profile of v9, /device:TPU:1, one launch (start us, length us, event | category | flops | bytes accessed | tf_op | source)
XLA Modules:
  0.0 147.9 jit_solution(5392186970365276829)
XLA Ops:
  0.0 1.0 copy-done
  1.0 1.7 %convolution_convert_fusion.4 = bf16[256,512]{1,0:T(8,128)(2,1)S(1)} fusion(bf16[1,1024,256]{2,1,0:T(8,128)(2,1)S(1)} %copy-done, bf16[1,1024,512]{2,1,0:T(8,128)(2,1)} %param.4), kind=kOutput, calls=%fused_computation.10 | convolution fusion | flops 268566528 | bytes 1835008 | tf_op jit(solution)/shard_map/lk,lr->kr/dot_general | solution.py:22
  2.7 6.6 %collective-permute-start = (bf16[256,512]{1,0:T(8,128)(2,1)S(1)}, bf16[256,512]{1,0:T(8,128)(2,1)S(1)}, u32[]{:S(2)}, u32[]{:S(2)}) collective-permute-start(bf16[256,512]{1,0:T(8,128)(2,1)S(1)} %convolution_convert_fusion.4), channel_id=1, source_target_pairs={{0,32},{32,0},{1,33},{33,1},{2,34},{34,2},{3,35},{35,3},{4,36},{36... | collective-permute-start | bytes 786440 | tf_op jit(solution)/shard_map/ppermute | solution.py:18
  9.4 4.7 %collective-permute-start.1 = (bf16[256,256]{1,0:T(8,128)(2,1)S(1)}, bf16[256,256]{1,0:T(8,128)(2,1)S(1)}, u32[]{:S(2)}, u32[]{:S(2)}) collective-permute-start(bf16[256,256]{1,0:T(8,128)(2,1)S(1)} %get-tuple-element.32), channel_id=1, source_target_pairs={{0,256},{128,384},{256,0},{384,128},{1,257},{129,385},{257,1},{385... | collective-permute-start | bytes 393224 | tf_op jit(solution)/shard_map/ppermute | solution.py:18
  14.3 5.5 %collective-permute-done = bf16[256,512]{1,0:T(8,128)(2,1)S(1)} collective-permute-done((bf16[256,512]{1,0:T(8,128)(2,1)S(1)}, bf16[256,512]{1,0:T(8,128)(2,1)S(1)}, u32[]{:S(2)}, u32[]{:S(2)}) %collective-permute-start) | collective-permute-done | bytes 262176 | tf_op jit(solution)/shard_map/ppermute | solution.py:18
  20.6 10.0 %collective-permute-start.2 = (bf16[256,512]{1,0:T(8,128)(2,1)S(1)}, bf16[256,512]{1,0:T(8,128)(2,1)S(1)}, u32[]{:S(2)}, u32[]{:S(2)}) collective-permute-start(bf16[256,512]{1,0:T(8,128)(2,1)S(1)} %fusion.2), channel_id=1, source_target_pairs={{0,64},{64,0},{1,65},{65,1},{2,66},{66,2},{3,67},{67,3},{4,68},{68... | collective-permute-start | bytes 786440 | tf_op jit(solution)/shard_map/ppermute | solution.py:18
  30.6 3.1 %collective-permute-start.3 = (bf16[512,256]{1,0:T(8,128)(2,1)S(1)}, bf16[512,256]{1,0:T(8,128)(2,1)S(1)}, u32[]{:S(2)}, u32[]{:S(2)}) collective-permute-start(bf16[512,256]{1,0:T(8,128)(2,1)S(1)} %convolution_convert_fusion.3), channel_id=1, source_target_pairs={{0,128},{128,0},{256,384},{384,256},{1,129},{129,1},{257,385},{385... | collective-permute-start | bytes 786440 | tf_op jit(solution)/shard_map/ppermute | solution.py:18
  33.8 3.8 %all-gather = bf16[1024,256]{1,0:T(8,128)(2,1)S(1)} all-gather(bf16[512,256]{1,0:T(8,128)(2,1)S(1)} %convolution_convert_fusion.2), channel_id=2, replica_groups=mesh['x'=4,'zb'=2,'za'=2,'zl'=2,'y'=8,'c'=2] {'c'}, dimensions={0}, use_global_device_ids=true | all-gather | bytes 786432 | tf_op jit(solution)/shard_map/all_gather | solution.py:114
  37.5 0.3 convolution_convert_fusion.5
  37.9 1.9 %collective-permute-start.4 = (bf16[256,256]{1,0:T(8,128)(2,1)S(1)}, bf16[256,256]{1,0:T(8,128)(2,1)S(1)}, u32[]{:S(2)}, u32[]{:S(2)}) collective-permute-start(bf16[256,256]{1,0:T(8,128)(2,1)S(1)} %convolution_convert_fusion.5), channel_id=1, source_target_pairs={{0,32},{32,0},{1,33},{33,1},{2,34},{34,2},{3,35},{35,3},{4,36},{36... | collective-permute-start | bytes 393224 | tf_op jit(solution)/shard_map/ppermute | solution.py:18
  40.4 6.6 %all-gather.1 = bf16[1536,256]{1,0:T(8,128)(2,1)S(1)} all-gather(bf16[768,256]{1,0:T(8,128)(2,1)S(1)} %pad_maximum_fusion.1), channel_id=3, replica_groups=mesh['x'=4,'zb'=2,'za'=2,'zl'=2,'y'=8,'c'=2] {'c'}, dimensions={0}, use_global_device_ids=true | all-gather | bytes 1179648 | tf_op jit(solution)/shard_map/all_gather | solution.py:124
  47.3 2.4 %collective-permute-done.4 = bf16[256,256]{1,0:T(8,128)(2,1)S(1)} collective-permute-done((bf16[256,256]{1,0:T(8,128)(2,1)S(1)}, bf16[256,256]{1,0:T(8,128)(2,1)S(1)}, u32[]{:S(2)}, u32[]{:S(2)}) %collective-permute-start.4) | collective-permute-done | bytes 131104 | tf_op jit(solution)/shard_map/ppermute | solution.py:18
  49.7 1.2 fusion
  50.9 10.3 %all-to-all-start = ((bf16[64,16,256]{2,1,0:T(8,128)(2,1)}), bf16[64,16,256]{2,1,0:T(8,128)(2,1)S(1)}, u32[]{:S(2)}, u32[]{:S(2)}) async-start(bf16[64,16,256]{2,1,0:T(8,128)(2,1)} %bitcast.16), calls=%async_computation | async-start | bytes 1048576 | tf_op jit(solution)/shard_map/all_to_all | solution.py:40
  61.2 1.1 convolution_convert_fusion.7
  62.4 1.1 convolution_convert_fusion.6
  63.5 0.7 pad_maximum_fusion.3
  64.2 4.8 %collective-permute-start.5 = (bf16[256,512]{0,1:T(8,128)(2,1)}, bf16[256,512]{0,1:T(8,128)(2,1)S(1)}, u32[]{:S(2)}, u32[]{:S(2)}) collective-permute-start(bf16[256,512]{0,1:T(8,128)(2,1)} %pad_maximum_fusion.3), channel_id=1, source_target_pairs={{0,64},{64,0},{1,65},{65,1},{2,66},{66,2},{3,67},{67,3},{4,68},{68... | collective-permute-start | bytes 786440 | tf_op jit(solution)/shard_map/ppermute | solution.py:18
  69.0 8.4 %all-to-all-done = bf16[64,16,256]{2,1,0:T(8,128)(2,1)S(1)} async-done(((bf16[64,16,256]{2,1,0:T(8,128)(2,1)}), bf16[64,16,256]{2,1,0:T(8,128)(2,1)S(1)}, u32[]{:S(2)}, u32[]{:S(2)}) %all-to-all-start) | async-done | bytes 524320 | tf_op jit(solution)/shard_map/all_to_all | solution.py:40
  77.5 0.8 broadcast_in_dim.23
  78.3 8.3 %all-to-all-start.1 = ((bf16[64,16,256]{2,1,0:T(8,128)(2,1)}), bf16[64,16,256]{2,1,0:T(8,128)(2,1)}, u32[]{:S(2)}, u32[]{:S(2)}) async-start(bf16[64,16,256]{2,1,0:T(8,128)(2,1)} %broadcast_in_dim.23), calls=%async_computation.1 | async-start | bytes 1048576 | tf_op jit(solution)/shard_map/all_to_all | solution.py:46
  86.7 1.2 convolution_convert_fusion
  87.9 1.2 convolution_convert_fusion.1
  89.2 4.0 %all-gather.3 = bf16[512,512]{1,0:T(8,128)(2,1)S(1)} all-gather(bf16[256,512]{1,0:T(8,128)(2,1)S(1)} %pad_maximum_fusion.5), channel_id=5, replica_groups=mesh['x'=4,'zb'=2,'za'=2,'zl'=2,'y'=8,'c'=2] {'c'}, dimensions={0}, use_global_device_ids=true | all-gather | bytes 786432 | tf_op jit(solution)/shard_map/all_gather | solution.py:140
  93.1 2.2 %all-gather.2 = bf16[512,512]{1,0:T(8,128)(2,1)S(1)} all-gather(bf16[256,512]{1,0:T(8,128)(2,1)S(1)} %pad_maximum_fusion.4), channel_id=4, replica_groups=mesh['x'=4,'zb'=2,'za'=2,'zl'=2,'y'=8,'c'=2] {'c'}, dimensions={0}, use_global_device_ids=true | all-gather | bytes 786432 | tf_op jit(solution)/shard_map/all_gather | solution.py:140
  95.3 6.6 %all-to-all-done.1 = bf16[64,16,256]{2,1,0:T(8,128)(2,1)} async-done(((bf16[64,16,256]{2,1,0:T(8,128)(2,1)}), bf16[64,16,256]{2,1,0:T(8,128)(2,1)}, u32[]{:S(2)}, u32[]{:S(2)}) %all-to-all-start.1) | async-done | bytes 524320 | tf_op jit(solution)/shard_map/all_to_all | solution.py:46
  101.9 1.5 subtract_convert_fusion
  103.4 0.4 fusion.1
  103.8 22.4 %all_to_all.20 = bf16[64,16,256]{2,1,0:T(8,128)(2,1)S(1)} all-to-all(bf16[64,16,256]{2,1,0:T(8,128)(2,1)S(1)} %bitcast.76), channel_id=1, replica_groups=mesh['x'=4,'zb'=2,'za'=2,'zl'=2,'y'=8,'c'=2] {'x','zl','y'}, dimensions={0} | all-to-all | bytes 1048576 | tf_op jit(solution)/shard_map/all_to_all | solution.py:40
  126.3 12.9 %all_to_all.21 = bf16[16,16,256]{2,1,0:T(8,128)(2,1)S(1)} all-to-all(bf16[16,16,256]{2,1,0:T(8,128)(2,1)S(1)} %broadcast_in_dim.24), channel_id=1, replica_groups=mesh['x'=4,'zb'=2,'za'=2,'zl'=2,'y'=8,'c'=2] {'zl','y'}, dimensions={0} | all-to-all | bytes 262144 | tf_op jit(solution)/shard_map/all_to_all | solution.py:46
  139.3 6.0 %all_gather.35.total_hbm = bf16[2,256,256]{2,1,0:T(8,128)(2,1)S(1)} all-gather(bf16[1,256,256]{2,1,0:T(8,128)(2,1)S(1)} %bitcast.78), channel_id=1, replica_groups=mesh['x'=4,'zb'=2,'za'=2,'zl'=2,'y'=8,'c'=2] {'c'}, dimensions={0}, use_global_device_ids=true | all-gather | bytes 393216 | tf_op jit(solution)/shard_map/all_gather | solution.py:146
  145.3 2.6 %shard_map.46 = f32[1024,512]{1,0:T(8,128)} custom-call(bf16[1024,512]{1,0:T(8,128)(2,1)S(1)} %bitcast.72, bf16[1024,256]{1,0:T(8,128)(2,1)S(1)} %bitcast.73, bf16[2,256,256]{2,1,0:T(8,128)(2,1)S(1)} %all_gather.35.total_hbm), custom_call_target="tpu_custom_call" | custom-call | tf_op jit(solution)/shard_map/pallas_call | solution.py:81
  (30 shorter events, 2.1 us)
Async XLA Ops:
  0.0 1.0 copy-start
  0.0 9.4 %copy-start.3 = (bf16[4,1,1,2,256,256]{5,4,3,2,1,0:T(8,128)(2,1)S(1)}, bf16[4,1,1,2,256,256]{5,4,3,2,1,0:T(8,128)(2,1)}, u32[]{:S(2)}) copy-start(bf16[4,1,1,2,256,256]{5,4,3,2,1,0:T(8,128)(2,1)} %param.7) | copy-start | bytes 3145732
  2.7 17.1 %collective-permute-start = (bf16[256,512]{1,0:T(8,128)(2,1)S(1)}, bf16[256,512]{1,0:T(8,128)(2,1)S(1)}, u32[]{:S(2)}, u32[]{:S(2)}) collective-permute-start(bf16[256,512]{1,0:T(8,128)(2,1)S(1)} %convolution_convert_fusion.4), channel_id=1, source_target_pairs={{0,32},{32,0},{1,33},{33,1},{2,34},{34,2},{3,35},{35,3},{4,36},{36... | collective-permute-start | bytes 786440 | tf_op jit(solution)/shard_map/ppermute | solution.py:18
  9.4 10.7 %collective-permute-start.1 = (bf16[256,256]{1,0:T(8,128)(2,1)S(1)}, bf16[256,256]{1,0:T(8,128)(2,1)S(1)}, u32[]{:S(2)}, u32[]{:S(2)}) collective-permute-start(bf16[256,256]{1,0:T(8,128)(2,1)S(1)} %get-tuple-element.32), channel_id=1, source_target_pairs={{0,256},{128,384},{256,0},{384,128},{1,257},{129,385},{257,1},{385... | collective-permute-start | bytes 393224 | tf_op jit(solution)/shard_map/ppermute | solution.py:18
  14.1 23.4 %copy-start.2 = (bf16[1,1024,256]{2,1,0:T(8,128)(2,1)S(1)}, bf16[1,1024,256]{2,1,0:T(8,128)(2,1)}, u32[]{:S(2)}) copy-start(bf16[1,1024,256]{2,1,0:T(8,128)(2,1)} %param.6) | copy-start | bytes 1572868
  20.6 19.2 %collective-permute-start.2 = (bf16[256,512]{1,0:T(8,128)(2,1)S(1)}, bf16[256,512]{1,0:T(8,128)(2,1)S(1)}, u32[]{:S(2)}, u32[]{:S(2)}) collective-permute-start(bf16[256,512]{1,0:T(8,128)(2,1)S(1)} %fusion.2), channel_id=1, source_target_pairs={{0,64},{64,0},{1,65},{65,1},{2,66},{66,2},{3,67},{67,3},{4,68},{68... | collective-permute-start | bytes 786440 | tf_op jit(solution)/shard_map/ppermute | solution.py:18
  30.6 9.7 %collective-permute-start.3 = (bf16[512,256]{1,0:T(8,128)(2,1)S(1)}, bf16[512,256]{1,0:T(8,128)(2,1)S(1)}, u32[]{:S(2)}, u32[]{:S(2)}) collective-permute-start(bf16[512,256]{1,0:T(8,128)(2,1)S(1)} %convolution_convert_fusion.3), channel_id=1, source_target_pairs={{0,128},{128,0},{256,384},{384,256},{1,129},{129,1},{257,385},{385... | collective-permute-start | bytes 786440 | tf_op jit(solution)/shard_map/ppermute | solution.py:18
  37.9 11.8 %collective-permute-start.4 = (bf16[256,256]{1,0:T(8,128)(2,1)S(1)}, bf16[256,256]{1,0:T(8,128)(2,1)S(1)}, u32[]{:S(2)}, u32[]{:S(2)}) collective-permute-start(bf16[256,256]{1,0:T(8,128)(2,1)S(1)} %convolution_convert_fusion.5), channel_id=1, source_target_pairs={{0,32},{32,0},{1,33},{33,1},{2,34},{34,2},{3,35},{35,3},{4,36},{36... | collective-permute-start | bytes 393224 | tf_op jit(solution)/shard_map/ppermute | solution.py:18
  50.9 26.5 %all-to-all-start = ((bf16[64,16,256]{2,1,0:T(8,128)(2,1)}), bf16[64,16,256]{2,1,0:T(8,128)(2,1)S(1)}, u32[]{:S(2)}, u32[]{:S(2)}) async-start(bf16[64,16,256]{2,1,0:T(8,128)(2,1)} %bitcast.16), calls=%async_computation | async-start | bytes 1048576 | tf_op jit(solution)/shard_map/all_to_all | solution.py:40
  64.2 23.6 %collective-permute-start.5 = (bf16[256,512]{0,1:T(8,128)(2,1)}, bf16[256,512]{0,1:T(8,128)(2,1)S(1)}, u32[]{:S(2)}, u32[]{:S(2)}) collective-permute-start(bf16[256,512]{0,1:T(8,128)(2,1)} %pad_maximum_fusion.3), channel_id=1, source_target_pairs={{0,64},{64,0},{1,65},{65,1},{2,66},{66,2},{3,67},{67,3},{4,68},{68... | collective-permute-start | bytes 786440 | tf_op jit(solution)/shard_map/ppermute | solution.py:18
  78.3 23.6 %all-to-all-start.1 = ((bf16[64,16,256]{2,1,0:T(8,128)(2,1)}), bf16[64,16,256]{2,1,0:T(8,128)(2,1)}, u32[]{:S(2)}, u32[]{:S(2)}) async-start(bf16[64,16,256]{2,1,0:T(8,128)(2,1)} %broadcast_in_dim.23), calls=%async_computation.1 | async-start | bytes 1048576 | tf_op jit(solution)/shard_map/all_to_all | solution.py:46
  103.4 41.9 %copy-start.1 = (bf16[1,1024,512]{2,1,0:T(8,128)(2,1)S(1)}, bf16[1,1024,512]{2,1,0:T(8,128)(2,1)}, u32[]{:S(2)}) copy-start(bf16[1,1024,512]{2,1,0:T(8,128)(2,1)} %param.4) | copy-start | bytes 3145732

commit v10 on v9

--- a/solution.py
+++ b/solution.py
@@ -34,9 +34,8 @@
     return blocks
 
 
-def add_up(tail, coefficient):
-    spread = mm("cij,cjr->ir", tail, coefficient).astype(BF)
-    pieces = spread.reshape(lax.axis_size(GROUP), -1, coefficient.shape[2])
+def add_up(spread):
+    pieces = spread.reshape(lax.axis_size(GROUP), -1, spread.shape[1])
     pieces = lax.all_to_all(pieces, GROUP, 0, 0, tiled=True)
     return jnp.sum(pieces.astype(F32), axis=0).astype(BF)
 
@@ -130,7 +129,8 @@
     field, near = lax.optimization_barrier((field, near))
     chain = jnp.concatenate([dot(own[0], gram).astype(BF), dot(other[0], near).astype(BF)], 1)
     field = tie(field)
-    share = add_up(tail, field)
+    spread = mm("cij,cjr->ir", tail, field).astype(BF)
+    share = add_up(spread)
     totals = hand_out(share, QUAD + LINE).reshape(4 * rank, half)
 
     chain_far = swap(chain, "zb", 1)
@@ -140,8 +140,9 @@
     back = [lax.all_gather(jnp.concatenate(back[i : i + 2], 1), "c") for i in (0, 2)]
     back = jnp.concatenate(back, 2)
 
-    field = (field.astype(F32) - mm("cij,jr->cir", back, totals)).astype(BF)
-    share = add_up(tail, lax.optimization_barrier(field))
+    whole, spread = tie((mm("cij,cjk->ik", tail, back).astype(BF), spread))
+    spread = (spread.astype(F32) - dot(whole, totals)).astype(BF)
+    share = add_up(spread)
     total = hand_out(share, LINE).reshape(rank, half)
     return finish(rhs, out_basis, lax.all_gather(total, "c"))[None]
 

time: 149 us -> 162 us (1.087)
  waiting for transfers between devices: 22.9 us -> 30.2 us
  starting transfers between devices: 49.8 us -> 53.2 us
  matrix products: 11.1 us -> 14.2 us
    ppermute x6, waiting for transfers between devices: 7.96 us -> 20.8 us  [swap(): return lax.ppermute(block, axis, [(i, i ^ bit) for i in range(size)])]
    all_to_all x1, waiting for transfers between devices: 8.38 us -> 0.01 us  [add_up(): pieces = lax.all_to_all(pieces, GROUP, 0, 0, tiled=True)]
    all_to_all x1, starting transfers between devices: 8.31 us -> 11.8 us  [hand_out(): return lax.all_to_all(copies, axes, 0, 0, tiled=True)]
    all_to_all x1, waiting for transfers between devices: 6.6 us -> 9.32 us  [hand_out(): return lax.all_to_all(copies, axes, 0, 0, tiled=True)]
    dot_general x10 -> x11, matrix products: 5.95 us -> 8.33 us  [dot(): return jnp.dot(a, b, preferred_element_type=F32)]
    dot_general x5 -> x4, matrix products: 5.16 us -> 5.82 us  [mm(): return jnp.einsum(spec, a, b, preferred_element_type=F32)]
  transfers between devices with their start and end apart: 8 -> 8, of which waited for: 4 -> 4; matrix products, arithmetic and copies ran while one was open for 5% -> 6% of each run, Pallas kernels for 0% -> 0%
where the time goes in v10:
time: 162 us; the launch traced here: 161 us
  blocking collectives  57.5 us (35%)
  starting transfers between devices  53.2 us (33%)
  waiting for transfers between devices  30.2 us (19%)
  matrix products  14.2 us (9%)
  Pallas kernels  2.63 us (2%)
  local copies, waits for them, and re-layouts  1.95 us (1%)
    ppermute x6, starting transfers between devices, swap(): return lax.ppermute(block, axis, [(i, i ^ bit) for i in range(size)])  31.2 us
    all_to_all x1, blocking collectives, add_up(): pieces = lax.all_to_all(pieces, GROUP, 0, 0, tiled=True)  23.3 us
    ppermute x6, waiting for transfers between devices, swap(): return lax.ppermute(block, axis, [(i, i ^ bit) for i in range(size)])  20.8 us
    all_to_all x1, blocking collectives, hand_out(): return lax.all_to_all(copies, axes, 0, 0, tiled=True)  13.2 us
    all_to_all x1, starting transfers between devices, hand_out(): return lax.all_to_all(copies, axes, 0, 0, tiled=True)  11.8 us
    all_to_all x1, starting transfers between devices, add_up(): pieces = lax.all_to_all(pieces, GROUP, 0, 0, tiled=True)  10.3 us
    all_to_all x1, waiting for transfers between devices, hand_out(): return lax.all_to_all(copies, axes, 0, 0, tiled=True)  9.32 us
    dot_general x11, matrix products, dot(): return jnp.dot(a, b, preferred_element_type=F32)  8.33 us
  transfers between devices with their start and end apart: 8, of which 4 were waited for; matrix products, arithmetic and copies ran while one was open for 6% of the time, Pallas kernels for 0%

profile of v10, /device:TPU:1, one launch (start us, length us, event | category | flops | bytes accessed | tf_op | source)
XLA Modules:
  0.0 161.2 jit_solution(3338038387681338080)
XLA Ops:
  0.0 1.0 copy-done
  1.0 1.7 %convolution_convert_fusion.4 = bf16[256,512]{1,0:T(8,128)(2,1)S(1)} fusion(bf16[1,1024,256]{2,1,0:T(8,128)(2,1)S(1)} %copy-done, bf16[1,1024,512]{2,1,0:T(8,128)(2,1)} %param.4), kind=kOutput, calls=%fused_computation.11 | convolution fusion | flops 268566528 | bytes 1835008 | tf_op jit(solution)/shard_map/lk,lr->kr/dot_general | solution.py:22
  2.7 6.6 %collective-permute-start = (bf16[256,512]{1,0:T(8,128)(2,1)S(1)}, bf16[256,512]{1,0:T(8,128)(2,1)S(1)}, u32[]{:S(2)}, u32[]{:S(2)}) collective-permute-start(bf16[256,512]{1,0:T(8,128)(2,1)S(1)} %convolution_convert_fusion.4), channel_id=1, source_target_pairs={{0,32},{32,0},{1,33},{33,1},{2,34},{34,2},{3,35},{35,3},{4,36},{36... | collective-permute-start | bytes 786440 | tf_op jit(solution)/shard_map/ppermute | solution.py:18
  9.4 4.7 %collective-permute-start.1 = (bf16[256,256]{1,0:T(8,128)(2,1)S(1)}, bf16[256,256]{1,0:T(8,128)(2,1)S(1)}, u32[]{:S(2)}, u32[]{:S(2)}) collective-permute-start(bf16[256,256]{1,0:T(8,128)(2,1)S(1)} %get-tuple-element.36), channel_id=1, source_target_pairs={{0,256},{128,384},{256,0},{384,128},{1,257},{129,385},{257,1},{385... | collective-permute-start | bytes 393224 | tf_op jit(solution)/shard_map/ppermute | solution.py:18
  14.3 5.5 %collective-permute-done = bf16[256,512]{1,0:T(8,128)(2,1)S(1)} collective-permute-done((bf16[256,512]{1,0:T(8,128)(2,1)S(1)}, bf16[256,512]{1,0:T(8,128)(2,1)S(1)}, u32[]{:S(2)}, u32[]{:S(2)}) %collective-permute-start) | collective-permute-done | bytes 262176 | tf_op jit(solution)/shard_map/ppermute | solution.py:18
  20.6 10.0 %collective-permute-start.2 = (bf16[256,512]{1,0:T(8,128)(2,1)S(1)}, bf16[256,512]{1,0:T(8,128)(2,1)S(1)}, u32[]{:S(2)}, u32[]{:S(2)}) collective-permute-start(bf16[256,512]{1,0:T(8,128)(2,1)S(1)} %fusion.2), channel_id=1, source_target_pairs={{0,64},{64,0},{1,65},{65,1},{2,66},{66,2},{3,67},{67,3},{4,68},{68... | collective-permute-start | bytes 786440 | tf_op jit(solution)/shard_map/ppermute | solution.py:18
  30.6 3.1 %collective-permute-start.3 = (bf16[512,256]{1,0:T(8,128)(2,1)S(1)}, bf16[512,256]{1,0:T(8,128)(2,1)S(1)}, u32[]{:S(2)}, u32[]{:S(2)}) collective-permute-start(bf16[512,256]{1,0:T(8,128)(2,1)S(1)} %convolution_convert_fusion.3), channel_id=1, source_target_pairs={{0,128},{128,0},{256,384},{384,256},{1,129},{129,1},{257,385},{385... | collective-permute-start | bytes 786440 | tf_op jit(solution)/shard_map/ppermute | solution.py:18
  33.7 3.8 %all-gather = bf16[1024,256]{1,0:T(8,128)(2,1)S(1)} all-gather(bf16[512,256]{1,0:T(8,128)(2,1)S(1)} %convolution_convert_fusion.2), channel_id=2, replica_groups=mesh['x'=4,'zb'=2,'za'=2,'zl'=2,'y'=8,'c'=2] {'c'}, dimensions={0}, use_global_device_ids=true | all-gather | bytes 786432 | tf_op jit(solution)/shard_map/all_gather | solution.py:113
  37.5 0.3 convolution_convert_fusion.5
  37.9 1.9 %collective-permute-start.4 = (bf16[256,256]{1,0:T(8,128)(2,1)S(1)}, bf16[256,256]{1,0:T(8,128)(2,1)S(1)}, u32[]{:S(2)}, u32[]{:S(2)}) collective-permute-start(bf16[256,256]{1,0:T(8,128)(2,1)S(1)} %convolution_convert_fusion.5), channel_id=1, source_target_pairs={{0,32},{32,0},{1,33},{33,1},{2,34},{34,2},{3,35},{35,3},{4,36},{36... | collective-permute-start | bytes 393224 | tf_op jit(solution)/shard_map/ppermute | solution.py:18
  40.4 6.7 %all-gather.1 = bf16[1536,256]{1,0:T(8,128)(2,1)S(1)} all-gather(bf16[768,256]{1,0:T(8,128)(2,1)S(1)} %pad_maximum_fusion.1), channel_id=3, replica_groups=mesh['x'=4,'zb'=2,'za'=2,'zl'=2,'y'=8,'c'=2] {'c'}, dimensions={0}, use_global_device_ids=true | all-gather | bytes 1179648 | tf_op jit(solution)/shard_map/all_gather | solution.py:123
  47.3 2.4 %collective-permute-done.4 = bf16[256,256]{1,0:T(8,128)(2,1)S(1)} collective-permute-done((bf16[256,256]{1,0:T(8,128)(2,1)S(1)}, bf16[256,256]{1,0:T(8,128)(2,1)S(1)}, u32[]{:S(2)}, u32[]{:S(2)}) %collective-permute-start.4) | collective-permute-done | bytes 131104 | tf_op jit(solution)/shard_map/ppermute | solution.py:18
  49.7 1.2 fusion
  50.9 10.3 %all-to-all-start = ((bf16[64,16,256]{2,1,0:T(8,128)(2,1)}), bf16[64,16,256]{2,1,0:T(8,128)(2,1)S(1)}, u32[]{:S(2)}, u32[]{:S(2)}) async-start(bf16[64,16,256]{2,1,0:T(8,128)(2,1)} %bitcast.17), calls=%async_computation | async-start | bytes 1048576 | tf_op jit(solution)/shard_map/all_to_all | solution.py:39
  61.2 1.1 convolution_convert_fusion.7
  62.4 1.1 convolution_convert_fusion.6
  63.5 0.7 pad_maximum_fusion.3
  64.2 4.8 %collective-permute-start.5 = (bf16[256,512]{0,1:T(8,128)(2,1)}, bf16[256,512]{0,1:T(8,128)(2,1)S(1)}, u32[]{:S(2)}, u32[]{:S(2)}) collective-permute-start(bf16[256,512]{0,1:T(8,128)(2,1)} %pad_maximum_fusion.3), channel_id=1, source_target_pairs={{0,64},{64,0},{1,65},{65,1},{2,66},{66,2},{3,67},{67,3},{4,68},{68... | collective-permute-start | bytes 786440 | tf_op jit(solution)/shard_map/ppermute | solution.py:18
  69.1 1.2 convolution_convert_fusion
  70.2 12.9 %collective-permute-done.5 = bf16[256,512]{0,1:T(8,128)(2,1)S(1)} collective-permute-done((bf16[256,512]{0,1:T(8,128)(2,1)}, bf16[256,512]{0,1:T(8,128)(2,1)S(1)}, u32[]{:S(2)}, u32[]{:S(2)}) %collective-permute-start.5) | collective-permute-done | bytes 262176 | tf_op jit(solution)/shard_map/ppermute | solution.py:18
  83.2 1.2 convolution_convert_fusion.1
  84.5 0.8 broadcast_in_dim.23
  85.3 11.8 %all-to-all-start.1 = ((bf16[64,16,256]{2,1,0:T(8,128)(2,1)}), bf16[64,16,256]{2,1,0:T(8,128)(2,1)S(1)}, u32[]{:S(2)}, u32[]{:S(2)}) async-start(bf16[64,16,256]{2,1,0:T(8,128)(2,1)} %broadcast_in_dim.23), calls=%async_computation.1 | async-start | bytes 1048576 | tf_op jit(solution)/shard_map/all_to_all | solution.py:45
  97.2 2.9 %all-gather.3 = bf16[512,512]{1,0:T(8,128)(2,1)S(1)} all-gather(bf16[256,512]{1,0:T(8,128)(2,1)S(1)} %pad_maximum_fusion.5), channel_id=5, replica_groups=mesh['x'=4,'zb'=2,'za'=2,'zl'=2,'y'=8,'c'=2] {'c'}, dimensions={0}, use_global_device_ids=true | all-gather | bytes 786432 | tf_op jit(solution)/shard_map/all_gather | solution.py:140
  100.1 2.2 %all-gather.2 = bf16[512,512]{1,0:T(8,128)(2,1)S(1)} all-gather(bf16[256,512]{1,0:T(8,128)(2,1)S(1)} %pad_maximum_fusion.4), channel_id=4, replica_groups=mesh['x'=4,'zb'=2,'za'=2,'zl'=2,'y'=8,'c'=2] {'c'}, dimensions={0}, use_global_device_ids=true | all-gather | bytes 786432 | tf_op jit(solution)/shard_map/all_gather | solution.py:140
  102.3 2.6 %bitcast_convert_fusion = bf16[1024,1024]{1,0:T(8,128)(2,1)} fusion(bf16[2,1024,256]{2,1,0:T(8,128)(2,1)S(1)} %pad_maximum_fusion, bf16[2,256,512]{2,1,0:T(8,128)(2,1)S(1)} %bitcast.74, bf16[2,256,512]{2,1,0:T(8,128)(2,1)S(1)} %bitcast.75), kind=kOutput, calls=%fused_computation | convolution fusion | flops 1076887552 | bytes 4194304 | tf_op jit(solution)/shard_map/cij,cjk->ik/dot_general | solution.py:22
  104.9 9.3 %all-to-all-done.1 = bf16[64,16,256]{2,1,0:T(8,128)(2,1)S(1)} async-done(((bf16[64,16,256]{2,1,0:T(8,128)(2,1)}), bf16[64,16,256]{2,1,0:T(8,128)(2,1)S(1)}, u32[]{:S(2)}, u32[]{:S(2)}) %all-to-all-start.1) | async-done | bytes 524320 | tf_op jit(solution)/shard_map/all_to_all | solution.py:45
  114.2 2.4 %fusion.1 = bf16[1024,256]{1,0:T(8,128)(2,1)S(1)} fusion(bf16[1024,1024]{1,0:T(8,128)(2,1)} %bitcast_convert_fusion, bf16[1024,256]{1,0:T(8,128)(2,1)S(1)} %bitcast.76, bf16[1024,256]{1,0:T(8,128)(2,1)} %fusion), kind=kOutput, calls=%fused_computation.4 | convolution fusion | flops 537657344 | bytes 3670016 | tf_op jit(solution)/shard_map/dot_general | solution.py:26
  116.6 23.3 %all_to_all.20 = bf16[64,16,256]{2,1,0:T(8,128)(2,1)S(1)} all-to-all(bf16[64,16,256]{2,1,0:T(8,128)(2,1)S(1)} %bitcast.77), channel_id=1, replica_groups=mesh['x'=4,'zb'=2,'za'=2,'zl'=2,'y'=8,'c'=2] {'x','zl','y'}, dimensions={0} | all-to-all | bytes 1048576 | tf_op jit(solution)/shard_map/all_to_all | solution.py:39
  140.0 13.2 %all_to_all.21 = bf16[16,16,256]{2,1,0:T(8,128)(2,1)S(1)} all-to-all(bf16[16,16,256]{2,1,0:T(8,128)(2,1)S(1)} %broadcast_in_dim.24), channel_id=1, replica_groups=mesh['x'=4,'zb'=2,'za'=2,'zl'=2,'y'=8,'c'=2] {'zl','y'}, dimensions={0} | all-to-all | bytes 262144 | tf_op jit(solution)/shard_map/all_to_all | solution.py:45
  153.2 5.4 %all_gather.35.total_hbm = bf16[2,256,256]{2,1,0:T(8,128)(2,1)S(1)} all-gather(bf16[1,256,256]{2,1,0:T(8,128)(2,1)S(1)} %bitcast.73), channel_id=1, replica_groups=mesh['x'=4,'zb'=2,'za'=2,'zl'=2,'y'=8,'c'=2] {'c'}, dimensions={0}, use_global_device_ids=true | all-gather | bytes 393216 | tf_op jit(solution)/shard_map/all_gather | solution.py:147
  158.6 2.6 %shard_map.46 = f32[1024,512]{1,0:T(8,128)} custom-call(bf16[1024,512]{1,0:T(8,128)(2,1)S(1)} %bitcast.68, bf16[1024,256]{1,0:T(8,128)(2,1)S(1)} %bitcast.69, bf16[2,256,256]{2,1,0:T(8,128)(2,1)S(1)} %all_gather.35.total_hbm), custom_call_target="tpu_custom_call" | custom-call | tf_op jit(solution)/shard_map/pallas_call | solution.py:80
  (30 shorter events, 2.1 us)
Async XLA Ops:
  0.0 1.0 copy-start
  0.0 9.4 %copy-start.3 = (bf16[4,1,1,2,256,256]{5,4,3,2,1,0:T(8,128)(2,1)S(1)}, bf16[4,1,1,2,256,256]{5,4,3,2,1,0:T(8,128)(2,1)}, u32[]{:S(2)}) copy-start(bf16[4,1,1,2,256,256]{5,4,3,2,1,0:T(8,128)(2,1)} %param.7) | copy-start | bytes 3145732
  2.7 17.1 %collective-permute-start = (bf16[256,512]{1,0:T(8,128)(2,1)S(1)}, bf16[256,512]{1,0:T(8,128)(2,1)S(1)}, u32[]{:S(2)}, u32[]{:S(2)}) collective-permute-start(bf16[256,512]{1,0:T(8,128)(2,1)S(1)} %convolution_convert_fusion.4), channel_id=1, source_target_pairs={{0,32},{32,0},{1,33},{33,1},{2,34},{34,2},{3,35},{35,3},{4,36},{36... | collective-permute-start | bytes 786440 | tf_op jit(solution)/shard_map/ppermute | solution.py:18
  9.4 10.7 %collective-permute-start.1 = (bf16[256,256]{1,0:T(8,128)(2,1)S(1)}, bf16[256,256]{1,0:T(8,128)(2,1)S(1)}, u32[]{:S(2)}, u32[]{:S(2)}) collective-permute-start(bf16[256,256]{1,0:T(8,128)(2,1)S(1)} %get-tuple-element.36), channel_id=1, source_target_pairs={{0,256},{128,384},{256,0},{384,128},{1,257},{129,385},{257,1},{385... | collective-permute-start | bytes 393224 | tf_op jit(solution)/shard_map/ppermute | solution.py:18
  14.1 23.4 %copy-start.2 = (bf16[1,1024,256]{2,1,0:T(8,128)(2,1)S(1)}, bf16[1,1024,256]{2,1,0:T(8,128)(2,1)}, u32[]{:S(2)}) copy-start(bf16[1,1024,256]{2,1,0:T(8,128)(2,1)} %param.6) | copy-start | bytes 1572868
  20.6 19.2 %collective-permute-start.2 = (bf16[256,512]{1,0:T(8,128)(2,1)S(1)}, bf16[256,512]{1,0:T(8,128)(2,1)S(1)}, u32[]{:S(2)}, u32[]{:S(2)}) collective-permute-start(bf16[256,512]{1,0:T(8,128)(2,1)S(1)} %fusion.2), channel_id=1, source_target_pairs={{0,64},{64,0},{1,65},{65,1},{2,66},{66,2},{3,67},{67,3},{4,68},{68... | collective-permute-start | bytes 786440 | tf_op jit(solution)/shard_map/ppermute | solution.py:18
  30.6 9.7 %collective-permute-start.3 = (bf16[512,256]{1,0:T(8,128)(2,1)S(1)}, bf16[512,256]{1,0:T(8,128)(2,1)S(1)}, u32[]{:S(2)}, u32[]{:S(2)}) collective-permute-start(bf16[512,256]{1,0:T(8,128)(2,1)S(1)} %convolution_convert_fusion.3), channel_id=1, source_target_pairs={{0,128},{128,0},{256,384},{384,256},{1,129},{129,1},{257,385},{385... | collective-permute-start | bytes 786440 | tf_op jit(solution)/shard_map/ppermute | solution.py:18
  37.9 11.8 %collective-permute-start.4 = (bf16[256,256]{1,0:T(8,128)(2,1)S(1)}, bf16[256,256]{1,0:T(8,128)(2,1)S(1)}, u32[]{:S(2)}, u32[]{:S(2)}) collective-permute-start(bf16[256,256]{1,0:T(8,128)(2,1)S(1)} %convolution_convert_fusion.5), channel_id=1, source_target_pairs={{0,32},{32,0},{1,33},{33,1},{2,34},{34,2},{3,35},{35,3},{4,36},{36... | collective-permute-start | bytes 393224 | tf_op jit(solution)/shard_map/ppermute | solution.py:18
  50.9 33.4 %all-to-all-start = ((bf16[64,16,256]{2,1,0:T(8,128)(2,1)}), bf16[64,16,256]{2,1,0:T(8,128)(2,1)S(1)}, u32[]{:S(2)}, u32[]{:S(2)}) async-start(bf16[64,16,256]{2,1,0:T(8,128)(2,1)} %bitcast.17), calls=%async_computation | async-start | bytes 1048576 | tf_op jit(solution)/shard_map/all_to_all | solution.py:39
  64.2 18.9 %collective-permute-start.5 = (bf16[256,512]{0,1:T(8,128)(2,1)}, bf16[256,512]{0,1:T(8,128)(2,1)S(1)}, u32[]{:S(2)}, u32[]{:S(2)}) collective-permute-start(bf16[256,512]{0,1:T(8,128)(2,1)} %pad_maximum_fusion.3), channel_id=1, source_target_pairs={{0,64},{64,0},{1,65},{65,1},{2,66},{66,2},{3,67},{67,3},{4,68},{68... | collective-permute-start | bytes 786440 | tf_op jit(solution)/shard_map/ppermute | solution.py:18
  85.3 28.9 %all-to-all-start.1 = ((bf16[64,16,256]{2,1,0:T(8,128)(2,1)}), bf16[64,16,256]{2,1,0:T(8,128)(2,1)S(1)}, u32[]{:S(2)}, u32[]{:S(2)}) async-start(bf16[64,16,256]{2,1,0:T(8,128)(2,1)} %broadcast_in_dim.23), calls=%async_computation.1 | async-start | bytes 1048576 | tf_op jit(solution)/shard_map/all_to_all | solution.py:45
  116.6 42.0 %copy-start.1 = (bf16[1,1024,512]{2,1,0:T(8,128)(2,1)S(1)}, bf16[1,1024,512]{2,1,0:T(8,128)(2,1)}, u32[]{:S(2)}) copy-start(bf16[1,1024,512]{2,1,0:T(8,128)(2,1)} %param.4) | copy-start | bytes 3145732

commit v11 on v8

--- a/solution.py
+++ b/solution.py
@@ -136,9 +136,8 @@
     field, near = lax.optimization_barrier((field, near))
     chain = jnp.concatenate([dot(own[0], gram).astype(BF), dot(other[0], near).astype(BF)], 1)
     share = add_over(mm("cij,cjr->ir", tail, field).astype(BF), "x")
-    share, chain = tie((share, chain))
     chain_far = swap(chain, "zb", 1)
-    share = add_over(share, LINE)
+    share, chain_far = tie((add_over(share, LINE), chain_far))
     totals = hand_out(share, QUAD + LINE).reshape(4 * rank, half)
 
     mine = dot(own[1], chain).astype(BF)

time: 150 us -> 154 us (1.027)
  waiting for transfers between devices: 23.1 us -> 26 us
  starting transfers between devices: 49.4 us -> 52 us
  blocking collectives: 59.5 us -> 57.4 us
    all_to_all x1, waiting for transfers between devices: 5.98 us -> 9.55 us  [hand_out(): return lax.all_to_all(copies, axes, 0, 0, tiled=True)]
    all_to_all x1, starting transfers between devices: 7.33 us -> 9.94 us  [hand_out(): return lax.all_to_all(copies, axes, 0, 0, tiled=True)]
    all_to_all x1, blocking collectives: 25.3 us -> 23.4 us  [add_up(): pieces = lax.all_to_all(pieces, GROUP, 0, 0, tiled=True)]
    all_gather x2, blocking collectives: 6.74 us -> 5.04 us  [body(): lax.all_gather(jnp.concatenate(back[i:i + 2], 1), 'c')]
where the time goes in v11:
time: 154 us; the launch traced here: 153 us
  blocking collectives  57.4 us (37%)
  starting transfers between devices  52 us (34%)
  waiting for transfers between devices  26 us (17%)
  matrix products  11.1 us (7%)
  Pallas kernels  2.63 us (2%)
  other arithmetic  2.02 us (1%)
  local copies, waits for them, and re-layouts  1.94 us (1%)
    ppermute x6, starting transfers between devices, swap(): return lax.ppermute(block, axis, [(i, i ^ bit) for i in range(size)])  31.1 us
    all_to_all x1, blocking collectives, add_up(): pieces = lax.all_to_all(pieces, GROUP, 0, 0, tiled=True)  23.4 us
    all_to_all x1, blocking collectives, hand_out(): return lax.all_to_all(copies, axes, 0, 0, tiled=True)  13.2 us
    all_to_all x2, starting transfers between devices, add_over(): pieces = lax.all_to_all(pieces, axes, 0, 0, tiled=True)  10.9 us
    all_to_all x1, starting transfers between devices, hand_out(): return lax.all_to_all(copies, axes, 0, 0, tiled=True)  9.94 us
    all_to_all x1, waiting for transfers between devices, hand_out(): return lax.all_to_all(copies, axes, 0, 0, tiled=True)  9.55 us
    all_to_all x2, waiting for transfers between devices, add_over(): pieces = lax.all_to_all(pieces, axes, 0, 0, tiled=True)  8.5 us
    ppermute x6, waiting for transfers between devices, swap(): return lax.ppermute(block, axis, [(i, i ^ bit) for i in range(size)])  7.96 us
  transfers between devices with their start and end apart: 9, of which 5 were waited for; matrix products, arithmetic and copies ran while one was open for 5% of the time, Pallas kernels for 0%

profile of v11, /device:TPU:1, one launch (start us, length us, event | category | flops | bytes accessed | tf_op | source)
XLA Modules:
  0.0 153.5 jit_solution(16159801669937506670)
XLA Ops:
  0.0 1.0 copy-done
  1.0 1.7 %convolution_convert_fusion.4 = bf16[256,512]{1,0:T(8,128)(2,1)S(1)} fusion(bf16[1,1024,256]{2,1,0:T(8,128)(2,1)S(1)} %copy-done, bf16[1,1024,512]{2,1,0:T(8,128)(2,1)} %param.4), kind=kOutput, calls=%fused_computation.10 | convolution fusion | flops 268566528 | bytes 1835008 | tf_op jit(solution)/shard_map/lk,lr->kr/dot_general | solution.py:22
  2.7 6.6 %collective-permute-start = (bf16[256,512]{1,0:T(8,128)(2,1)S(1)}, bf16[256,512]{1,0:T(8,128)(2,1)S(1)}, u32[]{:S(2)}, u32[]{:S(2)}) collective-permute-start(bf16[256,512]{1,0:T(8,128)(2,1)S(1)} %convolution_convert_fusion.4), channel_id=1, source_target_pairs={{0,32},{32,0},{1,33},{33,1},{2,34},{34,2},{3,35},{35,3},{4,36},{36... | collective-permute-start | bytes 786440 | tf_op jit(solution)/shard_map/ppermute | solution.py:18
  9.4 4.7 %collective-permute-start.1 = (bf16[256,256]{1,0:T(8,128)(2,1)S(1)}, bf16[256,256]{1,0:T(8,128)(2,1)S(1)}, u32[]{:S(2)}, u32[]{:S(2)}) collective-permute-start(bf16[256,256]{1,0:T(8,128)(2,1)S(1)} %get-tuple-element.36), channel_id=1, source_target_pairs={{0,256},{128,384},{256,0},{384,128},{1,257},{129,385},{257,1},{385... | collective-permute-start | bytes 393224 | tf_op jit(solution)/shard_map/ppermute | solution.py:18
  14.3 5.5 %collective-permute-done = bf16[256,512]{1,0:T(8,128)(2,1)S(1)} collective-permute-done((bf16[256,512]{1,0:T(8,128)(2,1)S(1)}, bf16[256,512]{1,0:T(8,128)(2,1)S(1)}, u32[]{:S(2)}, u32[]{:S(2)}) %collective-permute-start) | collective-permute-done | bytes 262176 | tf_op jit(solution)/shard_map/ppermute | solution.py:18
  20.6 10.0 %collective-permute-start.2 = (bf16[256,512]{1,0:T(8,128)(2,1)S(1)}, bf16[256,512]{1,0:T(8,128)(2,1)S(1)}, u32[]{:S(2)}, u32[]{:S(2)}) collective-permute-start(bf16[256,512]{1,0:T(8,128)(2,1)S(1)} %fusion.2), channel_id=1, source_target_pairs={{0,64},{64,0},{1,65},{65,1},{2,66},{66,2},{3,67},{67,3},{4,68},{68... | collective-permute-start | bytes 786440 | tf_op jit(solution)/shard_map/ppermute | solution.py:18
  30.6 3.1 %collective-permute-start.3 = (bf16[512,256]{1,0:T(8,128)(2,1)S(1)}, bf16[512,256]{1,0:T(8,128)(2,1)S(1)}, u32[]{:S(2)}, u32[]{:S(2)}) collective-permute-start(bf16[512,256]{1,0:T(8,128)(2,1)S(1)} %convolution_convert_fusion.3), channel_id=1, source_target_pairs={{0,128},{128,0},{256,384},{384,256},{1,129},{129,1},{257,385},{385... | collective-permute-start | bytes 786440 | tf_op jit(solution)/shard_map/ppermute | solution.py:18
  33.8 3.8 %all-gather = bf16[1024,256]{1,0:T(8,128)(2,1)S(1)} all-gather(bf16[512,256]{1,0:T(8,128)(2,1)S(1)} %convolution_convert_fusion.2), channel_id=2, replica_groups=mesh['x'=4,'zb'=2,'za'=2,'zl'=2,'y'=8,'c'=2] {'c'}, dimensions={0}, use_global_device_ids=true | all-gather | bytes 786432 | tf_op jit(solution)/shard_map/all_gather | solution.py:120
  37.9 1.9 %collective-permute-start.4 = (bf16[256,256]{1,0:T(8,128)(2,1)S(1)}, bf16[256,256]{1,0:T(8,128)(2,1)S(1)}, u32[]{:S(2)}, u32[]{:S(2)}) collective-permute-start(bf16[256,256]{1,0:T(8,128)(2,1)S(1)} %convolution_convert_fusion.5), channel_id=1, source_target_pairs={{0,32},{32,0},{1,33},{33,1},{2,34},{34,2},{3,35},{35,3},{4,36},{36... | collective-permute-start | bytes 393224 | tf_op jit(solution)/shard_map/ppermute | solution.py:18
  40.4 6.6 %all-gather.1 = bf16[1536,256]{1,0:T(8,128)(2,1)S(1)} all-gather(bf16[768,256]{1,0:T(8,128)(2,1)S(1)} %pad_maximum_fusion.1), channel_id=3, replica_groups=mesh['x'=4,'zb'=2,'za'=2,'zl'=2,'y'=8,'c'=2] {'c'}, dimensions={0}, use_global_device_ids=true | all-gather | bytes 1179648 | tf_op jit(solution)/shard_map/all_gather | solution.py:130
  47.3 2.4 %collective-permute-done.4 = bf16[256,256]{1,0:T(8,128)(2,1)S(1)} collective-permute-done((bf16[256,256]{1,0:T(8,128)(2,1)S(1)}, bf16[256,256]{1,0:T(8,128)(2,1)S(1)}, u32[]{:S(2)}, u32[]{:S(2)}) %collective-permute-start.4) | collective-permute-done | bytes 131104 | tf_op jit(solution)/shard_map/ppermute | solution.py:18
  49.7 1.2 fusion
  50.9 4.0 %all-to-all-start = ((bf16[4,256,256]{2,1,0:T(8,128)(2,1)}), bf16[4,256,256]{2,1,0:T(8,128)(2,1)S(1)}, u32[]{:S(2)}, u32[]{:S(2)}) async-start(bf16[4,256,256]{2,1,0:T(8,128)(2,1)} %bitcast.14), calls=%async_computation | async-start | bytes 1048576 | tf_op jit(solution)/shard_map/all_to_all | solution.py:46
  55.0 1.1 convolution_convert_fusion.7
  56.1 1.1 convolution_convert_fusion.6
  58.0 4.8 %collective-permute-start.5 = (bf16[256,512]{0,1:T(8,128)(2,1)}, bf16[256,512]{0,1:T(8,128)(2,1)S(1)}, u32[]{:S(2)}, u32[]{:S(2)}) collective-permute-start(bf16[256,512]{0,1:T(8,128)(2,1)} %pad_maximum_fusion.3), channel_id=1, source_target_pairs={{0,64},{64,0},{1,65},{65,1},{2,66},{66,2},{3,67},{67,3},{4,68},{68... | collective-permute-start | bytes 786440 | tf_op jit(solution)/shard_map/ppermute | solution.py:18
  62.8 1.0 all-to-all-done
  63.7 0.7 reduce_sum.36
  64.5 6.9 %all-to-all-start.1 = ((bf16[16,16,256]{2,1,0:T(8,128)(2,1)}), bf16[16,16,256]{2,1,0:T(8,128)(2,1)S(1)}, u32[]{:S(2)}, u32[]{:S(2)}) async-start(bf16[16,16,256]{2,1,0:T(8,128)(2,1)} %bitcast.15), calls=%async_computation.1 | async-start | bytes 262144 | tf_op jit(solution)/shard_map/all_to_all | solution.py:46
  71.4 7.5 %all-to-all-done.1 = bf16[16,16,256]{2,1,0:T(8,128)(2,1)S(1)} async-done(((bf16[16,16,256]{2,1,0:T(8,128)(2,1)}), bf16[16,16,256]{2,1,0:T(8,128)(2,1)S(1)}, u32[]{:S(2)}, u32[]{:S(2)}) %all-to-all-start.1) | async-done | bytes 131104 | tf_op jit(solution)/shard_map/all_to_all | solution.py:46
  79.0 0.8 broadcast_in_dim.23
  79.8 9.9 %all-to-all-start.2 = ((bf16[64,16,256]{2,1,0:T(8,128)(2,1)}), bf16[64,16,256]{2,1,0:T(8,128)(2,1)}, u32[]{:S(2)}, u32[]{:S(2)}) async-start(bf16[64,16,256]{2,1,0:T(8,128)(2,1)} %broadcast_in_dim.23), calls=%async_computation.2 | async-start | bytes 1048576 | tf_op jit(solution)/shard_map/all_to_all | solution.py:52
  89.7 1.2 convolution_convert_fusion
  90.9 1.2 convolution_convert_fusion.1
  92.2 2.9 %all-gather.3 = bf16[512,512]{1,0:T(8,128)(2,1)S(1)} all-gather(bf16[256,512]{1,0:T(8,128)(2,1)S(1)} %pad_maximum_fusion.5), channel_id=5, replica_groups=mesh['x'=4,'zb'=2,'za'=2,'zl'=2,'y'=8,'c'=2] {'c'}, dimensions={0}, use_global_device_ids=true | all-gather | bytes 786432 | tf_op jit(solution)/shard_map/all_gather | solution.py:146
  95.1 2.2 %all-gather.2 = bf16[512,512]{1,0:T(8,128)(2,1)S(1)} all-gather(bf16[256,512]{1,0:T(8,128)(2,1)S(1)} %pad_maximum_fusion.4), channel_id=4, replica_groups=mesh['x'=4,'zb'=2,'za'=2,'zl'=2,'y'=8,'c'=2] {'c'}, dimensions={0}, use_global_device_ids=true | all-gather | bytes 786432 | tf_op jit(solution)/shard_map/all_gather | solution.py:146
  97.2 9.6 %all-to-all-done.2 = bf16[64,16,256]{2,1,0:T(8,128)(2,1)} async-done(((bf16[64,16,256]{2,1,0:T(8,128)(2,1)}), bf16[64,16,256]{2,1,0:T(8,128)(2,1)}, u32[]{:S(2)}, u32[]{:S(2)}) %all-to-all-start.2) | async-done | bytes 524320 | tf_op jit(solution)/shard_map/all_to_all | solution.py:52
  106.8 1.5 subtract_convert_fusion
  108.7 23.4 %all_to_all.25 = bf16[64,16,256]{2,1,0:T(8,128)(2,1)S(1)} all-to-all(bf16[64,16,256]{2,1,0:T(8,128)(2,1)S(1)} %bitcast.77), channel_id=1, replica_groups=mesh['x'=4,'zb'=2,'za'=2,'zl'=2,'y'=8,'c'=2] {'x','zl','y'}, dimensions={0} | all-to-all | bytes 1048576 | tf_op jit(solution)/shard_map/all_to_all | solution.py:40
  132.2 13.2 %all_to_all.26 = bf16[16,16,256]{2,1,0:T(8,128)(2,1)S(1)} all-to-all(bf16[16,16,256]{2,1,0:T(8,128)(2,1)S(1)} %broadcast_in_dim.24), channel_id=1, replica_groups=mesh['x'=4,'zb'=2,'za'=2,'zl'=2,'y'=8,'c'=2] {'zl','y'}, dimensions={0} | all-to-all | bytes 262144 | tf_op jit(solution)/shard_map/all_to_all | solution.py:52
  145.5 5.4 %all_gather.35.total_hbm = bf16[2,256,256]{2,1,0:T(8,128)(2,1)S(1)} all-gather(bf16[1,256,256]{2,1,0:T(8,128)(2,1)S(1)} %bitcast.79), channel_id=1, replica_groups=mesh['x'=4,'zb'=2,'za'=2,'zl'=2,'y'=8,'c'=2] {'c'}, dimensions={0}, use_global_device_ids=true | all-gather | bytes 393216 | tf_op jit(solution)/shard_map/all_gather | solution.py:152
  150.9 2.6 %shard_map.46 = f32[1024,512]{1,0:T(8,128)} custom-call(bf16[1024,512]{1,0:T(8,128)(2,1)S(1)} %bitcast.73, bf16[1024,256]{1,0:T(8,128)(2,1)S(1)} %bitcast.74, bf16[2,256,256]{2,1,0:T(8,128)(2,1)S(1)} %all_gather.35.total_hbm), custom_call_target="tpu_custom_call" | custom-call | tf_op jit(solution)/shard_map/pallas_call | solution.py:87
  (33 shorter events, 3.5 us)
Async XLA Ops:
  0.0 1.0 copy-start
  0.0 9.4 %copy-start.3 = (bf16[4,1,1,2,256,256]{5,4,3,2,1,0:T(8,128)(2,1)S(1)}, bf16[4,1,1,2,256,256]{5,4,3,2,1,0:T(8,128)(2,1)}, u32[]{:S(2)}) copy-start(bf16[4,1,1,2,256,256]{5,4,3,2,1,0:T(8,128)(2,1)} %param.7) | copy-start | bytes 3145732
  2.7 17.1 %collective-permute-start = (bf16[256,512]{1,0:T(8,128)(2,1)S(1)}, bf16[256,512]{1,0:T(8,128)(2,1)S(1)}, u32[]{:S(2)}, u32[]{:S(2)}) collective-permute-start(bf16[256,512]{1,0:T(8,128)(2,1)S(1)} %convolution_convert_fusion.4), channel_id=1, source_target_pairs={{0,32},{32,0},{1,33},{33,1},{2,34},{34,2},{3,35},{35,3},{4,36},{36... | collective-permute-start | bytes 786440 | tf_op jit(solution)/shard_map/ppermute | solution.py:18
  9.4 10.7 %collective-permute-start.1 = (bf16[256,256]{1,0:T(8,128)(2,1)S(1)}, bf16[256,256]{1,0:T(8,128)(2,1)S(1)}, u32[]{:S(2)}, u32[]{:S(2)}) collective-permute-start(bf16[256,256]{1,0:T(8,128)(2,1)S(1)} %get-tuple-element.36), channel_id=1, source_target_pairs={{0,256},{128,384},{256,0},{384,128},{1,257},{129,385},{257,1},{385... | collective-permute-start | bytes 393224 | tf_op jit(solution)/shard_map/ppermute | solution.py:18
  14.1 23.4 %copy-start.2 = (bf16[1,1024,256]{2,1,0:T(8,128)(2,1)S(1)}, bf16[1,1024,256]{2,1,0:T(8,128)(2,1)}, u32[]{:S(2)}) copy-start(bf16[1,1024,256]{2,1,0:T(8,128)(2,1)} %param.6) | copy-start | bytes 1572868
  20.6 19.2 %collective-permute-start.2 = (bf16[256,512]{1,0:T(8,128)(2,1)S(1)}, bf16[256,512]{1,0:T(8,128)(2,1)S(1)}, u32[]{:S(2)}, u32[]{:S(2)}) collective-permute-start(bf16[256,512]{1,0:T(8,128)(2,1)S(1)} %fusion.2), channel_id=1, source_target_pairs={{0,64},{64,0},{1,65},{65,1},{2,66},{66,2},{3,67},{67,3},{4,68},{68... | collective-permute-start | bytes 786440 | tf_op jit(solution)/shard_map/ppermute | solution.py:18
  30.6 9.7 %collective-permute-start.3 = (bf16[512,256]{1,0:T(8,128)(2,1)S(1)}, bf16[512,256]{1,0:T(8,128)(2,1)S(1)}, u32[]{:S(2)}, u32[]{:S(2)}) collective-permute-start(bf16[512,256]{1,0:T(8,128)(2,1)S(1)} %convolution_convert_fusion.3), channel_id=1, source_target_pairs={{0,128},{128,0},{256,384},{384,256},{1,129},{129,1},{257,385},{385... | collective-permute-start | bytes 786440 | tf_op jit(solution)/shard_map/ppermute | solution.py:18
  37.9 11.8 %collective-permute-start.4 = (bf16[256,256]{1,0:T(8,128)(2,1)S(1)}, bf16[256,256]{1,0:T(8,128)(2,1)S(1)}, u32[]{:S(2)}, u32[]{:S(2)}) collective-permute-start(bf16[256,256]{1,0:T(8,128)(2,1)S(1)} %convolution_convert_fusion.5), channel_id=1, source_target_pairs={{0,32},{32,0},{1,33},{33,1},{2,34},{34,2},{3,35},{35,3},{4,36},{36... | collective-permute-start | bytes 393224 | tf_op jit(solution)/shard_map/ppermute | solution.py:18
  50.9 12.8 %all-to-all-start = ((bf16[4,256,256]{2,1,0:T(8,128)(2,1)}), bf16[4,256,256]{2,1,0:T(8,128)(2,1)S(1)}, u32[]{:S(2)}, u32[]{:S(2)}) async-start(bf16[4,256,256]{2,1,0:T(8,128)(2,1)} %bitcast.14), calls=%async_computation | async-start | bytes 1048576 | tf_op jit(solution)/shard_map/all_to_all | solution.py:46
  58.0 21.0 %collective-permute-start.5 = (bf16[256,512]{0,1:T(8,128)(2,1)}, bf16[256,512]{0,1:T(8,128)(2,1)S(1)}, u32[]{:S(2)}, u32[]{:S(2)}) collective-permute-start(bf16[256,512]{0,1:T(8,128)(2,1)} %pad_maximum_fusion.3), channel_id=1, source_target_pairs={{0,64},{64,0},{1,65},{65,1},{2,66},{66,2},{3,67},{67,3},{4,68},{68... | collective-permute-start | bytes 786440 | tf_op jit(solution)/shard_map/ppermute | solution.py:18
  64.5 14.4 %all-to-all-start.1 = ((bf16[16,16,256]{2,1,0:T(8,128)(2,1)}), bf16[16,16,256]{2,1,0:T(8,128)(2,1)S(1)}, u32[]{:S(2)}, u32[]{:S(2)}) async-start(bf16[16,16,256]{2,1,0:T(8,128)(2,1)} %bitcast.15), calls=%async_computation.1 | async-start | bytes 262144 | tf_op jit(solution)/shard_map/all_to_all | solution.py:46
  79.8 27.0 %all-to-all-start.2 = ((bf16[64,16,256]{2,1,0:T(8,128)(2,1)}), bf16[64,16,256]{2,1,0:T(8,128)(2,1)}, u32[]{:S(2)}, u32[]{:S(2)}) async-start(bf16[64,16,256]{2,1,0:T(8,128)(2,1)} %broadcast_in_dim.23), calls=%async_computation.2 | async-start | bytes 1048576 | tf_op jit(solution)/shard_map/all_to_all | solution.py:52
  108.3 42.6 %copy-start.1 = (bf16[1,1024,512]{2,1,0:T(8,128)(2,1)S(1)}, bf16[1,1024,512]{2,1,0:T(8,128)(2,1)}, u32[]{:S(2)}) copy-start(bf16[1,1024,512]{2,1,0:T(8,128)(2,1)} %param.4) | copy-start | bytes 3145732

commit v12 on v9

--- a/solution.py
+++ b/solution.py
@@ -10,7 +10,7 @@
 LINE = ("zl", "y")
 GROUP = ("x",) + LINE
 QUAD = ("zb", "za")
-CHUNKS = 4
+CHUNKS = 8
 
 
 def swap(block, axis, bit):
@@ -108,7 +108,7 @@
 
     far = swap(other[3], "x", 2)
     field = (dot(own[0], start) + dot(other[0], swap(start, "za", 1))).astype(BF)
-    field, far = tie((field, far))
+    _, far = tie((field, far))
     wide = jnp.concatenate([own[3], far], 0)
     came = swap(dot(wide, other[2]).astype(BF), "x", 1)
     kept = lax.all_gather(dot(wide, own[2]).astype(BF), "c")
@@ -117,7 +117,7 @@
     gram = mm("li,lj->ij", basis, out_basis).astype(BF)
     near = swap(gram, "za", 1)
     field = (dot(own[1], field) + dot(other[1], swap(field, "zb", 1))).astype(BF)
-    field, came, kept = tie((field, came, kept))
+    _, came, kept = tie((field, came, kept))
 
     keep = lax.dynamic_slice_in_dim(field, core * half, half, 1)
     give = lax.dynamic_slice_in_dim(field, (1 - core) * half, half, 1)

time: 149 us -> 150 us (level)
  Pallas kernels: 2.62 us -> 4.53 us
    pallas_call x1, Pallas kernels: 2.62 us -> 4.53 us  [finish(): pl.pallas_call(finish_kernel, in_specs=[pl.BlockSpec(memory_space=pl.ANY)...]
  transfers between devices with their start and end apart: 8 -> 8, of which waited for: 4 -> 4; matrix products, arithmetic and copies ran while one was open for 5% -> 6% of each run, Pallas kernels for 0% -> 0%
where the time goes in v12:
time: 150 us; the launch traced here: 149 us
  blocking collectives  57.1 us (38%)
  starting transfers between devices  50.9 us (34%)
  waiting for transfers between devices  22.1 us (15%)
  matrix products  11.1 us (7%)
  Pallas kernels  4.53 us (3%)
  local copies, waits for them, and re-layouts  1.95 us (1%)
    ppermute x6, starting transfers between devices, swap(): return lax.ppermute(block, axis, [(i, i ^ bit) for i in range(size)])  31.4 us
    all_to_all x1, blocking collectives, add_up(): pieces = lax.all_to_all(pieces, GROUP, 0, 0, tiled=True)  22.3 us
    all_to_all x1, blocking collectives, hand_out(): return lax.all_to_all(copies, axes, 0, 0, tiled=True)  12.8 us
    all_to_all x1, starting transfers between devices, add_up(): pieces = lax.all_to_all(pieces, GROUP, 0, 0, tiled=True)  10.7 us
    all_to_all x1, starting transfers between devices, hand_out(): return lax.all_to_all(copies, axes, 0, 0, tiled=True)  8.84 us
    all_to_all x1, waiting for transfers between devices, add_up(): pieces = lax.all_to_all(pieces, GROUP, 0, 0, tiled=True)  7.83 us
    ppermute x6, waiting for transfers between devices, swap(): return lax.ppermute(block, axis, [(i, i ^ bit) for i in range(size)])  7.62 us
    all_to_all x1, waiting for transfers between devices, hand_out(): return lax.all_to_all(copies, axes, 0, 0, tiled=True)  6.7 us
  transfers between devices with their start and end apart: 8, of which 4 were waited for; matrix products, arithmetic and copies ran while one was open for 6% of the time, Pallas kernels for 0%

profile of v12, /device:TPU:1, one launch (start us, length us, event | category | flops | bytes accessed | tf_op | source)
XLA Modules:
  0.0 149.4 jit_solution(10278758407932540215)
XLA Ops:
  0.0 1.0 copy-done
  1.0 1.7 %convolution_convert_fusion.4 = bf16[256,512]{1,0:T(8,128)(2,1)S(1)} fusion(bf16[1,1024,256]{2,1,0:T(8,128)(2,1)S(1)} %copy-done, bf16[1,1024,512]{2,1,0:T(8,128)(2,1)} %param.4), kind=kOutput, calls=%fused_computation.10 | convolution fusion | flops 268566528 | bytes 1835008 | tf_op jit(solution)/shard_map/lk,lr->kr/dot_general | solution.py:22
  2.7 6.6 %collective-permute-start = (bf16[256,512]{1,0:T(8,128)(2,1)S(1)}, bf16[256,512]{1,0:T(8,128)(2,1)S(1)}, u32[]{:S(2)}, u32[]{:S(2)}) collective-permute-start(bf16[256,512]{1,0:T(8,128)(2,1)S(1)} %convolution_convert_fusion.4), channel_id=1, source_target_pairs={{0,32},{32,0},{1,33},{33,1},{2,34},{34,2},{3,35},{35,3},{4,36},{36... | collective-permute-start | bytes 786440 | tf_op jit(solution)/shard_map/ppermute | solution.py:18
  9.4 4.7 %collective-permute-start.2 = (bf16[256,256]{1,0:T(8,128)(2,1)S(1)}, bf16[256,256]{1,0:T(8,128)(2,1)S(1)}, u32[]{:S(2)}, u32[]{:S(2)}) collective-permute-start(bf16[256,256]{1,0:T(8,128)(2,1)S(1)} %get-tuple-element.28), channel_id=1, source_target_pairs={{0,256},{128,384},{256,0},{384,128},{1,257},{129,385},{257,1},{385... | collective-permute-start | bytes 393224 | tf_op jit(solution)/shard_map/ppermute | solution.py:18
  14.3 5.5 %collective-permute-done = bf16[256,512]{1,0:T(8,128)(2,1)S(1)} collective-permute-done((bf16[256,512]{1,0:T(8,128)(2,1)S(1)}, bf16[256,512]{1,0:T(8,128)(2,1)S(1)}, u32[]{:S(2)}, u32[]{:S(2)}) %collective-permute-start) | collective-permute-done | bytes 262176 | tf_op jit(solution)/shard_map/ppermute | solution.py:18
  20.1 10.0 %collective-permute-start.1 = (bf16[256,512]{1,0:T(8,128)(2,1)S(1)}, bf16[256,512]{1,0:T(8,128)(2,1)S(1)}, u32[]{:S(2)}, u32[]{:S(2)}) collective-permute-start(bf16[256,512]{1,0:T(8,128)(2,1)S(1)} %fusion.2), channel_id=1, source_target_pairs={{0,64},{64,0},{1,65},{65,1},{2,66},{66,2},{3,67},{67,3},{4,68},{68... | collective-permute-start | bytes 786440 | tf_op jit(solution)/shard_map/ppermute | solution.py:18
  30.6 3.1 %collective-permute-start.3 = (bf16[512,256]{1,0:T(8,128)(2,1)S(1)}, bf16[512,256]{1,0:T(8,128)(2,1)S(1)}, u32[]{:S(2)}, u32[]{:S(2)}) collective-permute-start(bf16[512,256]{1,0:T(8,128)(2,1)S(1)} %convolution_convert_fusion.3), channel_id=1, source_target_pairs={{0,128},{128,0},{256,384},{384,256},{1,129},{129,1},{257,385},{385... | collective-permute-start | bytes 786440 | tf_op jit(solution)/shard_map/ppermute | solution.py:18
  33.8 3.8 %all-gather = bf16[1024,256]{1,0:T(8,128)(2,1)S(1)} all-gather(bf16[512,256]{1,0:T(8,128)(2,1)S(1)} %convolution_convert_fusion.2), channel_id=2, replica_groups=mesh['x'=4,'zb'=2,'za'=2,'zl'=2,'y'=8,'c'=2] {'c'}, dimensions={0}, use_global_device_ids=true | all-gather | bytes 786432 | tf_op jit(solution)/shard_map/all_gather | solution.py:114
  37.5 0.3 convolution_convert_fusion.5
  38.1 1.9 %collective-permute-start.4 = (bf16[256,256]{1,0:T(8,128)(2,1)S(1)}, bf16[256,256]{1,0:T(8,128)(2,1)S(1)}, u32[]{:S(2)}, u32[]{:S(2)}) collective-permute-start(bf16[256,256]{1,0:T(8,128)(2,1)S(1)} %convolution_convert_fusion.5), channel_id=1, source_target_pairs={{0,32},{32,0},{1,33},{33,1},{2,34},{34,2},{3,35},{35,3},{4,36},{36... | collective-permute-start | bytes 393224 | tf_op jit(solution)/shard_map/ppermute | solution.py:18
  40.4 5.9 %all-gather.1 = bf16[1536,256]{1,0:T(8,128)(2,1)S(1)} all-gather(bf16[768,256]{1,0:T(8,128)(2,1)S(1)} %pad_maximum_fusion.1), channel_id=3, replica_groups=mesh['x'=4,'zb'=2,'za'=2,'zl'=2,'y'=8,'c'=2] {'c'}, dimensions={0}, use_global_device_ids=true | all-gather | bytes 1179648 | tf_op jit(solution)/shard_map/all_gather | solution.py:124
  46.5 2.1 %collective-permute-done.4 = bf16[256,256]{1,0:T(8,128)(2,1)S(1)} collective-permute-done((bf16[256,256]{1,0:T(8,128)(2,1)S(1)}, bf16[256,256]{1,0:T(8,128)(2,1)S(1)}, u32[]{:S(2)}, u32[]{:S(2)}) %collective-permute-start.4) | collective-permute-done | bytes 131104 | tf_op jit(solution)/shard_map/ppermute | solution.py:18
  48.6 1.2 fusion
  49.8 10.7 %all-to-all-start = ((bf16[64,16,256]{2,1,0:T(8,128)(2,1)}), bf16[64,16,256]{2,1,0:T(8,128)(2,1)S(1)}, u32[]{:S(2)}, u32[]{:S(2)}) async-start(bf16[64,16,256]{2,1,0:T(8,128)(2,1)} %bitcast.16), calls=%async_computation | async-start | bytes 1048576 | tf_op jit(solution)/shard_map/all_to_all | solution.py:40
  60.5 1.1 convolution_convert_fusion.7
  61.6 1.1 convolution_convert_fusion.6
  62.8 0.7 pad_maximum_fusion.3
  63.5 5.0 %collective-permute-start.5 = (bf16[256,512]{0,1:T(8,128)(2,1)}, bf16[256,512]{0,1:T(8,128)(2,1)S(1)}, u32[]{:S(2)}, u32[]{:S(2)}) collective-permute-start(bf16[256,512]{0,1:T(8,128)(2,1)} %pad_maximum_fusion.3), channel_id=1, source_target_pairs={{0,64},{64,0},{1,65},{65,1},{2,66},{66,2},{3,67},{67,3},{4,68},{68... | collective-permute-start | bytes 786440 | tf_op jit(solution)/shard_map/ppermute | solution.py:18
  68.5 7.8 %all-to-all-done = bf16[64,16,256]{2,1,0:T(8,128)(2,1)S(1)} async-done(((bf16[64,16,256]{2,1,0:T(8,128)(2,1)}), bf16[64,16,256]{2,1,0:T(8,128)(2,1)S(1)}, u32[]{:S(2)}, u32[]{:S(2)}) %all-to-all-start) | async-done | bytes 524320 | tf_op jit(solution)/shard_map/all_to_all | solution.py:40
  76.5 0.8 broadcast_in_dim.23
  77.3 8.8 %all-to-all-start.1 = ((bf16[64,16,256]{2,1,0:T(8,128)(2,1)}), bf16[64,16,256]{2,1,0:T(8,128)(2,1)}, u32[]{:S(2)}, u32[]{:S(2)}) async-start(bf16[64,16,256]{2,1,0:T(8,128)(2,1)} %broadcast_in_dim.23), calls=%async_computation.1 | async-start | bytes 1048576 | tf_op jit(solution)/shard_map/all_to_all | solution.py:46
  86.2 1.2 convolution_convert_fusion
  87.3 1.2 convolution_convert_fusion.1
  88.6 4.1 %all-gather.3 = bf16[512,512]{1,0:T(8,128)(2,1)S(1)} all-gather(bf16[256,512]{1,0:T(8,128)(2,1)S(1)} %pad_maximum_fusion.5), channel_id=5, replica_groups=mesh['x'=4,'zb'=2,'za'=2,'zl'=2,'y'=8,'c'=2] {'c'}, dimensions={0}, use_global_device_ids=true | all-gather | bytes 786432 | tf_op jit(solution)/shard_map/all_gather | solution.py:140
  92.7 2.2 %all-gather.2 = bf16[512,512]{1,0:T(8,128)(2,1)S(1)} all-gather(bf16[256,512]{1,0:T(8,128)(2,1)S(1)} %pad_maximum_fusion.4), channel_id=4, replica_groups=mesh['x'=4,'zb'=2,'za'=2,'zl'=2,'y'=8,'c'=2] {'c'}, dimensions={0}, use_global_device_ids=true | all-gather | bytes 786432 | tf_op jit(solution)/shard_map/all_gather | solution.py:140
  94.9 6.7 %all-to-all-done.1 = bf16[64,16,256]{2,1,0:T(8,128)(2,1)} async-done(((bf16[64,16,256]{2,1,0:T(8,128)(2,1)}), bf16[64,16,256]{2,1,0:T(8,128)(2,1)}, u32[]{:S(2)}, u32[]{:S(2)}) %all-to-all-start.1) | async-done | bytes 524320 | tf_op jit(solution)/shard_map/all_to_all | solution.py:46
  101.6 1.5 subtract_convert_fusion
  103.1 0.4 fusion.1
  103.5 22.3 %all_to_all.20 = bf16[64,16,256]{2,1,0:T(8,128)(2,1)S(1)} all-to-all(bf16[64,16,256]{2,1,0:T(8,128)(2,1)S(1)} %bitcast.76), channel_id=1, replica_groups=mesh['x'=4,'zb'=2,'za'=2,'zl'=2,'y'=8,'c'=2] {'x','zl','y'}, dimensions={0} | all-to-all | bytes 1048576 | tf_op jit(solution)/shard_map/all_to_all | solution.py:40
  125.9 12.8 %all_to_all.21 = bf16[16,16,256]{2,1,0:T(8,128)(2,1)S(1)} all-to-all(bf16[16,16,256]{2,1,0:T(8,128)(2,1)S(1)} %broadcast_in_dim.24), channel_id=1, replica_groups=mesh['x'=4,'zb'=2,'za'=2,'zl'=2,'y'=8,'c'=2] {'zl','y'}, dimensions={0} | all-to-all | bytes 262144 | tf_op jit(solution)/shard_map/all_to_all | solution.py:46
  138.8 6.1 %all_gather.35.total_hbm = bf16[2,256,256]{2,1,0:T(8,128)(2,1)S(1)} all-gather(bf16[1,256,256]{2,1,0:T(8,128)(2,1)S(1)} %bitcast.78), channel_id=1, replica_groups=mesh['x'=4,'zb'=2,'za'=2,'zl'=2,'y'=8,'c'=2] {'c'}, dimensions={0}, use_global_device_ids=true | all-gather | bytes 393216 | tf_op jit(solution)/shard_map/all_gather | solution.py:146
  144.9 4.5 %shard_map.46 = f32[1024,512]{1,0:T(8,128)} custom-call(bf16[1024,512]{1,0:T(8,128)(2,1)S(1)} %bitcast.72, bf16[1024,256]{1,0:T(8,128)(2,1)S(1)} %bitcast.73, bf16[2,256,256]{2,1,0:T(8,128)(2,1)S(1)} %all_gather.35.total_hbm), custom_call_target="tpu_custom_call" | custom-call | tf_op jit(solution)/shard_map/pallas_call | solution.py:81
  (30 shorter events, 2.1 us)
Async XLA Ops:
  0.0 1.0 copy-start
  0.0 9.4 %copy-start.3 = (bf16[4,1,1,2,256,256]{5,4,3,2,1,0:T(8,128)(2,1)S(1)}, bf16[4,1,1,2,256,256]{5,4,3,2,1,0:T(8,128)(2,1)}, u32[]{:S(2)}) copy-start(bf16[4,1,1,2,256,256]{5,4,3,2,1,0:T(8,128)(2,1)} %param.7) | copy-start | bytes 3145732
  2.7 17.1 %collective-permute-start = (bf16[256,512]{1,0:T(8,128)(2,1)S(1)}, bf16[256,512]{1,0:T(8,128)(2,1)S(1)}, u32[]{:S(2)}, u32[]{:S(2)}) collective-permute-start(bf16[256,512]{1,0:T(8,128)(2,1)S(1)} %convolution_convert_fusion.4), channel_id=1, source_target_pairs={{0,32},{32,0},{1,33},{33,1},{2,34},{34,2},{3,35},{35,3},{4,36},{36... | collective-permute-start | bytes 786440 | tf_op jit(solution)/shard_map/ppermute | solution.py:18
  9.4 20.7 %collective-permute-start.2 = (bf16[256,256]{1,0:T(8,128)(2,1)S(1)}, bf16[256,256]{1,0:T(8,128)(2,1)S(1)}, u32[]{:S(2)}, u32[]{:S(2)}) collective-permute-start(bf16[256,256]{1,0:T(8,128)(2,1)S(1)} %get-tuple-element.28), channel_id=1, source_target_pairs={{0,256},{128,384},{256,0},{384,128},{1,257},{129,385},{257,1},{385... | collective-permute-start | bytes 393224 | tf_op jit(solution)/shard_map/ppermute | solution.py:18
  14.1 23.4 %copy-start.2 = (bf16[1,1024,256]{2,1,0:T(8,128)(2,1)S(1)}, bf16[1,1024,256]{2,1,0:T(8,128)(2,1)}, u32[]{:S(2)}) copy-start(bf16[1,1024,256]{2,1,0:T(8,128)(2,1)} %param.6) | copy-start | bytes 1572868
  20.1 20.0 %collective-permute-start.1 = (bf16[256,512]{1,0:T(8,128)(2,1)S(1)}, bf16[256,512]{1,0:T(8,128)(2,1)S(1)}, u32[]{:S(2)}, u32[]{:S(2)}) collective-permute-start(bf16[256,512]{1,0:T(8,128)(2,1)S(1)} %fusion.2), channel_id=1, source_target_pairs={{0,64},{64,0},{1,65},{65,1},{2,66},{66,2},{3,67},{67,3},{4,68},{68... | collective-permute-start | bytes 786440 | tf_op jit(solution)/shard_map/ppermute | solution.py:18
  30.6 9.7 %collective-permute-start.3 = (bf16[512,256]{1,0:T(8,128)(2,1)S(1)}, bf16[512,256]{1,0:T(8,128)(2,1)S(1)}, u32[]{:S(2)}, u32[]{:S(2)}) collective-permute-start(bf16[512,256]{1,0:T(8,128)(2,1)S(1)} %convolution_convert_fusion.3), channel_id=1, source_target_pairs={{0,128},{128,0},{256,384},{384,256},{1,129},{129,1},{257,385},{385... | collective-permute-start | bytes 786440 | tf_op jit(solution)/shard_map/ppermute | solution.py:18
  38.1 10.5 %collective-permute-start.4 = (bf16[256,256]{1,0:T(8,128)(2,1)S(1)}, bf16[256,256]{1,0:T(8,128)(2,1)S(1)}, u32[]{:S(2)}, u32[]{:S(2)}) collective-permute-start(bf16[256,256]{1,0:T(8,128)(2,1)S(1)} %convolution_convert_fusion.5), channel_id=1, source_target_pairs={{0,32},{32,0},{1,33},{33,1},{2,34},{34,2},{3,35},{35,3},{4,36},{36... | collective-permute-start | bytes 393224 | tf_op jit(solution)/shard_map/ppermute | solution.py:18
  49.8 26.5 %all-to-all-start = ((bf16[64,16,256]{2,1,0:T(8,128)(2,1)}), bf16[64,16,256]{2,1,0:T(8,128)(2,1)S(1)}, u32[]{:S(2)}, u32[]{:S(2)}) async-start(bf16[64,16,256]{2,1,0:T(8,128)(2,1)} %bitcast.16), calls=%async_computation | async-start | bytes 1048576 | tf_op jit(solution)/shard_map/all_to_all | solution.py:40
  63.5 23.8 %collective-permute-start.5 = (bf16[256,512]{0,1:T(8,128)(2,1)}, bf16[256,512]{0,1:T(8,128)(2,1)S(1)}, u32[]{:S(2)}, u32[]{:S(2)}) collective-permute-start(bf16[256,512]{0,1:T(8,128)(2,1)} %pad_maximum_fusion.3), channel_id=1, source_target_pairs={{0,64},{64,0},{1,65},{65,1},{2,66},{66,2},{3,67},{67,3},{4,68},{68... | collective-permute-start | bytes 786440 | tf_op jit(solution)/shard_map/ppermute | solution.py:18
  77.3 24.3 %all-to-all-start.1 = ((bf16[64,16,256]{2,1,0:T(8,128)(2,1)}), bf16[64,16,256]{2,1,0:T(8,128)(2,1)}, u32[]{:S(2)}, u32[]{:S(2)}) async-start(bf16[64,16,256]{2,1,0:T(8,128)(2,1)} %broadcast_in_dim.23), calls=%async_computation.1 | async-start | bytes 1048576 | tf_op jit(solution)/shard_map/all_to_all | solution.py:46
  103.0 41.8 %copy-start.1 = (bf16[1,1024,512]{2,1,0:T(8,128)(2,1)S(1)}, bf16[1,1024,512]{2,1,0:T(8,128)(2,1)}, u32[]{:S(2)}) copy-start(bf16[1,1024,512]{2,1,0:T(8,128)(2,1)} %param.4) | copy-start | bytes 3145732
